TPU v7x, 32 devices: a whole 2x2x4 slice. The times are simulated.
32 devices in a mesh: groups: 2 (over y), blk: 4 (over z), occ: 2 (over x), sub: 2 (over core).
Axes of the slice: x: 2, y: 2, z: 4, core: 2. Of those that a mesh axis runs over, the one named last changes fastest.
Arguments:
- amplitudes: bfloat16 [512, 64], P(('groups', 'occ'), 'blk'), parts along dimension 0, may hold values from -6 to 6
- integrals: bfloat16 [401408, 64], P(('groups', 'blk', 'sub')), parts along dimension 0, may hold values from -0.75 to 0.75
Outputs:
- residual: float32 [512, 200704], P(('groups', 'occ'), ('blk', 'sub')), parts along dimension 0
There are 2 independent parts, one for each index of `groups`. A program takes and returns all parts, laid end to end along the dimension named above; each array names one. Nothing has to cross between parts.
All inputs are finite; a program needn't handle non-finite values.
Results may differ from a plain program's by a relative error of at most 0.0003.
Values may be sent and summed in bfloat16 or wider, within the bound.
No kernel may reach another device: no remote copies, remote signals or barrier semaphores. Data moves between devices by JAX's collectives and lax.ppermute only.
A program may use at most 128 MiB of HBM per device.

v0:
```python
import jax
import jax.numpy as jnp
from jax import lax
from jax.sharding import PartitionSpec as P

NOCC = 16
NVIR = 448


def shards(amplitudes, integrals):
    pair_rows = amplitudes.shape[0]
    orbital_rows = integrals.shape[0]
    whole = lax.all_gather(amplitudes, "blk", axis=1, tiled=True)
    ladder = lax.dot_general(
        whole, integrals, (((1,), (1,)), ((), ())), preferred_element_type=jnp.float32
    )
    occ_local = pair_rows // NOCC
    vir_local = orbital_rows // NVIR
    blocks = ladder.reshape(occ_local, NOCC, vir_local, NVIR)
    arrived = lax.all_to_all(
        lax.all_to_all(blocks, ("blk", "sub"), split_axis=3, concat_axis=2, tiled=True),
        "occ",
        split_axis=1,
        concat_axis=0,
        tiled=True,
    )
    partner = jnp.transpose(arrived, (1, 0, 3, 2))
    return (blocks + partner).reshape(pair_rows, orbital_rows)


def solution(mesh):
    placed = (P(("groups", "occ"), "blk"), P(("groups", "blk", "sub"), None))
    return jax.shard_map(
        shards,
        mesh=mesh,
        in_specs=placed,
        out_specs=P(("groups", "occ"), ("blk", "sub")),
        check_vma=False,
    )
```

profile of v0, /device:TPU:0, one launch (start us, length us, event | category | flops | bytes accessed | tf_op | source)
XLA Modules:
  0.0 819.5 jit_solution(17474712964386806985)
XLA Ops:
  0.0 0.0 copy-start
  0.0 15.1 %all_gather.3 = bf16[128,64]{0,1:T(8,128)(2,1)S(1)} all-gather(bf16[128,16]{0,1:T(8,128)(2,1)} %param.2), channel_id=1, replica_groups=mesh['groups'=2,'blk'=4,'occ'=2,'sub'=2] {'blk'}, dimensions={1}, use_global_device_ids=true | all-gather | bytes 20480 | tf_op jit(solution)/shard_map/all_gather | solution.py:13
  15.1 0.0 copy-done
  15.1 6.7 fusion
  21.8 14.8 %reshape.6 = f32[8,16,56,448]{3,2,1,0:T(8,128)} reshape(f32[128,25088]{1,0:T(8,128)} %fusion) | data formatting | bytes 25690112 | tf_op jit(solution)/shard_map/reshape | solution.py:19
  36.6 21.4 %copy.10 = f32[8,16,56,448]{2,1,0,3:T(8,128)} copy(f32[8,16,56,448]{3,2,1,0:T(8,128)} %reshape.6) | data formatting | bytes 25690112 | tf_op jit(solution)/shard_map/reshape | solution.py:19
  58.0 37.8 %reshape.9 = f32[8,1,401408]{2,1,0:T(1,128)} reshape(f32[448,8,16,56]{3,2,1,0:T(8,128)} %bitcast.22) | data formatting | bytes 25690112
  95.8 287.2 %all_to_all.36 = f32[8,1,401408]{2,1,0:T(1,128)} all-to-all(f32[8,1,401408]{2,1,0:T(1,128)} %reshape.9), channel_id=1, replica_groups=mesh['groups'=2,'blk'=4,'occ'=2,'sub'=2] {'blk','sub'}, dimensions={0} | all-to-all | bytes 25690112 | tf_op jit(solution)/shard_map/all_to_all | solution.py:21
  383.1 0.6 broadcast
  383.6 109.8 %reduce = f32[8,401408]{1,0:T(8,128)} reduce(f32[8,1,401408]{2,1,0:T(1,128)} %all_to_all.36, f32[]{:T(128)} %broadcast), dimensions={1}, to_apply=%all_to_all.26.reduce_sub_computation | reduce | bytes 25690116 | tf_op jit(solution)/shard_map/all_to_all | solution.py:21
  493.4 40.0 %reshape.10 = f32[448,8,16,56]{3,2,1,0:T(8,128)} reshape(f32[8,401408]{1,0:T(8,128)} %reduce) | data formatting | bytes 25690112
  533.5 28.5 %copy.20 = f32[8,16,8,56,56]{3,2,4,0,1:T(8,128)} copy(f32[8,16,8,56,56]{3,1,0,4,2:T(8,128)} %bitcast.21) | data formatting | bytes 25690112 | tf_op jit(solution)/shard_map/all_to_all | solution.py:21
  562.0 25.3 %reshape.8 = f32[8,16,448,56]{2,3,0,1:T(8,128)} reshape(f32[8,16,8,56,56]{3,2,4,0,1:T(8,128)} %copy.20) | data formatting | bytes 25690112 | tf_op jit(solution)/shard_map/all_to_all | solution.py:21
  587.3 176.0 %all_to_all.37 = f32[8,16,448,56]{2,3,0,1:T(8,128)} all-to-all(f32[8,16,448,56]{2,3,0,1:T(8,128)} %reshape.8), channel_id=1, replica_groups=mesh['groups'=2,'blk'=4,'occ'=2,'sub'=2] {'occ'}, dimensions={1} | all-to-all | bytes 25690112 | tf_op jit(solution)/shard_map/all_to_all | solution.py:20
  763.3 13.0 %copy.15 = f32[2,8,8,448,56]{3,4,2,1,0:T(8,128)} copy(f32[2,8,8,448,56]{3,4,1,2,0:T(8,128)} %bitcast.23) | data formatting | bytes 25690112 | tf_op jit(solution)/shard_map/all_to_all | solution.py:20
  776.2 14.9 %bitcast_add_fusion = f32[8,16,56,448]{3,2,0,1:T(8,128)} fusion(f32[2,8,8,448,56]{3,4,2,1,0:T(8,128)} %copy.15, f32[8,16,56,448]{3,2,1,0:T(8,128)} %reshape.6), kind=kLoop, calls=%fused_computation | loop fusion | flops 3211264 | bytes 38535168 | tf_op jit(solution)/shard_map/add | solution.py:28
  791.2 0.0 copy-start.1
  791.2 13.1 %copy.17 = f32[8,16,56,448]{3,2,1,0:T(8,128)} copy(f32[8,16,56,448]{3,2,0,1:T(8,128)} %bitcast_add_fusion) | data formatting | bytes 25690112 | tf_op jit(solution)/shard_map/add | solution.py:28
  804.3 14.8 %reshape.7 = f32[128,25088]{1,0:T(8,128)} reshape(f32[8,16,56,448]{3,2,1,0:T(8,128)} %copy.17) | data formatting | bytes 25690112 | tf_op jit(solution)/shard_map/reshape | solution.py:28
  819.0 0.0 copy-done.1
Async XLA Ops:
  0.0 15.1 %copy-start = (bf16[25088,64]{0,1:T(8,128)(2,1)S(1)}, bf16[25088,64]{0,1:T(8,128)(2,1)}, u32[]{:S(2)}) copy-start(bf16[25088,64]{0,1:T(8,128)(2,1)} %param.3) | copy-start | bytes 9633796
  791.2 27.9 %copy-start.1 = (bf16[25088,64]{0,1:T(8,128)(2,1)S(1)}, bf16[25088,64]{0,1:T(8,128)(2,1)}, u32[]{:S(2)}) copy-start(bf16[25088,64]{0,1:T(8,128)(2,1)} %param.3) | copy-start | bytes 9633796
where the time goes:
time: 827 us; the launch traced here: 819 us
  blocking collectives  478 us (58%)
  local copies, waits for them, and re-layouts  209 us (25%)
  other arithmetic  125 us (15%)
    all_to_all x1, blocking collectives, shards(): lax.all_to_all(blocks, ('blk', 'sub'), split_axis=3, concat_axis=2, tiled...  287 us
    all_to_all x1, blocking collectives, shards(): lax.all_to_all(lax.all_to_all(blocks, ('blk', 'sub'), split_axis=3, conca...  176 us
    all_to_all x1, other arithmetic, shards(): lax.all_to_all(blocks, ('blk', 'sub'), split_axis=3, concat_axis=2, tiled...  110 us
    unnamed x6, local copies, waits for them, and re-layouts  77.8 us
    all_to_all x3, local copies, waits for them, and re-layouts, shards(): lax.all_to_all(blocks, ('blk', 'sub'), split_axis=3, concat_axis=2, tiled...  54.4 us
    reshape x2, local copies, waits for them, and re-layouts, shards(): blocks = ladder.reshape(occ_local, NOCC, vir_local, NVIR)  36.3 us

commit v1 on v0

v1 whole, which is shorter than its diff:
```python
import functools

import jax
import jax.numpy as jnp
from jax import lax
from jax.experimental import pallas as pl
from jax.experimental.pallas import tpu as pltpu
from jax.sharding import PartitionSpec as P

NOCC = 16
NVIR = 448
LANES = 128
VMEM = 56 * 2**20
NT = (((1,), (1,)), ((), ()))
NN = (((1,), (0,)), ((), ()))


def position():
    return lax.axis_index("blk") * 2 + lax.axis_index("sub"), lax.axis_index("occ")


def pack_kernel(plan, vt, *rest):
    outs, rows = rest[:-1], rest[-1]
    kw = vt.shape[0]
    vl = rows.shape[0]
    half = vl // 2
    tiles = 2 * NVIR // LANES
    me, plane = position()

    def turn(pair, carry):
        base = pl.multiple_of(pair * (2 * NVIR), LANES)
        for t in range(tiles):
            block = vt[:, pl.ds(pl.multiple_of(base + t * LANES, LANES), LANES)]
            turned = jnp.concatenate([block, block], axis=0).T.astype(jnp.float32)
            start = t * LANES
            if start + LANES <= NVIR:
                rows[2 * pair, start : start + LANES, :] = turned
            elif start >= NVIR:
                rows[2 * pair + 1, start - NVIR : start - NVIR + LANES, :] = turned
            else:
                cut = NVIR - start
                rows[2 * pair, start:NVIR, :] = turned[:cut]
                rows[2 * pair + 1, 0 : LANES - cut, :] = turned[cut:]
        return carry

    lax.fori_loop(0, vl // 2, turn, 0)
    low = lax.broadcasted_iota(jnp.int32, (vl, LANES), 1) < kw
    for out, (far, first, count, shared) in zip(outs, plan):
        base = jnp.bitwise_xor(me, far) * vl

        def gather(n, carry, out=out, base=base, first=first, shared=shared):
            if shared:
                m, at = 2 * (first + n) + plane, (n,)
            else:
                m, at = n, (n % 2, n // 2)
            for h in range(2):
                a = base + 2 * m + h
                both = jnp.where(low, rows[:, a, :], rows[:, a + half, :])
                out[(*at, slice(h * vl, (h + 1) * vl), slice(None))] = both.astype(jnp.bfloat16)
            return carry

        lax.fori_loop(0, count, gather, 0)


def pack(vt, plan, vl):
    shapes = []
    for _, _, count, shared in plan:
        lead = (count,) if shared else (2, count // 2)
        shapes.append(jax.ShapeDtypeStruct((*lead, 2 * vl, LANES), jnp.bfloat16))
    whole = pl.BlockSpec(memory_space=pltpu.VMEM)
    return pl.pallas_call(
        functools.partial(pack_kernel, plan),
        in_specs=[whole],
        out_specs=[whole] * len(plan),
        out_shape=shapes,
        scratch_shapes=[pltpu.VMEM((vl, NVIR, LANES), jnp.float32)],
        compiler_params=pltpu.CompilerParams(vmem_limit_bytes=VMEM),
        cost_estimate=pl.CostEstimate(flops=0, bytes_accessed=16 * 2**20, transcendentals=0),
    )(vt)


def combine_kernel(sources, first, count, own, n_prev, gathered, vt, *rest):
    arrivals = rest[: len(sources)]
    out = rest[len(sources) + n_prev]
    slot, lhs, direct, second, sems = rest[len(sources) + n_prev + 1 :]
    kw = vt.shape[0]
    pairs = out.shape[0]
    vl = slot.shape[3] // 2
    me, plane = position()
    i, xx, h = pl.program_id(0), pl.program_id(1), pl.program_id(2)

    @pl.when((i == 0) & (xx == 0) & (h == 0))
    def _():
        copies = []
        for n, (ref, (far, kind, start)) in enumerate(zip(arrivals, sources)):
            q = jnp.bitwise_xor(me, far)
            if kind == "both":
                copy = pltpu.make_async_copy(ref.at[:, pl.ds(start, count)], slot.at[q], sems.at[n])
            else:
                side = plane if kind == "own" else 1 - plane
                copy = pltpu.make_async_copy(ref.at[pl.ds(start, count)], slot.at[q, side], sems.at[n])
            copy.start()
            copies.append(copy)
        row = lax.broadcasted_iota(jnp.int32, (pairs, LANES), 0)
        col = lax.broadcasted_iota(jnp.int32, (pairs, LANES), 1)
        occ_i, occ_j = row // NOCC, row % NOCC
        per = pairs // NOCC
        zeros = jnp.zeros((kw, pairs), jnp.bfloat16)
        left = jnp.zeros((pairs, LANES), jnp.float32)
        right = jnp.zeros((pairs, LANES), jnp.float32)
        mine = jnp.zeros((pairs, kw), jnp.float32)
        for part in range(2):
            block = gathered[part * kw : (part + 1) * kw, :]
            swap = (occ_j // per == part) & (col == (occ_j % per) * NOCC + plane * per + occ_i)
            pick = jnp.where(swap, 1.0, 0.0).astype(jnp.bfloat16)
            left += lax.dot_general(pick, jnp.concatenate([block, zeros], axis=0), NT, preferred_element_type=jnp.float32)
            right += lax.dot_general(pick, jnp.concatenate([zeros, block], axis=0), NT, preferred_element_type=jnp.float32)
            keep = jnp.where((row == col) & (plane == part), 1.0, 0.0).astype(jnp.bfloat16)
            mine += lax.dot_general(keep, block, NT, preferred_element_type=jnp.float32)
        lhs[:pairs, :] = left.astype(jnp.bfloat16)
        lhs[pairs:, :] = right.astype(jnp.bfloat16)
        direct[...] = mine.astype(jnp.bfloat16)
        for copy in copies:
            copy.wait()

    ladder = lax.dot_general(direct[...], vt[...], NN, preferred_element_type=jnp.float32)

    @pl.when(h == 0)
    def _():
        blocks = [slot[q, xx, i].astype(jnp.float32) for q in range(slot.shape[0])]
        rows = [b[:vl] for b in blocks] + [b[vl:] for b in blocks]
        rhs = jnp.concatenate(rows, axis=0).astype(jnp.bfloat16)
        both = lax.dot_general(lhs[...], rhs, NT, preferred_element_type=jnp.float32)
        out[...] = ladder + both[:pairs]
        second[...] = both[pairs:]

    @pl.when(h == 1)
    def _():
        out[...] = ladder + second[...]


def combine(gathered, vt, arrivals, sources, first, count, previous, vl, pairs):
    n_dev = NVIR // vl
    steps = vl // 4
    width = 2 * NVIR
    any_space = pl.BlockSpec(memory_space=pl.ANY)

    def block(i, xx, h):
        return 0, 2 * (first + i) + xx + steps * h

    prev = [] if previous is None else [previous]
    return pl.pallas_call(
        functools.partial(combine_kernel, sources, first, count, None, len(prev)),
        grid=(count, 2, 2),
        in_specs=[
            pl.BlockSpec(gathered.shape, lambda i, xx, h: (0, 0)),
            pl.BlockSpec((vt.shape[0], width), block),
        ]
        + [any_space] * (len(arrivals) + len(prev)),
        out_specs=pl.BlockSpec((pairs, width), block),
        out_shape=jax.ShapeDtypeStruct((pairs, vl * NVIR), jnp.float32),
        scratch_shapes=[
            pltpu.VMEM((n_dev, 2, count, 2 * vl, LANES), jnp.bfloat16),
            pltpu.VMEM((2 * pairs, LANES), jnp.bfloat16),
            pltpu.VMEM((pairs, vt.shape[0]), jnp.bfloat16),
            pltpu.VMEM((pairs, width), jnp.float32),
            pltpu.SemaphoreType.DMA((len(sources),)),
        ],
        input_output_aliases={2 + len(arrivals): 0} if prev else {},
        compiler_params=pltpu.CompilerParams(vmem_limit_bytes=VMEM),
        cost_estimate=pl.CostEstimate(
            flops=8 * count * pairs * 3 * vt.shape[0] * width, bytes_accessed=count * 4 * pairs * width * 5, transcendentals=0
        ),
    )(gathered, vt, *arrivals, *prev)


def shards_fast(amplitudes, integrals):
    pairs = amplitudes.shape[0]
    vl = integrals.shape[0] // NVIR
    half = vl // 8
    late = 2
    early = half - late
    n_dev = NVIR // vl
    vt = integrals.T
    gathered = lax.all_gather(amplitudes.T, ("occ", "blk"), axis=0, tiled=True)

    def far_swap(x, far):
        return lax.ppermute(x, ("blk", "sub"), [(i, i ^ far) for i in range(n_dev)])

    def plane_swap(x):
        return lax.ppermute(x, "occ", [(0, 1), (1, 0)])

    center = pack(vt, [(4, 0, half, True), (5, 0, half, True), (6, 0, half, True), (7, 0, early, True), (7, early, late, True)], vl)
    near = pack(vt, [(f, 0, 2 * half, False) for f in range(4)], vl)
    got = [far_swap(x, f) for x, f in zip(center, (4, 5, 6, 7, 7))]
    forwarded = [plane_swap(x) for x in got]
    nears = [near[0]] + [far_swap(near[f], f) for f in (1, 2, 3)]

    def piece(start, count, last):
        arrivals, sources = [], []
        for f in range(4):
            arrivals.append(nears[f])
            sources.append((f, "both", start))
        for n, f in enumerate((4, 5, 6)):
            arrivals += [got[n], forwarded[n]]
            sources += [(f, "own", start), (f, "other", start)]
        arrivals += [got[last], forwarded[last]]
        sources += [(7, "own", 0), (7, "other", 0)]
        return arrivals, sources

    arrivals, sources = piece(0, early, 3)
    out = combine(gathered, vt, arrivals, sources, 0, early, None, vl, pairs)
    arrivals, sources = piece(early, late, 4)
    return combine(gathered, vt, arrivals, sources, early, late, out, vl, pairs)


def shards_any(amplitudes, integrals):
    pairs, columns = amplitudes.shape[0], integrals.shape[1]
    vl = integrals.shape[0] // NVIR
    per = pairs // NOCC
    swapped = lax.all_to_all(
        integrals.reshape(vl, NVIR, columns), ("blk", "sub"), split_axis=1, concat_axis=0, tiled=True
    )
    swapped = jnp.transpose(swapped, (1, 0, 2)).reshape(vl * NVIR, columns)
    whole = lax.all_gather(amplitudes, "blk", axis=1, tiled=True)
    every = lax.all_gather(whole, "occ", axis=0, tiled=True).reshape(NOCC, NOCC, columns)
    mine = lax.dynamic_slice_in_dim(every, lax.axis_index("occ") * per, per, axis=1)
    mine = jnp.transpose(mine, (1, 0, 2)).reshape(pairs, columns)
    return lax.dot_general(whole, integrals, NT, preferred_element_type=jnp.float32) + lax.dot_general(
        mine, swapped, NT, preferred_element_type=jnp.float32
    )


def shards(amplitudes, integrals):
    vl = integrals.shape[0] // NVIR
    fits = NVIR == 8 * vl and integrals.shape[1] * 2 == LANES and amplitudes.shape[0] == LANES
    fits = fits and lax.axis_size("blk") == 4 and lax.axis_size("sub") == 2 and lax.axis_size("occ") == 2
    return (shards_fast if fits else shards_any)(amplitudes, integrals)


def solution(mesh):
    placed = (P(("groups", "occ"), "blk"), P(("groups", "blk", "sub"), None))
    return jax.shard_map(
        shards,
        mesh=mesh,
        in_specs=placed,
        out_specs=P(("groups", "occ"), ("blk", "sub")),
        check_vma=False,
    )
```

time: 827 us -> 128 us (0.15)
  blocking collectives: 478 us -> 38.6 us
  local copies, waits for them, and re-layouts: 209 us -> 1.66 us
  other arithmetic: 125 us -> 0 us
  Pallas kernels: 0 us -> 45.2 us
  starting transfers between devices: 0 us -> 30.4 us
  waiting for transfers between devices: 0 us -> 10.6 us
    all_to_all x2 -> x0, blocking collectives: 463 us -> none  [the longest x1 287 us: shards(): lax.all_to_all(blocks, ('blk', 'sub'), split_axis=3, concat_axis=2, tiled...]
    all_to_all x1 -> x0, other arithmetic: 110 us -> none  [shards(): lax.all_to_all(blocks, ('blk', 'sub'), split_axis=3, concat_axis=2, tiled...]
    unnamed x6 -> x26, local copies, waits for them, and re-layouts: 77.8 us -> 1.66 us
    all_to_all x4 -> x0, local copies, waits for them, and re-layouts: 67.4 us -> none  [the longest x3 54.4 us: shards(): lax.all_to_all(blocks, ('blk', 'sub'), split_axis=3, concat_axis=2, tiled...]
    reshape x3 -> x0, local copies, waits for them, and re-layouts: 51 us -> none  [the longest x2 36.3 us: shards(): blocks = ladder.reshape(occ_local, NOCC, vir_local, NVIR)]
    pallas_call x0 -> x4, Pallas kernels: none -> 45.2 us  [the longest x2 26.8 us: combine(): pl.pallas_call(functools.partial(combine_kernel, sources, first, count, N...]
    ppermute x0 -> x13, starting transfers between devices: none -> 30.4 us  [the longest x8 24.2 us: far_swap(): return lax.ppermute(x, ('blk', 'sub'), [(i, i ^ far) for i in range(n_dev)])]
    all_gather x1, blocking collectives: 15.1 us -> 38.6 us  [shards_fast(): gathered = lax.all_gather(amplitudes.T, ('occ', 'blk'), axis=0, tiled=True)]
  transfers between devices with their start and end apart: 0 -> 13, of which waited for: 0 -> 3; matrix products, arithmetic and copies ran while one was open for 0% -> 0% of each run, Pallas kernels for 0% -> 23%
where the time goes in v1:
time: 128 us; the launch traced here: 127 us
  Pallas kernels  45.2 us (35%)
  blocking collectives  38.6 us (30%)
  starting transfers between devices  30.4 us (24%)
  waiting for transfers between devices  10.6 us (8%)
  local copies, waits for them, and re-layouts  1.66 us (1%)
    all_gather x1, blocking collectives, shards_fast(): gathered = lax.all_gather(amplitudes.T, ('occ', 'blk'), axis=0, tiled=True)  38.6 us
    pallas_call x2, Pallas kernels, combine(): pl.pallas_call(functools.partial(combine_kernel, sources, first, count, N...  26.8 us
    ppermute x8, starting transfers between devices, far_swap(): return lax.ppermute(x, ('blk', 'sub'), [(i, i ^ far) for i in range(n_dev)])  24.2 us
    pallas_call x2, Pallas kernels, pack(): pl.pallas_call(functools.partial(pack_kernel, plan), in_specs=[whole], ou...  18.4 us
    ppermute x5, starting transfers between devices, plane_swap(): return lax.ppermute(x, 'occ', [(0, 1), (1, 0)])  6.17 us
    ppermute x8, waiting for transfers between devices, far_swap(): return lax.ppermute(x, ('blk', 'sub'), [(i, i ^ far) for i in range(n_dev)])  5.32 us
    ppermute x5, waiting for transfers between devices, plane_swap(): return lax.ppermute(x, 'occ', [(0, 1), (1, 0)])  5.26 us
  transfers between devices with their start and end apart: 13, of which 3 were waited for; matrix products, arithmetic and copies ran while one was open for 0% of the time, Pallas kernels for 23%

profile of v1, /device:TPU:0, one launch (start us, length us, event | category | flops | bytes accessed | tf_op | source)
XLA Modules:
  0.0 126.6 jit_solution(10924958830634158350)
XLA Ops:
  0.0 8.1 %shard_map.29 = (bf16[7,112,128]{2,1,0:T(8,128)(2,1)}, bf16[7,112,128]{2,1,0:T(8,128)(2,1)}, bf16[7,112,128]{2,1,0:T(8,128)(2,1)}, bf16[5,112,128]{2,1,0:T(8,128)(2,1)}, bf16[2,112,128]{2,1,0:T(8,128)(2,1)}) custom-call(bf16[64,25088]{1,0:T(8,128)(2,1)} %bitcast.2), custom_call_target="tpu_custom_call" | custom-call | bytes 16777216 | tf_op jit(solution)/shard_map/pallas_call | solution.py:71
  8.1 4.0 %collective-permute-start.3 = (bf16[7,112,128]{2,1,0:T(8,128)(2,1)}, bf16[7,112,128]{2,1,0:T(8,128)(2,1)S(1)}, u32[]{:S(2)}, u32[]{:S(2)}) collective-permute-start(bf16[7,112,128]{2,1,0:T(8,128)(2,1)} %get-tuple-element.18), channel_id=1, source_target_pairs={{0,8},{1,9},{4,12},{5,13},{8,0},{9,1},{12,4},{13,5},{2,10},{3,11},... | collective-permute-start | bytes 602120 | tf_op jit(solution)/shard_map/ppermute | solution.py:188
  12.1 0.0 collective-permute-start.5
  12.1 3.1 %collective-permute-start.7 = (bf16[7,112,128]{2,1,0:T(8,128)(2,1)}, bf16[7,112,128]{2,1,0:T(8,128)(2,1)S(1)}, u32[]{:S(2)}, u32[]{:S(2)}) collective-permute-start(bf16[7,112,128]{2,1,0:T(8,128)(2,1)} %get-tuple-element.20), channel_id=1, source_target_pairs={{0,12},{1,13},{4,8},{5,9},{8,4},{9,5},{12,0},{13,1},{2,14},{3,15},... | collective-permute-start | bytes 602120 | tf_op jit(solution)/shard_map/ppermute | solution.py:188
  15.2 0.6 collective-permute-start.11
  15.8 3.0 %collective-permute-start.9 = (bf16[2,112,128]{2,1,0:T(8,128)(2,1)}, bf16[2,112,128]{2,1,0:T(8,128)(2,1)S(1)}, u32[]{:S(2)}, u32[]{:S(2)}) collective-permute-start(bf16[2,112,128]{2,1,0:T(8,128)(2,1)} %get-tuple-element.21), channel_id=1, source_target_pairs={{0,13},{1,12},{4,9},{5,8},{8,5},{9,4},{12,1},{13,0},{2,15},{3,14},... | collective-permute-start | bytes 172040 | tf_op jit(solution)/shard_map/ppermute | solution.py:188
  18.8 10.4 %shard_map.28 = (bf16[2,7,112,128]{3,2,1,0:T(8,128)(2,1)}, bf16[2,7,112,128]{3,2,1,0:T(8,128)(2,1)}, bf16[2,7,112,128]{3,2,1,0:T(8,128)(2,1)}, bf16[2,7,112,128]{3,2,1,0:T(8,128)(2,1)}) custom-call(bf16[64,25088]{1,0:T(8,128)(2,1)} %bitcast.3), custom_call_target="tpu_custom_call" | custom-call | bytes 16777216 | tf_op jit(solution)/shard_map/pallas_call | solution.py:71
  29.1 1.2 collective-permute-done.9.rest_10_
  30.3 0.9 collective-permute-start
  31.2 4.1 %collective-permute-done.3.rest_4_ = bf16[7,112,128]{2,1,0:T(8,128)(2,1)S(1)} collective-permute-done((bf16[7,112,128]{2,1,0:T(8,128)(2,1)}, bf16[7,112,128]{2,1,0:T(8,128)(2,1)S(1)}, u32[]{:S(2)}, u32[]{:S(2)}) %collective-permute-start.3) | collective-permute-done | bytes 200736 | tf_op jit(solution)/shard_map/ppermute | solution.py:188
  35.3 1.8 %collective-permute-start.4 = (bf16[7,112,128]{2,1,0:T(8,128)(2,1)S(1)}, bf16[7,112,128]{2,1,0:T(8,128)(2,1)S(1)}, u32[]{:S(2)}, u32[]{:S(2)}) collective-permute-start(bf16[7,112,128]{2,1,0:T(8,128)(2,1)S(1)} %collective-permute-done.3.rest_4_), channel_id=1, source_target_pairs={{0,2},{2,0},{1,3},{3,1},{4,6},{6,4},{5,7},{7,5},{8,10},{10,8},{9,1... | collective-permute-start | bytes 602120 | tf_op jit(solution)/shard_map/ppermute | solution.py:191
  37.2 0.0 collective-permute-done.11.rest_10_
  37.2 12.6 %collective-permute-start.1 = (bf16[2,7,112,128]{3,2,1,0:T(8,128)(2,1)}, bf16[2,7,112,128]{3,2,1,0:T(8,128)(2,1)S(1)}, u32[]{:S(2)}, u32[]{:S(2)}) collective-permute-start(bf16[2,7,112,128]{3,2,1,0:T(8,128)(2,1)} %get-tuple-element.16), channel_id=1, source_target_pairs={{0,4},{1,5},{4,0},{5,1},{8,12},{9,13},{12,8},{13,9},{2,6},{3,7},{6... | collective-permute-start | bytes 1204232 | tf_op jit(solution)/shard_map/ppermute | solution.py:188
  49.8 0.0 collective-permute-done.5.rest_6_
  49.8 0.0 collective-permute-start.2
  49.8 0.0 collective-permute-done.7.rest_8_
  49.8 0.0 copy-start.5
  49.9 0.6 collective-permute-start.12
  50.5 5.2 %collective-permute-done.12.rest_11_ = bf16[5,112,128]{2,1,0:T(8,128)(2,1)S(1)} collective-permute-done((bf16[5,112,128]{2,1,0:T(8,128)(2,1)S(1)}, bf16[5,112,128]{2,1,0:T(8,128)(2,1)S(1)}, u32[]{:S(2)}, u32[]{:S(2)}) %collective-permute-start.12) | collective-permute-done | bytes 143392 | tf_op jit(solution)/shard_map/ppermute | solution.py:191
  55.7 0.5 collective-permute-start.6
  56.2 0.0 collective-permute-done.4.rest_5_
  56.2 1.5 %collective-permute-start.8 = (bf16[7,112,128]{2,1,0:T(8,128)(2,1)S(1)}, bf16[7,112,128]{2,1,0:T(8,128)(2,1)S(1)}, u32[]{:S(2)}, u32[]{:S(2)}) collective-permute-start(bf16[7,112,128]{2,1,0:T(8,128)(2,1)S(1)} %collective-permute-done.7.rest_8_), channel_id=1, source_target_pairs={{0,2},{2,0},{1,3},{3,1},{4,6},{6,4},{5,7},{7,5},{8,10},{10,8},{9,1... | collective-permute-start | bytes 602120 | tf_op jit(solution)/shard_map/ppermute | solution.py:191
  57.7 38.6 %all_gather.3.gathered = bf16[128,128]{1,0:T(8,128)(2,1)} all-gather(bf16[16,128]{1,0:T(8,128)(2,1)} %bitcast.6), channel_id=1, replica_groups=mesh['groups'=2,'blk'=4,'occ'=2,'sub'=2] {'occ','blk'}, dimensions={0}, use_global_device_ids=true | all-gather | bytes 36864 | tf_op jit(solution)/shard_map/all_gather | solution.py:185
  96.3 0.0 collective-permute-done.6.rest_7_
  96.3 1.7 %collective-permute-start.10 = (bf16[2,112,128]{2,1,0:T(8,128)(2,1)S(1)}, bf16[2,112,128]{2,1,0:T(8,128)(2,1)S(1)}, u32[]{:S(2)}, u32[]{:S(2)}) collective-permute-start(bf16[2,112,128]{2,1,0:T(8,128)(2,1)S(1)} %collective-permute-done.9.rest_10_), channel_id=1, source_target_pairs={{0,2},{2,0},{1,3},{3,1},{4,6},{6,4},{5,7},{7,5},{8,10},{10,8},{9,1... | collective-permute-start | bytes 172040 | tf_op jit(solution)/shard_map/ppermute | solution.py:191
  98.0 0.0 collective-permute-done.8.rest_9_
  98.0 0.0 collective-permute-done.rest_1_
  98.0 0.0 copy-start
  98.0 0.0 collective-permute-done.1.rest_2_
  98.0 0.0 copy-start.1
  98.1 0.0 collective-permute-done.2.rest_3_
  98.1 0.0 copy-start.2
  98.1 0.0 copy-done.3
  98.1 0.0 copy-done.9
  98.1 0.0 copy-done.4
  98.1 0.0 copy-done.5
  98.1 0.0 copy-done.10
  98.1 0.0 copy-done.6
  98.1 0.5 copy-done.8
  98.7 0.1 copy-done
  98.8 0.1 copy-done.1
  99.0 0.2 copy-done.2
  99.2 18.3 %shard_map.30.rest_12_ = f32[128,25088]{1,0:T(8,128)} custom-call(bf16[128,128]{1,0:T(8,128)(2,1)} %all_gather.3.gathered, bf16[64,25088]{1,0:T(8,128)(2,1)} %bitcast.4, bf16[2,7,112,128]{3,2,1,0:T(8,128)(2,1)} %get-tuple-element.14.rest_0_, bf16[2,7,112,128]{3,2,1,0:T(8,128)(2,1)} %copy-done, bf16[2,7,112,128]{3,2,1,0:T(8,128)(2,1)} %copy-done.1, ...), custom_call_target="tpu_custom_call" | custom-call | flops 880803840 | bytes 11468800 | tf_op jit(solution)/shard_map/pallas_call | solution.py:152
  117.4 0.0 collective-permute-done.10.rest_11_
  117.4 0.0 copy-done.11
  117.5 0.0 copy-start.12
  117.5 0.6 copy-done.12
  118.1 8.5 %shard_map.31 = f32[128,25088]{1,0:T(8,128)} custom-call(bf16[128,128]{1,0:T(8,128)(2,1)} %all_gather.3.gathered, bf16[64,25088]{1,0:T(8,128)(2,1)} %bitcast.5, bf16[2,7,112,128]{3,2,1,0:T(8,128)(2,1)} %get-tuple-element.14.rest_0_, bf16[2,7,112,128]{3,2,1,0:T(8,128)(2,1)} %copy-done, ...), custom_call_target="tpu_custom_call", output_to_operand_aliasing={{}: (14, {})} | custom-call | flops 352321536 | bytes 4587520 | tf_op jit(solution)/shard_map/pallas_call | solution.py:152
  (9 shorter events, 0.0 us)
Async XLA Ops:
  8.1 27.3 %collective-permute-start.3 = (bf16[7,112,128]{2,1,0:T(8,128)(2,1)}, bf16[7,112,128]{2,1,0:T(8,128)(2,1)S(1)}, u32[]{:S(2)}, u32[]{:S(2)}) collective-permute-start(bf16[7,112,128]{2,1,0:T(8,128)(2,1)} %get-tuple-element.18), channel_id=1, source_target_pairs={{0,8},{1,9},{4,12},{5,13},{8,0},{9,1},{12,4},{13,5},{2,10},{3,11},... | collective-permute-start | bytes 602120 | tf_op jit(solution)/shard_map/ppermute | solution.py:188
  12.1 37.7 %collective-permute-start.5 = (bf16[7,112,128]{2,1,0:T(8,128)(2,1)}, bf16[7,112,128]{2,1,0:T(8,128)(2,1)S(1)}, u32[]{:S(2)}, u32[]{:S(2)}) collective-permute-start(bf16[7,112,128]{2,1,0:T(8,128)(2,1)} %get-tuple-element.19), channel_id=1, source_target_pairs={{0,9},{1,8},{4,13},{5,12},{8,1},{9,0},{12,5},{13,4},{2,11},{3,10},... | collective-permute-start | bytes 602120 | tf_op jit(solution)/shard_map/ppermute | solution.py:188
  12.1 37.7 %collective-permute-start.7 = (bf16[7,112,128]{2,1,0:T(8,128)(2,1)}, bf16[7,112,128]{2,1,0:T(8,128)(2,1)S(1)}, u32[]{:S(2)}, u32[]{:S(2)}) collective-permute-start(bf16[7,112,128]{2,1,0:T(8,128)(2,1)} %get-tuple-element.20), channel_id=1, source_target_pairs={{0,12},{1,13},{4,8},{5,9},{8,4},{9,5},{12,0},{13,1},{2,14},{3,15},... | collective-permute-start | bytes 602120 | tf_op jit(solution)/shard_map/ppermute | solution.py:188
  15.2 22.0 %collective-permute-start.11 = (bf16[5,112,128]{2,1,0:T(8,128)(2,1)}, bf16[5,112,128]{2,1,0:T(8,128)(2,1)S(1)}, u32[]{:S(2)}, u32[]{:S(2)}) collective-permute-start(bf16[5,112,128]{2,1,0:T(8,128)(2,1)} %get-tuple-element.22), channel_id=1, source_target_pairs={{0,13},{1,12},{4,9},{5,8},{8,5},{9,4},{12,1},{13,0},{2,15},{3,14},... | collective-permute-start | bytes 430088 | tf_op jit(solution)/shard_map/ppermute | solution.py:188
  15.8 14.5 %collective-permute-start.9 = (bf16[2,112,128]{2,1,0:T(8,128)(2,1)}, bf16[2,112,128]{2,1,0:T(8,128)(2,1)S(1)}, u32[]{:S(2)}, u32[]{:S(2)}) collective-permute-start(bf16[2,112,128]{2,1,0:T(8,128)(2,1)} %get-tuple-element.21), channel_id=1, source_target_pairs={{0,13},{1,12},{4,9},{5,8},{8,5},{9,4},{12,1},{13,0},{2,15},{3,14},... | collective-permute-start | bytes 172040 | tf_op jit(solution)/shard_map/ppermute | solution.py:188
  30.3 87.2 %copy-start.11 = (bf16[2,112,128]{2,1,0:T(8,128)(2,1)}, bf16[2,112,128]{2,1,0:T(8,128)(2,1)S(1)}, u32[]{:S(2)}) copy-start(bf16[2,112,128]{2,1,0:T(8,128)(2,1)S(1)} %collective-permute-done.9.rest_10_) | copy-start | bytes 172036
  30.3 67.7 %collective-permute-start = (bf16[2,7,112,128]{3,2,1,0:T(8,128)(2,1)}, bf16[2,7,112,128]{3,2,1,0:T(8,128)(2,1)S(1)}, u32[]{:S(2)}, u32[]{:S(2)}) collective-permute-start(bf16[2,7,112,128]{3,2,1,0:T(8,128)(2,1)} %get-tuple-element.15), channel_id=1, source_target_pairs={{0,1},{1,0},{4,5},{5,4},{8,9},{9,8},{12,13},{13,12},{2,3},{3,2},{6... | collective-permute-start | bytes 1204232 | tf_op jit(solution)/shard_map/ppermute | solution.py:188
  35.3 62.7 %copy-start.3 = (bf16[7,112,128]{2,1,0:T(8,128)(2,1)}, bf16[7,112,128]{2,1,0:T(8,128)(2,1)S(1)}, u32[]{:S(2)}) copy-start(bf16[7,112,128]{2,1,0:T(8,128)(2,1)S(1)} %collective-permute-done.3.rest_4_) | copy-start | bytes 602116
  35.3 20.9 %collective-permute-start.4 = (bf16[7,112,128]{2,1,0:T(8,128)(2,1)S(1)}, bf16[7,112,128]{2,1,0:T(8,128)(2,1)S(1)}, u32[]{:S(2)}, u32[]{:S(2)}) collective-permute-start(bf16[7,112,128]{2,1,0:T(8,128)(2,1)S(1)} %collective-permute-done.3.rest_4_), channel_id=1, source_target_pairs={{0,2},{2,0},{1,3},{3,1},{4,6},{6,4},{5,7},{7,5},{8,10},{10,8},{9,1... | collective-permute-start | bytes 602120 | tf_op jit(solution)/shard_map/ppermute | solution.py:191
  37.2 60.9 %copy-start.9 = (bf16[5,112,128]{2,1,0:T(8,128)(2,1)}, bf16[5,112,128]{2,1,0:T(8,128)(2,1)S(1)}, u32[]{:S(2)}) copy-start(bf16[5,112,128]{2,1,0:T(8,128)(2,1)S(1)} %collective-permute-done.11.rest_10_) | copy-start | bytes 430084
  37.2 60.8 %collective-permute-start.1 = (bf16[2,7,112,128]{3,2,1,0:T(8,128)(2,1)}, bf16[2,7,112,128]{3,2,1,0:T(8,128)(2,1)S(1)}, u32[]{:S(2)}, u32[]{:S(2)}) collective-permute-start(bf16[2,7,112,128]{3,2,1,0:T(8,128)(2,1)} %get-tuple-element.16), channel_id=1, source_target_pairs={{0,4},{1,5},{4,0},{5,1},{8,12},{9,13},{12,8},{13,9},{2,6},{3,7},{6... | collective-permute-start | bytes 1204232 | tf_op jit(solution)/shard_map/ppermute | solution.py:188
  49.8 48.3 %copy-start.4 = (bf16[7,112,128]{2,1,0:T(8,128)(2,1)}, bf16[7,112,128]{2,1,0:T(8,128)(2,1)S(1)}, u32[]{:S(2)}) copy-start(bf16[7,112,128]{2,1,0:T(8,128)(2,1)S(1)} %collective-permute-done.5.rest_6_) | copy-start | bytes 602116
  49.8 48.2 %collective-permute-start.2 = (bf16[2,7,112,128]{3,2,1,0:T(8,128)(2,1)}, bf16[2,7,112,128]{3,2,1,0:T(8,128)(2,1)S(1)}, u32[]{:S(2)}, u32[]{:S(2)}) collective-permute-start(bf16[2,7,112,128]{3,2,1,0:T(8,128)(2,1)} %get-tuple-element.17), channel_id=1, source_target_pairs={{0,5},{1,4},{4,1},{5,0},{8,13},{9,12},{12,9},{13,8},{2,7},{3,6},{6... | collective-permute-start | bytes 1204232 | tf_op jit(solution)/shard_map/ppermute | solution.py:188
  49.8 48.3 %copy-start.5 = (bf16[7,112,128]{2,1,0:T(8,128)(2,1)}, bf16[7,112,128]{2,1,0:T(8,128)(2,1)S(1)}, u32[]{:S(2)}) copy-start(bf16[7,112,128]{2,1,0:T(8,128)(2,1)S(1)} %collective-permute-done.7.rest_8_) | copy-start | bytes 602116
  49.9 5.8 %collective-permute-start.12 = (bf16[5,112,128]{2,1,0:T(8,128)(2,1)S(1)}, bf16[5,112,128]{2,1,0:T(8,128)(2,1)S(1)}, u32[]{:S(2)}, u32[]{:S(2)}) collective-permute-start(bf16[5,112,128]{2,1,0:T(8,128)(2,1)S(1)} %collective-permute-done.11.rest_10_), channel_id=1, source_target_pairs={{0,2},{2,0},{1,3},{3,1},{4,6},{6,4},{5,7},{7,5},{8,10},{10,8},{9,1... | collective-permute-start | bytes 430088 | tf_op jit(solution)/shard_map/ppermute | solution.py:191
  55.7 42.4 %copy-start.10 = (bf16[5,112,128]{2,1,0:T(8,128)(2,1)}, bf16[5,112,128]{2,1,0:T(8,128)(2,1)S(1)}, u32[]{:S(2)}) copy-start(bf16[5,112,128]{2,1,0:T(8,128)(2,1)S(1)} %collective-permute-done.12.rest_11_) | copy-start | bytes 430084
  55.7 40.6 %collective-permute-start.6 = (bf16[7,112,128]{2,1,0:T(8,128)(2,1)S(1)}, bf16[7,112,128]{2,1,0:T(8,128)(2,1)S(1)}, u32[]{:S(2)}, u32[]{:S(2)}) collective-permute-start(bf16[7,112,128]{2,1,0:T(8,128)(2,1)S(1)} %collective-permute-done.5.rest_6_), channel_id=1, source_target_pairs={{0,2},{2,0},{1,3},{3,1},{4,6},{6,4},{5,7},{7,5},{8,10},{10,8},{9,1... | collective-permute-start | bytes 602120 | tf_op jit(solution)/shard_map/ppermute | solution.py:191
  56.2 41.9 %copy-start.6 = (bf16[7,112,128]{2,1,0:T(8,128)(2,1)}, bf16[7,112,128]{2,1,0:T(8,128)(2,1)S(1)}, u32[]{:S(2)}) copy-start(bf16[7,112,128]{2,1,0:T(8,128)(2,1)S(1)} %collective-permute-done.4.rest_5_) | copy-start | bytes 602116
  56.2 41.8 %collective-permute-start.8 = (bf16[7,112,128]{2,1,0:T(8,128)(2,1)S(1)}, bf16[7,112,128]{2,1,0:T(8,128)(2,1)S(1)}, u32[]{:S(2)}, u32[]{:S(2)}) collective-permute-start(bf16[7,112,128]{2,1,0:T(8,128)(2,1)S(1)} %collective-permute-done.7.rest_8_), channel_id=1, source_target_pairs={{0,2},{2,0},{1,3},{3,1},{4,6},{6,4},{5,7},{7,5},{8,10},{10,8},{9,1... | collective-permute-start | bytes 602120 | tf_op jit(solution)/shard_map/ppermute | solution.py:191
  96.3 1.8 %copy-start.7 = (bf16[7,112,128]{2,1,0:T(8,128)(2,1)}, bf16[7,112,128]{2,1,0:T(8,128)(2,1)S(1)}, u32[]{:S(2)}) copy-start(bf16[7,112,128]{2,1,0:T(8,128)(2,1)S(1)} %collective-permute-done.6.rest_7_) | copy-start | bytes 602116
  96.3 21.1 %collective-permute-start.10 = (bf16[2,112,128]{2,1,0:T(8,128)(2,1)S(1)}, bf16[2,112,128]{2,1,0:T(8,128)(2,1)S(1)}, u32[]{:S(2)}, u32[]{:S(2)}) collective-permute-start(bf16[2,112,128]{2,1,0:T(8,128)(2,1)S(1)} %collective-permute-done.9.rest_10_), channel_id=1, source_target_pairs={{0,2},{2,0},{1,3},{3,1},{4,6},{6,4},{5,7},{7,5},{8,10},{10,8},{9,1... | collective-permute-start | bytes 172040 | tf_op jit(solution)/shard_map/ppermute | solution.py:191
  98.0 0.7 copy-start.8
  98.0 0.8 copy-start
  98.0 0.9 copy-start.1
  98.1 1.1 copy-start.2
  117.5 0.6 copy-start.12

commit v2 on v0

v2 whole, which is shorter than its diff:
```python
import functools

import jax
import jax.numpy as jnp
from jax import lax
from jax.experimental import pallas as pl
from jax.experimental.pallas import tpu as pltpu
from jax.sharding import PartitionSpec as P

NOCC = 16
NVIR = 448
LANES = 128
NT = (((1,), (1,)), ((), ()))
NN = (((1,), (0,)), ((), ()))


def position():
    return lax.axis_index("blk"), lax.axis_index("sub"), lax.axis_index("occ")


def far_of(cross, plane):
    return 2 * (2 + jnp.bitwise_xor(plane, cross)) + cross


def pack_kernel(plan, has_rider, vt, *rest):
    rider = rest[0] if has_rider else None
    outs = rest[has_rider : has_rider + len(plan)]
    local, rows, staged, in_sems, out_sems, rider_sem = rest[has_rider + len(plan) :]
    kw = vt.shape[0]
    vl = rows.shape[0]
    half = vl // 2
    tiles = 2 * NVIR // LANES
    chunks = in_sems.shape[0]
    per = vl // 2 // chunks
    z, core, plane = position()
    me = 2 * z + core

    def load(c):
        span = pl.ds(c * per * 2 * NVIR, per * 2 * NVIR)
        return pltpu.make_async_copy(vt.at[:, span], local.at[:, span], in_sems.at[c])

    for c in range(chunks):
        load(c).start()

    def turn(pair, carry):
        base = pl.multiple_of(pair * (2 * NVIR), LANES)
        for t in range(tiles):
            block = local[:, pl.ds(pl.multiple_of(base + t * LANES, LANES), LANES)]
            turned = jnp.concatenate([block, block], axis=0).T.astype(jnp.float32)
            start = t * LANES
            if start + LANES <= NVIR:
                rows[2 * pair, start : start + LANES, :] = turned
            elif start >= NVIR:
                rows[2 * pair + 1, start - NVIR : start - NVIR + LANES, :] = turned
            else:
                cut = NVIR - start
                rows[2 * pair, start:NVIR, :] = turned[:cut]
                rows[2 * pair + 1, 0 : LANES - cut, :] = turned[cut:]
        return carry

    for c in range(chunks):
        load(c).wait()
        lax.fori_loop(c * per, (c + 1) * per, turn, 0, unroll=True)

    low = lax.broadcasted_iota(jnp.int32, (vl, LANES), 1) < kw
    copies = []
    at = 0
    for n, (out, (kind, first, count, rides)) in enumerate(zip(outs, plan)):
        far = {"own": 0, "core": 1, "near": 2 + plane, "same": far_of(0, plane), "cross": far_of(1, plane)}[kind]
        base = jnp.bitwise_xor(me, far) * vl

        def gather(i, carry, base=base, first=first, at=at):
            both = []
            for h in range(2):
                a = base + 2 * (first + i) + h
                both.append(jnp.where(low, rows[:, a, :], rows[:, a + half, :]))
            spot = pl.multiple_of(at + i * 2 * vl, 16)
            staged[pl.ds(spot, 2 * vl), :] = jnp.concatenate(both, axis=0).astype(jnp.bfloat16)
            return carry

        lax.fori_loop(0, count, gather, 0)
        size = count * 2 * vl
        copy = pltpu.make_async_copy(staged.at[pl.ds(at, size)], out.at[pl.ds(0, size)], out_sems.at[n])
        copy.start()
        copies.append(copy)
        if rides:
            copy = pltpu.make_async_copy(rider, out.at[pl.ds(size, rider.shape[0])], rider_sem.at[n])
            copy.start()
            copies.append(copy)
        at += size
    for copy in copies:
        copy.wait()


def pack(vt, plan, vl, rider):
    sizes = [count * 2 * vl for _, _, count, _ in plan]
    extra = rider.shape[0]
    has_rider = any(rides for _, _, _, rides in plan)
    anywhere = pl.BlockSpec(memory_space=pl.ANY)
    chunks = 4
    return pl.pallas_call(
        functools.partial(pack_kernel, plan, has_rider),
        in_specs=[anywhere] * (1 + has_rider),
        out_specs=[anywhere] * len(plan),
        out_shape=[
            jax.ShapeDtypeStruct((size + extra * rides, LANES), jnp.bfloat16)
            for size, (_, _, _, rides) in zip(sizes, plan)
        ],
        scratch_shapes=[
            pltpu.VMEM(vt.shape, vt.dtype),
            pltpu.VMEM((vl, NVIR, LANES), jnp.float32),
            pltpu.VMEM((sum(sizes), LANES), jnp.bfloat16),
            pltpu.SemaphoreType.DMA((chunks,)),
            pltpu.SemaphoreType.DMA((len(plan),)),
            pltpu.SemaphoreType.DMA((len(plan),)),
        ],
        compiler_params=pltpu.CompilerParams(vmem_limit_bytes=24 * 2**20),
        cost_estimate=pl.CostEstimate(flops=0, bytes_accessed=16 * 2**20, transcendentals=0),
    )(vt, *([rider] if has_rider else []))


def amplitude_kernel(sides, own, others, tall, sems, z, plane):
    copies = [
        pltpu.make_async_copy(own, tall.at[plane, z], sems.at[0]),
        pltpu.make_async_copy(others[0], tall.at[1 - plane, z], sems.at[1]),
    ]
    for n, (ref, (kind, mine)) in enumerate(zip(others[1:], sides)):
        side = plane if mine else 1 - plane
        far = {"near": 1, "same": far_of(0, side) // 2, "cross": far_of(1, side) // 2}[kind]
        spot = tall.at[side, jnp.bitwise_xor(z, far)]
        size = spot.shape[0]
        copies.append(pltpu.make_async_copy(ref.at[pl.ds(ref.shape[0] - size, size)], spot, sems.at[2 + n]))
    return copies


def combine_kernel(sources, first, count, opening, vt, *rest):
    arrivals, rest = rest[: len(sources)], rest[len(sources) :]
    if opening:
        own, across, out, lhs, direct, slot, local, made, in_sems, vt_sems, out_sems, tall, tall_sems = rest
    else:
        lhs, direct, _, out, slot, local, made, in_sems, vt_sems, out_sems = rest
    kw = vt.shape[0]
    pairs = out.shape[0]
    vl = NVIR // slot.shape[0]
    steps = vl // 4
    width = 2 * NVIR
    z, core, plane = position()
    me = 2 * z + core

    copies = []
    for h in range(2):
        span = pl.ds((first + steps * h) * width, count * width)
        copies.append(pltpu.make_async_copy(vt.at[:, span], local.at[h], vt_sems.at[h]))
    for n, (ref, (kind, mine, start)) in enumerate(zip(arrivals, sources)):
        side = plane if mine else 1 - plane
        far = {"own": 0, "core": 1, "near": 2 + side, "same": far_of(0, side), "cross": far_of(1, side)}[kind]
        span = pl.ds(start * 2 * vl, count * 2 * vl)
        copies.append(pltpu.make_async_copy(ref.at[span], slot.at[jnp.bitwise_xor(me, far)], in_sems.at[n]))
    if opening:
        riders = [(ref, (kind, mine)) for ref, (kind, mine, _) in zip(arrivals, sources) if kind in ("near", "same", "cross")]
        gathers = amplitude_kernel([s for _, s in riders], own, [across] + [r for r, _ in riders], tall, tall_sems, z, plane)
        for copy in gathers + copies:
            copy.start()
        for copy in gathers:
            copy.wait()
        row = lax.broadcasted_iota(jnp.int32, (pairs, LANES), 0)
        col = lax.broadcasted_iota(jnp.int32, (pairs, LANES), 1)
        occ_i, occ_j = row // NOCC, row % NOCC
        per = pairs // NOCC
        zeros = jnp.zeros((kw, pairs), jnp.bfloat16)
        left = jnp.zeros((pairs, LANES), jnp.float32)
        right = jnp.zeros((pairs, LANES), jnp.float32)
        same = jnp.zeros((pairs, kw), jnp.float32)
        for part in range(2):
            block = tall[part].reshape(kw, pairs)
            swap = (occ_j // per == part) & (col == (occ_j % per) * NOCC + plane * per + occ_i)
            pick = jnp.where(swap, 1.0, 0.0).astype(jnp.bfloat16)
            left += lax.dot_general(pick, jnp.concatenate([block, zeros], axis=0), NT, preferred_element_type=jnp.float32)
            right += lax.dot_general(pick, jnp.concatenate([zeros, block], axis=0), NT, preferred_element_type=jnp.float32)
            keep = jnp.where((row == col) & (plane == part), 1.0, 0.0).astype(jnp.bfloat16)
            same += lax.dot_general(keep, block, NT, preferred_element_type=jnp.float32)
        lhs[:pairs, :] = left.astype(jnp.bfloat16)
        lhs[pairs:, :] = right.astype(jnp.bfloat16)
        direct[...] = same.astype(jnp.bfloat16)
    else:
        for copy in copies:
            copy.start()
    for copy in copies:
        copy.wait()

    def put(h, m):
        spot = pl.ds((first + m + steps * h) * width, width)
        return pltpu.make_async_copy(made.at[h, m], out.at[:, spot], out_sems.at[h, m])

    def step(m, carry):
        span = pl.ds(pl.multiple_of(m * 2 * vl, 16), 2 * vl)
        blocks = [slot[q, span, :].astype(jnp.float32) for q in range(slot.shape[0])]
        rhs = jnp.concatenate([b[:vl] for b in blocks] + [b[vl:] for b in blocks], axis=0).astype(jnp.bfloat16)
        both = lax.dot_general(lhs[...], rhs, NT, preferred_element_type=jnp.float32)
        for h in range(2):
            near = local[h, :, pl.ds(pl.multiple_of(m * width, LANES), width)]
            ladder = lax.dot_general(direct[...], near, NN, preferred_element_type=jnp.float32)
            made[h, m] = ladder + both[h * pairs : (h + 1) * pairs]
            put(h, m).start()
        return carry

    lax.fori_loop(0, count, step, 0)

    def finish(m, carry):
        for h in range(2):
            put(h, m).wait()
        return carry

    lax.fori_loop(0, count, finish, 0)


def combine(vt, arrivals, sources, first, count, vl, pairs, opening=None, later=None):
    kw, width, n_dev = vt.shape[0], 2 * NVIR, NVIR // vl
    anywhere = pl.BlockSpec(memory_space=pl.ANY)
    vmem = pl.BlockSpec(memory_space=pltpu.VMEM)
    out_shape = jax.ShapeDtypeStruct((pairs, vl * NVIR), jnp.float32)
    scratch = [
        pltpu.VMEM((n_dev, count * 2 * vl, LANES), jnp.bfloat16),
        pltpu.VMEM((2, kw, count * width), jnp.bfloat16),
        pltpu.VMEM((2, count, pairs, width), jnp.float32),
        pltpu.SemaphoreType.DMA((len(sources),)),
        pltpu.SemaphoreType.DMA((2,)),
        pltpu.SemaphoreType.DMA((2, count)),
    ]
    if opening is not None:
        extra = list(opening)
        specs = [anywhere] * 2
        outs = [out_shape, jax.ShapeDtypeStruct((2 * pairs, LANES), jnp.bfloat16), jax.ShapeDtypeStruct((pairs, kw), jnp.bfloat16)]
        out_specs = [anywhere, vmem, vmem]
        planes = 2
        scratch += [
            pltpu.VMEM((planes, kw // opening[0].shape[0], *opening[0].shape), jnp.bfloat16),
            pltpu.SemaphoreType.DMA((2 + len(sources),)),
        ]
        aliases = {}
    else:
        extra = list(later)
        specs = [vmem, vmem, anywhere]
        outs, out_specs = out_shape, anywhere
        aliases = {1 + len(arrivals) + 2: 0}
    return pl.pallas_call(
        functools.partial(combine_kernel, sources, first, count, opening is not None),
        in_specs=[anywhere] * (1 + len(arrivals)) + specs,
        out_specs=out_specs,
        out_shape=outs,
        scratch_shapes=scratch,
        input_output_aliases=aliases,
        compiler_params=pltpu.CompilerParams(vmem_limit_bytes=24 * 2**20),
        cost_estimate=pl.CostEstimate(
            flops=4 * count * pairs * 3 * kw * width, bytes_accessed=count * 2 * pairs * width * 6, transcendentals=0
        ),
    )(vt, *arrivals, *extra)


SIZES = (9, 5)


def shards_fast(amplitudes, integrals):
    pairs = amplitudes.shape[0]
    vl = integrals.shape[0] // NVIR
    steps = vl // 4
    vt = integrals.T
    own = amplitudes.T
    everyone = [(z, x, s) for z in range(4) for x in range(2) for s in range(2)]

    def number(z, x, s):
        return (z * 2 + x) * 2 + s

    def send(x, kind):
        def to(z, plane, s):
            if kind == "core":
                return number(z, plane, 1 - s)
            if kind == "plane":
                return number(z, 1 - plane, s)
            if kind == "near":
                return number(z ^ 1, plane, s ^ plane)
            cross = kind == "cross"
            return number(z ^ (2 + (plane ^ cross)), plane, s ^ cross)

        return lax.ppermute(x, ("blk", "occ", "sub"), [(number(*d), to(*d)) for d in everyone])

    across = send(own, "plane")
    spans, start = [], 0
    for size in SIZES:
        spans.append((start, size))
        start += size
    kinds = ("same", "cross")
    head = pack(vt, [(kind, *spans[0], True) for kind in kinds], vl, own)
    plan = [("near", 0, steps, True), ("core", 0, steps, False)]
    plan += [(kind, *span, False) for span in spans[1:] for kind in kinds]
    plan += [("own", 0, steps, False)]
    tail = pack(vt, plan, vl, own)
    near, core, mine = send(tail[0], "near"), send(tail[1], "core"), tail[-1]
    near_across = send(near, "plane")
    out = None
    for n, (first, count) in enumerate(spans):
        messages = head if n == 0 else tail[2 * n : 2 * n + 2]
        got = [send(x, kind) for x, kind in zip(messages, kinds)]
        passed = [send(x, "plane") for x in got]
        arrivals = [mine, core, near, near_across] + got + passed
        sources = [("own", True, first), ("core", True, first), ("near", True, first), ("near", False, first)]
        sources += [(kind, True, 0) for kind in kinds] + [(kind, False, 0) for kind in kinds]
        if n == 0:
            out, lhs, direct = combine(vt, arrivals, sources, first, count, vl, pairs, opening=(own, across))
        else:
            out = combine(vt, arrivals, sources, first, count, vl, pairs, later=(lhs, direct, out))
    return out


def shards_any(amplitudes, integrals):
    pairs, columns = amplitudes.shape[0], integrals.shape[1]
    vl = integrals.shape[0] // NVIR
    per = pairs // NOCC
    swapped = lax.all_to_all(
        integrals.reshape(vl, NVIR, columns), ("blk", "sub"), split_axis=1, concat_axis=0, tiled=True
    )
    swapped = jnp.transpose(swapped, (1, 0, 2)).reshape(vl * NVIR, columns)
    whole = lax.all_gather(amplitudes, "blk", axis=1, tiled=True)
    every = lax.all_gather(whole, "occ", axis=0, tiled=True).reshape(NOCC, NOCC, columns)
    mine = lax.dynamic_slice_in_dim(every, lax.axis_index("occ") * per, per, axis=1)
    mine = jnp.transpose(mine, (1, 0, 2)).reshape(pairs, columns)
    return lax.dot_general(whole, integrals, NT, preferred_element_type=jnp.float32) + lax.dot_general(
        mine, swapped, NT, preferred_element_type=jnp.float32
    )


def shards(amplitudes, integrals):
    vl = integrals.shape[0] // NVIR
    fits = NVIR == 8 * vl and integrals.shape[1] * 2 == LANES and amplitudes.shape[0] == LANES
    fits = fits and lax.axis_size("blk") == 4 and lax.axis_size("sub") == 2 and lax.axis_size("occ") == 2
    return (shards_fast if fits else shards_any)(amplitudes, integrals)


def solution(mesh):
    placed = (P(("groups", "occ"), "blk"), P(("groups", "blk", "sub"), None))
    return jax.shard_map(
        shards,
        mesh=mesh,
        in_specs=placed,
        out_specs=P(("groups", "occ"), ("blk", "sub")),
        check_vma=False,
    )
```

time: 827 us -> 71 us (0.09)
  blocking collectives: 478 us -> 0 us
  local copies, waits for them, and re-layouts: 209 us -> 2.59 us
  other arithmetic: 125 us -> 0 us
  waiting for transfers between devices: 0 us -> 26.1 us
  Pallas kernels: 0 us -> 23.6 us
  starting transfers between devices: 0 us -> 18.5 us
    all_to_all x2 -> x0, blocking collectives: 463 us -> none  [the longest x1 287 us: shards(): lax.all_to_all(blocks, ('blk', 'sub'), split_axis=3, concat_axis=2, tiled...]
    all_to_all x1 -> x0, other arithmetic: 110 us -> none  [shards(): lax.all_to_all(blocks, ('blk', 'sub'), split_axis=3, concat_axis=2, tiled...]
    unnamed x6 -> x4, local copies, waits for them, and re-layouts: 77.8 us -> 2.59 us
    all_to_all x4 -> x0, local copies, waits for them, and re-layouts: 67.4 us -> none  [the longest x3 54.4 us: shards(): lax.all_to_all(blocks, ('blk', 'sub'), split_axis=3, concat_axis=2, tiled...]
    reshape x3 -> x0, local copies, waits for them, and re-layouts: 51 us -> none  [the longest x2 36.3 us: shards(): blocks = ladder.reshape(occ_local, NOCC, vir_local, NVIR)]
    ppermute x0 -> x12, waiting for transfers between devices: none -> 26.1 us  [send(): lax.ppermute(x, ('blk', 'occ', 'sub'), [(number(*d), to(*d)) for d in eve...]
    pallas_call x0 -> x4, Pallas kernels: none -> 23.6 us  [the longest x2 12.9 us: combine(): pl.pallas_call(functools.partial(combine_kernel, sources, first, count, o...]
    ppermute x0 -> x12, starting transfers between devices: none -> 18.5 us  [send(): lax.ppermute(x, ('blk', 'occ', 'sub'), [(number(*d), to(*d)) for d in eve...]
  transfers between devices with their start and end apart: 0 -> 12, of which waited for: 0 -> 5; matrix products, arithmetic and copies ran while one was open for 0% -> 0% of each run, Pallas kernels for 0% -> 17%
where the time goes in v2:
time: 71 us; the launch traced here: 70.8 us
  waiting for transfers between devices  26.1 us (37%)
  Pallas kernels  23.6 us (33%)
  starting transfers between devices  18.5 us (26%)
  local copies, waits for them, and re-layouts  2.59 us (4%)
    ppermute x12, waiting for transfers between devices, send(): lax.ppermute(x, ('blk', 'occ', 'sub'), [(number(*d), to(*d)) for d in eve...  26.1 us
    ppermute x12, starting transfers between devices, send(): lax.ppermute(x, ('blk', 'occ', 'sub'), [(number(*d), to(*d)) for d in eve...  18.5 us
    pallas_call x2, Pallas kernels, combine(): pl.pallas_call(functools.partial(combine_kernel, sources, first, count, o...  12.9 us
    pallas_call x2, Pallas kernels, pack(): pl.pallas_call(functools.partial(pack_kernel, plan, has_rider), in_specs=...  10.7 us
    unnamed x4, local copies, waits for them, and re-layouts  2.59 us
  transfers between devices with their start and end apart: 12, of which 5 were waited for; matrix products, arithmetic and copies ran while one was open for 0% of the time, Pallas kernels for 17%

profile of v2, /device:TPU:0, one launch (start us, length us, event | category | flops | bytes accessed | tf_op | source)
XLA Modules:
  0.0 70.8 jit_solution(438837953306016374)
XLA Ops:
  0.0 0.0 copy-start
  0.0 1.9 %copy-done = bf16[25088,64]{0,1:T(8,128)(2,1)S(1)} copy-done((bf16[25088,64]{0,1:T(8,128)(2,1)S(1)}, bf16[25088,64]{0,1:T(8,128)(2,1)}, u32[]{:S(2)}) %copy-start) | copy-done | bytes 3211288
  1.9 0.0 copy-start.1
  1.9 0.7 copy-done.1
  2.6 6.7 %shard_map.28 = (bf16[1584,128]{1,0:T(8,128)(2,1)S(1)}, bf16[1568,128]{1,0:T(8,128)(2,1)S(1)}, bf16[560,128]{1,0:T(8,128)(2,1)S(1)}, bf16[560,128]{1,0:T(8,128)(2,1)S(1)}, bf16[1568,128]{1,0:T(8,128)(2,1)S(1)}) custom-call(bf16[64,25088]{1,0:T(8,128)(2,1)S(1)} %bitcast.2, bf16[16,128]{1,0:T(8,128)(2,1)S(1)} %bitcast.6), custom_call_target="tpu_custom_call" | custom-call | bytes 16777216 | tf_op jit(solution)/shard_map/pallas_call | solution.py:101
  9.3 3.1 %collective-permute-start.1 = (bf16[1584,128]{1,0:T(8,128)(2,1)S(1)}, bf16[1584,128]{1,0:T(8,128)(2,1)S(1)}, u32[]{:S(2)}, u32[]{:S(2)}) collective-permute-start(bf16[1584,128]{1,0:T(8,128)(2,1)S(1)} %get-tuple-element.17), channel_id=1, source_target_pairs={{0,4},{1,5},{2,7},{3,6},{4,0},{5,1},{6,3},{7,2},{8,12},{9,13},{10,... | collective-permute-start | bytes 1216520 | tf_op jit(solution)/shard_map/ppermute | solution.py:285
  12.4 4.1 %shard_map.29 = (bf16[1024,128]{1,0:T(8,128)(2,1)S(1)}, bf16[1024,128]{1,0:T(8,128)(2,1)S(1)}) custom-call(bf16[64,25088]{1,0:T(8,128)(2,1)S(1)} %bitcast.3, bf16[16,128]{1,0:T(8,128)(2,1)S(1)} %bitcast.7), custom_call_target="tpu_custom_call" | custom-call | bytes 16777216 | tf_op jit(solution)/shard_map/pallas_call | solution.py:101
  16.4 2.7 %collective-permute-start.7 = (bf16[1024,128]{1,0:T(8,128)(2,1)S(1)}, bf16[1024,128]{1,0:T(8,128)(2,1)S(1)}, u32[]{:S(2)}, u32[]{:S(2)}) collective-permute-start(bf16[1024,128]{1,0:T(8,128)(2,1)S(1)} %get-tuple-element.20), channel_id=1, source_target_pairs={{0,8},{1,9},{2,14},{3,15},{4,12},{5,13},{6,10},{7,11},{8,0},{9,1},... | collective-permute-start | bytes 786440 | tf_op jit(solution)/shard_map/ppermute | solution.py:285
  19.1 0.0 collective-permute-start.8
  19.1 0.1 collective-permute-start
  19.2 6.9 %collective-permute-done.1.rest_2_ = bf16[1584,128]{1,0:T(8,128)(2,1)S(1)} collective-permute-done((bf16[1584,128]{1,0:T(8,128)(2,1)S(1)}, bf16[1584,128]{1,0:T(8,128)(2,1)S(1)}, u32[]{:S(2)}, u32[]{:S(2)}) %collective-permute-start.1) | collective-permute-done | bytes 405536 | tf_op jit(solution)/shard_map/ppermute | solution.py:285
  26.1 0.0 collective-permute-start.2
  26.1 2.0 %collective-permute-start.11 = (bf16[16,128]{1,0:T(8,128)(2,1)S(1)}, bf16[16,128]{1,0:T(8,128)(2,1)S(1)}, u32[]{:S(2)}, u32[]{:S(2)}) collective-permute-start(bf16[16,128]{1,0:T(8,128)(2,1)S(1)} %bitcast.8), channel_id=1, source_target_pairs={{0,2},{1,3},{2,0},{3,1},{4,6},{5,7},{6,4},{7,5},{8,10},{9,11},{10,... | collective-permute-start | bytes 12296 | tf_op jit(solution)/shard_map/ppermute | solution.py:285
  28.1 8.6 %collective-permute-done.11.rest_9_ = bf16[16,128]{1,0:T(8,128)(2,1)S(1)} collective-permute-done((bf16[16,128]{1,0:T(8,128)(2,1)S(1)}, bf16[16,128]{1,0:T(8,128)(2,1)S(1)}, u32[]{:S(2)}, u32[]{:S(2)}) %collective-permute-start.11) | collective-permute-done | bytes 4128 | tf_op jit(solution)/shard_map/ppermute | solution.py:285
  36.7 0.5 collective-permute-start.3
  37.2 0.6 collective-permute-done.7.rest_4_
  37.9 6.8 %collective-permute-start.9 = (bf16[1024,128]{1,0:T(8,128)(2,1)S(1)}, bf16[1024,128]{1,0:T(8,128)(2,1)S(1)}, u32[]{:S(2)}, u32[]{:S(2)}) collective-permute-start(bf16[1024,128]{1,0:T(8,128)(2,1)S(1)} %collective-permute-done.7.rest_4_), channel_id=1, source_target_pairs={{0,2},{1,3},{2,0},{3,1},{4,6},{5,7},{6,4},{7,5},{8,10},{9,11},{10,... | collective-permute-start | bytes 786440 | tf_op jit(solution)/shard_map/ppermute | solution.py:285
  44.7 0.0 collective-permute-done.8.rest_5_
  44.7 0.1 collective-permute-start.10
  44.7 3.5 %collective-permute-done.3.rest_4_ = bf16[560,128]{1,0:T(8,128)(2,1)S(1)} collective-permute-done((bf16[560,128]{1,0:T(8,128)(2,1)S(1)}, bf16[560,128]{1,0:T(8,128)(2,1)S(1)}, u32[]{:S(2)}, u32[]{:S(2)}) %collective-permute-start.3) | collective-permute-done | bytes 143392 | tf_op jit(solution)/shard_map/ppermute | solution.py:285
  48.2 0.8 %collective-permute-start.4 = (bf16[560,128]{1,0:T(8,128)(2,1)S(1)}, bf16[560,128]{1,0:T(8,128)(2,1)S(1)}, u32[]{:S(2)}, u32[]{:S(2)}) collective-permute-start(bf16[560,128]{1,0:T(8,128)(2,1)S(1)} %get-tuple-element.19), channel_id=1, source_target_pairs={{0,13},{1,12},{2,11},{3,10},{4,9},{5,8},{6,15},{7,14},{8,5},{9,4},... | collective-permute-start | bytes 430088 | tf_op jit(solution)/shard_map/ppermute | solution.py:285
  49.0 6.4 %collective-permute-done.4.rest_5_ = bf16[560,128]{1,0:T(8,128)(2,1)S(1)} collective-permute-done((bf16[560,128]{1,0:T(8,128)(2,1)S(1)}, bf16[560,128]{1,0:T(8,128)(2,1)S(1)}, u32[]{:S(2)}, u32[]{:S(2)}) %collective-permute-start.4) | collective-permute-done | bytes 143392 | tf_op jit(solution)/shard_map/ppermute | solution.py:285
  55.4 2.5 %collective-permute-start.5 = (bf16[560,128]{1,0:T(8,128)(2,1)S(1)}, bf16[560,128]{1,0:T(8,128)(2,1)S(1)}, u32[]{:S(2)}, u32[]{:S(2)}) collective-permute-start(bf16[560,128]{1,0:T(8,128)(2,1)S(1)} %collective-permute-done.3.rest_4_), channel_id=1, source_target_pairs={{0,2},{1,3},{2,0},{3,1},{4,6},{5,7},{6,4},{7,5},{8,10},{9,11},{10,... | collective-permute-start | bytes 430088 | tf_op jit(solution)/shard_map/ppermute | solution.py:285
  57.9 0.0 collective-permute-done.rest_1_
  57.9 0.0 collective-permute-start.6
  57.9 0.0 collective-permute-done.9.rest_6_
  57.9 0.0 collective-permute-done.10.rest_7_
  57.9 0.0 collective-permute-done.2.rest_3_
  57.9 8.2 %shard_map.30 = (f32[128,25088]{1,0:T(8,128)}, bf16[256,128]{1,0:T(8,128)(2,1)S(1)}, bf16[128,64]{1,0:T(8,128)(2,1)S(1)}) custom-call(bf16[64,25088]{1,0:T(8,128)(2,1)S(1)} %bitcast.4, bf16[1568,128]{1,0:T(8,128)(2,1)S(1)} %get-tuple-element.15.rest_0_, bf16[1568,128]{1,0:T(8,128)(2,1)S(1)} %collective-permute-done.rest_1_, ...), custom_call_target="tpu_custom_call" | custom-call | flops 792723456 | bytes 12386304 | tf_op jit(solution)/shard_map/pallas_call | solution.py:246
  66.1 0.0 collective-permute-done.5.rest_6_
  66.1 0.0 collective-permute-done.6.rest_7_
  66.1 4.7 %shard_map.31 = f32[128,25088]{1,0:T(8,128)} custom-call(bf16[64,25088]{1,0:T(8,128)(2,1)S(1)} %bitcast.5, bf16[1568,128]{1,0:T(8,128)(2,1)S(1)} %get-tuple-element.15.rest_0_, bf16[1568,128]{1,0:T(8,128)(2,1)S(1)} %collective-permute-done.rest_1_, bf16[1584,128]{1,0:T(8,128)(2,1)S(1)} %collective-permute-done.1.rest_2_, ...), custom_call_target="tpu_custom_call", output_to_operand_aliasing={{}: (11, {})} | custom-call | flops 440401920 | bytes 6881280 | tf_op jit(solution)/shard_map/pallas_call | solution.py:246
Async XLA Ops:
  0.0 1.9 %copy-start = (bf16[25088,64]{0,1:T(8,128)(2,1)S(1)}, bf16[25088,64]{0,1:T(8,128)(2,1)}, u32[]{:S(2)}) copy-start(bf16[25088,64]{0,1:T(8,128)(2,1)} %param.3) | copy-start | bytes 9633796
  1.9 0.7 copy-start.1
  9.3 16.8 %collective-permute-start.1 = (bf16[1584,128]{1,0:T(8,128)(2,1)S(1)}, bf16[1584,128]{1,0:T(8,128)(2,1)S(1)}, u32[]{:S(2)}, u32[]{:S(2)}) collective-permute-start(bf16[1584,128]{1,0:T(8,128)(2,1)S(1)} %get-tuple-element.17), channel_id=1, source_target_pairs={{0,4},{1,5},{2,7},{3,6},{4,0},{5,1},{6,3},{7,2},{8,12},{9,13},{10,... | collective-permute-start | bytes 1216520 | tf_op jit(solution)/shard_map/ppermute | solution.py:285
  16.4 21.4 %collective-permute-start.7 = (bf16[1024,128]{1,0:T(8,128)(2,1)S(1)}, bf16[1024,128]{1,0:T(8,128)(2,1)S(1)}, u32[]{:S(2)}, u32[]{:S(2)}) collective-permute-start(bf16[1024,128]{1,0:T(8,128)(2,1)S(1)} %get-tuple-element.20), channel_id=1, source_target_pairs={{0,8},{1,9},{2,14},{3,15},{4,12},{5,13},{6,10},{7,11},{8,0},{9,1},... | collective-permute-start | bytes 786440 | tf_op jit(solution)/shard_map/ppermute | solution.py:285
  19.1 25.6 %collective-permute-start.8 = (bf16[1024,128]{1,0:T(8,128)(2,1)S(1)}, bf16[1024,128]{1,0:T(8,128)(2,1)S(1)}, u32[]{:S(2)}, u32[]{:S(2)}) collective-permute-start(bf16[1024,128]{1,0:T(8,128)(2,1)S(1)} %get-tuple-element.21), channel_id=1, source_target_pairs={{0,13},{1,12},{2,11},{3,10},{4,9},{5,8},{6,15},{7,14},{8,5},{9,4},... | collective-permute-start | bytes 786440 | tf_op jit(solution)/shard_map/ppermute | solution.py:285
  19.1 38.8 %collective-permute-start = (bf16[1568,128]{1,0:T(8,128)(2,1)S(1)}, bf16[1568,128]{1,0:T(8,128)(2,1)S(1)}, u32[]{:S(2)}, u32[]{:S(2)}) collective-permute-start(bf16[1568,128]{1,0:T(8,128)(2,1)S(1)} %get-tuple-element.16), channel_id=1, source_target_pairs={{0,1},{1,0},{2,3},{3,2},{4,5},{5,4},{6,7},{7,6},{8,9},{9,8},{10,11... | collective-permute-start | bytes 1204232 | tf_op jit(solution)/shard_map/ppermute | solution.py:285
  26.1 31.9 %collective-permute-start.2 = (bf16[1584,128]{1,0:T(8,128)(2,1)S(1)}, bf16[1584,128]{1,0:T(8,128)(2,1)S(1)}, u32[]{:S(2)}, u32[]{:S(2)}) collective-permute-start(bf16[1584,128]{1,0:T(8,128)(2,1)S(1)} %collective-permute-done.1.rest_2_), channel_id=1, source_target_pairs={{0,2},{1,3},{2,0},{3,1},{4,6},{5,7},{6,4},{7,5},{8,10},{9,11},{10,... | collective-permute-start | bytes 1216520 | tf_op jit(solution)/shard_map/ppermute | solution.py:285
  26.1 10.6 %collective-permute-start.11 = (bf16[16,128]{1,0:T(8,128)(2,1)S(1)}, bf16[16,128]{1,0:T(8,128)(2,1)S(1)}, u32[]{:S(2)}, u32[]{:S(2)}) collective-permute-start(bf16[16,128]{1,0:T(8,128)(2,1)S(1)} %bitcast.8), channel_id=1, source_target_pairs={{0,2},{1,3},{2,0},{3,1},{4,6},{5,7},{6,4},{7,5},{8,10},{9,11},{10,... | collective-permute-start | bytes 12296 | tf_op jit(solution)/shard_map/ppermute | solution.py:285
  36.7 11.5 %collective-permute-start.3 = (bf16[560,128]{1,0:T(8,128)(2,1)S(1)}, bf16[560,128]{1,0:T(8,128)(2,1)S(1)}, u32[]{:S(2)}, u32[]{:S(2)}) collective-permute-start(bf16[560,128]{1,0:T(8,128)(2,1)S(1)} %get-tuple-element.18), channel_id=1, source_target_pairs={{0,8},{1,9},{2,14},{3,15},{4,12},{5,13},{6,10},{7,11},{8,0},{9,1},... | collective-permute-start | bytes 430088 | tf_op jit(solution)/shard_map/ppermute | solution.py:285
  37.9 20.0 %collective-permute-start.9 = (bf16[1024,128]{1,0:T(8,128)(2,1)S(1)}, bf16[1024,128]{1,0:T(8,128)(2,1)S(1)}, u32[]{:S(2)}, u32[]{:S(2)}) collective-permute-start(bf16[1024,128]{1,0:T(8,128)(2,1)S(1)} %collective-permute-done.7.rest_4_), channel_id=1, source_target_pairs={{0,2},{1,3},{2,0},{3,1},{4,6},{5,7},{6,4},{7,5},{8,10},{9,11},{10,... | collective-permute-start | bytes 786440 | tf_op jit(solution)/shard_map/ppermute | solution.py:285
  44.7 13.3 %collective-permute-start.10 = (bf16[1024,128]{1,0:T(8,128)(2,1)S(1)}, bf16[1024,128]{1,0:T(8,128)(2,1)S(1)}, u32[]{:S(2)}, u32[]{:S(2)}) collective-permute-start(bf16[1024,128]{1,0:T(8,128)(2,1)S(1)} %collective-permute-done.8.rest_5_), channel_id=1, source_target_pairs={{0,2},{1,3},{2,0},{3,1},{4,6},{5,7},{6,4},{7,5},{8,10},{9,11},{10,... | collective-permute-start | bytes 786440 | tf_op jit(solution)/shard_map/ppermute | solution.py:285
  48.2 7.2 %collective-permute-start.4 = (bf16[560,128]{1,0:T(8,128)(2,1)S(1)}, bf16[560,128]{1,0:T(8,128)(2,1)S(1)}, u32[]{:S(2)}, u32[]{:S(2)}) collective-permute-start(bf16[560,128]{1,0:T(8,128)(2,1)S(1)} %get-tuple-element.19), channel_id=1, source_target_pairs={{0,13},{1,12},{2,11},{3,10},{4,9},{5,8},{6,15},{7,14},{8,5},{9,4},... | collective-permute-start | bytes 430088 | tf_op jit(solution)/shard_map/ppermute | solution.py:285
  55.4 10.7 %collective-permute-start.5 = (bf16[560,128]{1,0:T(8,128)(2,1)S(1)}, bf16[560,128]{1,0:T(8,128)(2,1)S(1)}, u32[]{:S(2)}, u32[]{:S(2)}) collective-permute-start(bf16[560,128]{1,0:T(8,128)(2,1)S(1)} %collective-permute-done.3.rest_4_), channel_id=1, source_target_pairs={{0,2},{1,3},{2,0},{3,1},{4,6},{5,7},{6,4},{7,5},{8,10},{9,11},{10,... | collective-permute-start | bytes 430088 | tf_op jit(solution)/shard_map/ppermute | solution.py:285
  57.9 8.2 %collective-permute-start.6 = (bf16[560,128]{1,0:T(8,128)(2,1)S(1)}, bf16[560,128]{1,0:T(8,128)(2,1)S(1)}, u32[]{:S(2)}, u32[]{:S(2)}) collective-permute-start(bf16[560,128]{1,0:T(8,128)(2,1)S(1)} %collective-permute-done.4.rest_5_), channel_id=1, source_target_pairs={{0,2},{1,3},{2,0},{3,1},{4,6},{5,7},{6,4},{7,5},{8,10},{9,11},{10,... | collective-permute-start | bytes 430088 | tf_op jit(solution)/shard_map/ppermute | solution.py:285

commit v3 on v2

v3 whole, which is shorter than its diff:
```python
import functools

import jax
import jax.numpy as jnp
from jax import lax
from jax.experimental import pallas as pl
from jax.experimental.pallas import tpu as pltpu
from jax.sharding import PartitionSpec as P

NOCC = 16
NVIR = 448
LANES = 128
NT = (((1,), (1,)), ((), ()))
NN = (((1,), (0,)), ((), ()))


def position():
    return lax.axis_index("blk"), lax.axis_index("sub"), lax.axis_index("occ")


def far_of(cross, plane):
    return 2 * (2 + jnp.bitwise_xor(plane, cross)) + cross


def pack_kernel(plan, opening, vt, *rest):
    if opening:
        amplitudes, outs, (local, rider) = rest[0], rest[1 : 1 + len(plan)], rest[1 + len(plan) : 3 + len(plan)]
        rows, in_sems, rider_sem = rest[3 + len(plan) :]
    else:
        outs, rows, local = rest[: len(plan)], rest[len(plan)], vt
    kw = vt.shape[0]
    vl = rows.shape[0]
    half = vl // 2
    tiles = 2 * NVIR // LANES
    chunks = in_sems.shape[0] if opening else 4
    per = vl // 2 // chunks
    z, core, plane = position()
    me = 2 * z + core

    def load(c):
        span = pl.ds(c * per * 2 * NVIR, per * 2 * NVIR)
        return pltpu.make_async_copy(vt.at[:, span], local.at[:, span], in_sems.at[c])

    if opening:
        for c in range(chunks):
            load(c).start()
        ride = pltpu.make_async_copy(amplitudes, rider, rider_sem)
        ride.start()

    def turn(pair, carry):
        base = pl.multiple_of(pair * (2 * NVIR), LANES)
        for t in range(tiles):
            block = local[:, pl.ds(pl.multiple_of(base + t * LANES, LANES), LANES)]
            turned = jnp.concatenate([block, block], axis=0).T.astype(jnp.float32)
            start = t * LANES
            if start + LANES <= NVIR:
                rows[2 * pair, start : start + LANES, :] = turned
            elif start >= NVIR:
                rows[2 * pair + 1, start - NVIR : start - NVIR + LANES, :] = turned
            else:
                cut = NVIR - start
                rows[2 * pair, start:NVIR, :] = turned[:cut]
                rows[2 * pair + 1, 0 : LANES - cut, :] = turned[cut:]
        return carry

    for c in range(chunks):
        if opening:
            load(c).wait()
        lax.fori_loop(c * per, (c + 1) * per, turn, 0, unroll=True)
    if opening:
        ride.wait()

    low = lax.broadcasted_iota(jnp.int32, (vl, LANES), 1) < kw
    for out, (kind, first, count, rides) in zip(outs, plan):
        far = {"own": 0, "core": 1, "near": 2 + plane, "same": far_of(0, plane), "cross": far_of(1, plane)}[kind]
        base = jnp.bitwise_xor(me, far) * vl

        def gather(i, carry, out=out, base=base, first=first):
            both = []
            for h in range(2):
                a = base + 2 * (first + i) + h
                both.append(jnp.where(low, rows[:, a, :], rows[:, a + half, :]))
            spot = pl.multiple_of(i * 2 * vl, 16)
            out[pl.ds(spot, 2 * vl), :] = jnp.concatenate(both, axis=0).astype(jnp.bfloat16)
            return carry

        lax.fori_loop(0, count, gather, 0)
        if rides:
            out[count * 2 * vl :, :] = rider[...]


def pack(vt, plan, vl, amplitudes=None):
    extra = 0 if amplitudes is None else amplitudes.shape[0]
    opening = amplitudes is not None
    vmem = pl.BlockSpec(memory_space=pltpu.VMEM)
    anywhere = pl.BlockSpec(memory_space=pl.ANY)
    chunks = 4
    shapes = [
        jax.ShapeDtypeStruct((count * 2 * vl + extra * rides, LANES), jnp.bfloat16) for _, _, count, rides in plan
    ]
    scratch = [pltpu.VMEM((vl, NVIR, LANES), jnp.float32)]
    if opening:
        shapes += [jax.ShapeDtypeStruct(x.shape, x.dtype) for x in (vt, amplitudes)]
        scratch += [pltpu.SemaphoreType.DMA((chunks,)), pltpu.SemaphoreType.DMA]
    return pl.pallas_call(
        functools.partial(pack_kernel, plan, opening),
        in_specs=[anywhere, anywhere] if opening else [vmem],
        out_specs=[vmem] * len(shapes),
        out_shape=shapes,
        scratch_shapes=scratch,
        compiler_params=pltpu.CompilerParams(vmem_limit_bytes=(HEAD_MB if opening else 20) * 2**20),
        cost_estimate=pl.CostEstimate(flops=0, bytes_accessed=PACK_COST * 2**20, transcendentals=0),
    )(vt, *([amplitudes] if opening else []))


def combine_kernel(sources, first, count, opening, vt, *rest):
    arrivals, rest = rest[: len(sources)], rest[len(sources) :]
    if opening:
        own, across, out, lhs, direct, turned, made, out_sems, tall = rest
    else:
        lhs, direct, _, out, turned, made, out_sems = rest
    kw = vt.shape[0]
    pairs = out.shape[0]
    n_dev = turned.shape[1] // 2
    vl = NVIR // n_dev
    steps = vl // 4
    width = 2 * NVIR
    z, core, plane = position()
    me = 2 * z + core

    def far(kind, side):
        return {"own": 0, "core": 1, "near": 2 + side, "same": far_of(0, side), "cross": far_of(1, side)}[kind]

    if opening:
        size = own.shape[0]
        tall[plane, z] = own[...]
        tall[1 - plane, z] = across[...]
        for ref, (kind, mine, start, at, _) in zip(arrivals, sources):
            if kind in ("near", "same", "cross") and start == 0 and at == 0:
                side = plane if mine else 1 - plane
                there = jnp.bitwise_xor(z, 1 if kind == "near" else far(kind, side) // 2)
                tall[side, there] = ref[ref.shape[0] - size :, :]
        row = lax.broadcasted_iota(jnp.int32, (pairs, LANES), 0)
        col = lax.broadcasted_iota(jnp.int32, (pairs, LANES), 1)
        occ_i, occ_j = row // NOCC, row % NOCC
        per = pairs // NOCC
        zeros = jnp.zeros((kw, pairs), jnp.bfloat16)
        left = jnp.zeros((pairs, LANES), jnp.float32)
        right = jnp.zeros((pairs, LANES), jnp.float32)
        same = jnp.zeros((pairs, kw), jnp.float32)
        for part in range(2):
            block = tall[part].reshape(kw, pairs)
            swap = (occ_j // per == part) & (col == (occ_j % per) * NOCC + plane * per + occ_i)
            pick = jnp.where(swap, 1.0, 0.0).astype(jnp.bfloat16)
            left += lax.dot_general(pick, jnp.concatenate([block, zeros], axis=0), NT, preferred_element_type=jnp.float32)
            right += lax.dot_general(pick, jnp.concatenate([zeros, block], axis=0), NT, preferred_element_type=jnp.float32)
            keep = jnp.where((row == col) & (plane == part), 1.0, 0.0).astype(jnp.bfloat16)
            same += lax.dot_general(keep, block, NT, preferred_element_type=jnp.float32)
        lhs[:pairs, :] = left.astype(jnp.bfloat16)
        lhs[pairs:, :] = right.astype(jnp.bfloat16)
        direct[...] = same.astype(jnp.bfloat16)

    def put(h, m):
        spot = pl.ds((first + m + steps * h) * width, width)
        return pltpu.make_async_copy(made.at[h, m], out.at[:, spot], out_sems.at[h, m])

    for m in range(count):
        buffer = turned.at[m % turned.shape[0]]
        for ref, (kind, mine, start, at, size) in zip(arrivals, sources):
            if at <= m < at + size:
                q = jnp.bitwise_xor(me, far(kind, plane if mine else 1 - plane))
                block = ref[(start + m - at) * 2 * vl : (start + m - at + 1) * 2 * vl, :].astype(jnp.float32)
                buffer[q] = block[:vl]
                buffer[q + n_dev] = block[vl:]
        rhs = buffer[...].reshape(2 * NVIR, LANES).astype(jnp.bfloat16)
        both = lax.dot_general(lhs[...], rhs, NT, preferred_element_type=jnp.float32)
        for h in range(2):
            begin = (first + m + steps * h) * width
            ladder = lax.dot_general(direct[...], vt[:, begin : begin + width], NN, preferred_element_type=jnp.float32)
            made[h, m] = ladder + both[h * pairs : (h + 1) * pairs]
            put(h, m).start()
    for m in range(count):
        for h in range(2):
            put(h, m).wait()


def combine(vt, arrivals, sources, first, count, vl, pairs, opening=None, later=None):
    kw, width, n_dev = vt.shape[0], 2 * NVIR, NVIR // vl
    anywhere = pl.BlockSpec(memory_space=pl.ANY)
    vmem = pl.BlockSpec(memory_space=pltpu.VMEM)
    out_shape = jax.ShapeDtypeStruct((pairs, vl * NVIR), jnp.float32)
    scratch = [
        pltpu.VMEM((2, 2 * n_dev, vl, LANES), jnp.float32),
        pltpu.VMEM((2, count, pairs, width), jnp.float32),
        pltpu.SemaphoreType.DMA((2, count)),
    ]
    if opening is not None:
        extra = list(opening)
        specs = [vmem] * 2
        outs = [out_shape, jax.ShapeDtypeStruct((2 * pairs, LANES), jnp.bfloat16), jax.ShapeDtypeStruct((pairs, kw), jnp.bfloat16)]
        out_specs = [anywhere, vmem, vmem]
        scratch += [pltpu.VMEM((2, kw // opening[0].shape[0], *opening[0].shape), jnp.bfloat16)]
        aliases = {}
    else:
        extra = list(later)
        specs = [vmem, vmem, anywhere]
        outs, out_specs = out_shape, anywhere
        aliases = {1 + len(arrivals) + 2: 0}
    return pl.pallas_call(
        functools.partial(combine_kernel, sources, first, count, opening is not None),
        in_specs=[vmem] * (1 + len(arrivals)) + specs,
        out_specs=out_specs,
        out_shape=outs,
        scratch_shapes=scratch,
        input_output_aliases=aliases,
        compiler_params=pltpu.CompilerParams(vmem_limit_bytes=20 * 2**20),
        cost_estimate=pl.CostEstimate(
            flops=4 * count * pairs * 3 * kw * width, bytes_accessed=count * 2 * pairs * width * 6, transcendentals=0
        ),
    )(vt, *arrivals, *extra)


HEAD_MB = 54
PACK_COST = 16
FLOWS = (('same', 0, 6, None), ('cross', 0, 9, None), ('near', 0, 14, None), ('same', 6, 5, 0), ('cross', 9, 5, 1), ('same', 11, 3, 3))
PIECES = ((0, 9), (9, 5))


def shards_fast(amplitudes, integrals):
    pairs = amplitudes.shape[0]
    vl = integrals.shape[0] // NVIR
    steps = vl // 4
    everyone = [(z, x, s) for z in range(4) for x in range(2) for s in range(2)]

    def number(z, x, s):
        return (z * 2 + x) * 2 + s

    def send(x, kind):
        def to(z, plane, s):
            if kind == "core":
                return number(z, plane, 1 - s)
            if kind == "plane":
                return number(z, 1 - plane, s)
            if kind == "near":
                return number(z ^ 1, plane, s ^ plane)
            cross = kind == "cross"
            return number(z ^ (2 + (plane ^ cross)), plane, s ^ cross)

        return lax.ppermute(x, ("blk", "occ", "sub"), [(number(*d), to(*d)) for d in everyone])

    def before(first, then):
        return lax.optimization_barrier((first, then))

    across = send(amplitudes.T, "plane")
    heads = [f for f, flow in enumerate(FLOWS) if flow[3] is None]
    tails = [f for f, flow in enumerate(FLOWS) if flow[3] is not None]
    plan = [(*FLOWS[f][:3], FLOWS[f][1] == 0) for f in heads]
    *packed, vt, own = pack(integrals.T, plan, vl, amplitudes.T)
    messages = dict(zip(heads, packed))
    across, messages[0] = before(across, messages[0])
    plan = [("core", 0, steps, False), ("own", 0, steps, False)] + [(*FLOWS[f][:3], False) for f in tails]
    core, mine, *packed = pack(vt, plan, vl)
    messages.update(zip(tails, packed))
    core = send(core, "core")
    got = []
    for f, (kind, _, _, after) in enumerate(FLOWS):
        if after is not None:
            got[after], messages[f] = before(got[after], messages[f])
        got.append(send(messages[f], kind))
    passed = [send(x, "plane") for x in got]
    out = None
    for n, (first, count) in enumerate(PIECES):
        arrivals = [mine, core]
        sources = [("own", True, first, 0, count), ("core", True, first, 0, count)]
        for flow, (kind, start, size, _) in enumerate(FLOWS):
            low, high = max(first, start), min(first + count, start + size)
            if low < high:
                arrivals += [got[flow], passed[flow]]
                span = (low - start, low - first, high - low)
                sources += [(kind, True, *span), (kind, False, *span)]
        if n == 0:
            out, lhs, direct = combine(vt, arrivals, sources, first, count, vl, pairs, opening=(own, across))
        else:
            out = combine(vt, arrivals, sources, first, count, vl, pairs, later=(lhs, direct, out))
    return out


def shards_any(amplitudes, integrals):
    pairs, columns = amplitudes.shape[0], integrals.shape[1]
    vl = integrals.shape[0] // NVIR
    per = pairs // NOCC
    swapped = lax.all_to_all(
        integrals.reshape(vl, NVIR, columns), ("blk", "sub"), split_axis=1, concat_axis=0, tiled=True
    )
    swapped = jnp.transpose(swapped, (1, 0, 2)).reshape(vl * NVIR, columns)
    whole = lax.all_gather(amplitudes, "blk", axis=1, tiled=True)
    every = lax.all_gather(whole, "occ", axis=0, tiled=True).reshape(NOCC, NOCC, columns)
    mine = lax.dynamic_slice_in_dim(every, lax.axis_index("occ") * per, per, axis=1)
    mine = jnp.transpose(mine, (1, 0, 2)).reshape(pairs, columns)
    return lax.dot_general(whole, integrals, NT, preferred_element_type=jnp.float32) + lax.dot_general(
        mine, swapped, NT, preferred_element_type=jnp.float32
    )


def shards(amplitudes, integrals):
    vl = integrals.shape[0] // NVIR
    fits = NVIR == 8 * vl and integrals.shape[1] * 2 == LANES and amplitudes.shape[0] == LANES
    fits = fits and lax.axis_size("blk") == 4 and lax.axis_size("sub") == 2 and lax.axis_size("occ") == 2
    return (shards_fast if fits else shards_any)(amplitudes, integrals)


def solution(mesh):
    placed = (P(("groups", "occ"), "blk"), P(("groups", "blk", "sub"), None))
    return jax.shard_map(
        shards,
        mesh=mesh,
        in_specs=placed,
        out_specs=P(("groups", "occ"), ("blk", "sub")),
        check_vma=False,
    )
```

time: 71 us -> 60.5 us (0.85)
  waiting for transfers between devices: 26.1 us -> 13.5 us
  starting transfers between devices: 18.5 us -> 26.3 us
  Pallas kernels: 23.6 us -> 17.9 us
    ppermute x12 -> x14, waiting for transfers between devices: 26.1 us -> 13.5 us  [send(): lax.ppermute(x, ('blk', 'occ', 'sub'), [(number(*d), to(*d)) for d in eve...]
    ppermute x12 -> x14, starting transfers between devices: 18.5 us -> 26.3 us  [send(): lax.ppermute(x, ('blk', 'occ', 'sub'), [(number(*d), to(*d)) for d in eve...]
    pallas_call x2, Pallas kernels: 12.9 us -> 6.54 us  [combine(): pl.pallas_call(functools.partial(combine_kernel, sources, first, count, o...]
  transfers between devices with their start and end apart: 12 -> 14, of which waited for: 5 -> 6; matrix products, arithmetic and copies ran while one was open for 0% -> 0% of each run, Pallas kernels for 17% -> 14%
where the time goes in v3:
time: 60.5 us; the launch traced here: 60.3 us
  starting transfers between devices  26.3 us (43%)
  Pallas kernels  17.9 us (30%)
  waiting for transfers between devices  13.5 us (22%)
  local copies, waits for them, and re-layouts  2.58 us (4%)
    ppermute x14, starting transfers between devices, send(): lax.ppermute(x, ('blk', 'occ', 'sub'), [(number(*d), to(*d)) for d in eve...  26.3 us
    ppermute x14, waiting for transfers between devices, send(): lax.ppermute(x, ('blk', 'occ', 'sub'), [(number(*d), to(*d)) for d in eve...  13.5 us
    pallas_call x2, Pallas kernels, pack(): pl.pallas_call(functools.partial(pack_kernel, plan, opening), in_specs=[a...  11.4 us
    pallas_call x2, Pallas kernels, combine(): pl.pallas_call(functools.partial(combine_kernel, sources, first, count, o...  6.54 us
    unnamed x4, local copies, waits for them, and re-layouts  2.58 us
  transfers between devices with their start and end apart: 14, of which 6 were waited for; matrix products, arithmetic and copies ran while one was open for 0% of the time, Pallas kernels for 14%

profile of v3, /device:TPU:0, one launch (start us, length us, event | category | flops | bytes accessed | tf_op | source)
XLA Modules:
  0.0 60.3 jit_solution(1677676313844551737)
XLA Ops:
  0.0 6.9 %shard_map.28 = (bf16[688,128]{1,0:T(8,128)(2,1)}, bf16[1024,128]{1,0:T(8,128)(2,1)}, bf16[1584,128]{1,0:T(8,128)(2,1)}, bf16[64,25088]{1,0:T(8,128)(2,1)}, bf16[16,128]{1,0:T(8,128)(2,1)}) custom-call(bf16[64,25088]{1,0:T(8,128)(2,1)} %bitcast.2, bf16[16,128]{1,0:T(8,128)(2,1)} %bitcast.3), custom_call_target="tpu_custom_call" | custom-call | bytes 16777216 | tf_op jit(solution)/shard_map/pallas_call | solution.py:105
  6.9 3.1 %collective-permute-start.1 = (bf16[1584,128]{1,0:T(8,128)(2,1)}, bf16[1584,128]{1,0:T(8,128)(2,1)S(1)}, u32[]{:S(2)}, u32[]{:S(2)}) collective-permute-start(bf16[1584,128]{1,0:T(8,128)(2,1)} %get-tuple-element.29), channel_id=1, source_target_pairs={{0,4},{1,5},{2,7},{3,6},{4,0},{5,1},{6,3},{7,2},{8,12},{9,13},{10,... | collective-permute-start | bytes 1216520 | tf_op jit(solution)/shard_map/ppermute | solution.py:249
  10.0 0.9 %collective-permute-start.3 = (bf16[16,128]{1,0:T(8,128)(2,1)}, bf16[16,128]{1,0:T(8,128)(2,1)S(1)}, u32[]{:S(2)}, u32[]{:S(2)}) collective-permute-start(bf16[16,128]{1,0:T(8,128)(2,1)} %bitcast.4), channel_id=1, source_target_pairs={{0,2},{1,3},{2,0},{3,1},{4,6},{5,7},{6,4},{7,5},{8,10},{9,11},{10,... | collective-permute-start | bytes 12296 | tf_op jit(solution)/shard_map/ppermute | solution.py:249
  11.0 2.9 %collective-permute-done.3.rest_11_ = bf16[16,128]{1,0:T(8,128)(2,1)S(1)} collective-permute-done((bf16[16,128]{1,0:T(8,128)(2,1)}, bf16[16,128]{1,0:T(8,128)(2,1)S(1)}, u32[]{:S(2)}, u32[]{:S(2)}) %collective-permute-start.3) | collective-permute-done | bytes 4128 | tf_op jit(solution)/shard_map/ppermute | solution.py:249
  13.9 2.6 %collective-permute-start.4 = (bf16[688,128]{1,0:T(8,128)(2,1)}, bf16[688,128]{1,0:T(8,128)(2,1)S(1)}, u32[]{:S(2)}, u32[]{:S(2)}) collective-permute-start(bf16[688,128]{1,0:T(8,128)(2,1)} %get-tuple-element.31), channel_id=1, source_target_pairs={{0,8},{1,9},{2,14},{3,15},{4,12},{5,13},{6,10},{7,11},{8,0},{9,1},... | collective-permute-start | bytes 528392 | tf_op jit(solution)/shard_map/ppermute | solution.py:249
  16.4 0.0 collective-permute-start.7
  16.4 0.0 copy-start
  16.4 1.9 %copy-done = bf16[64,25088]{1,0:T(8,128)(2,1)S(1)} copy-done((bf16[64,25088]{1,0:T(8,128)(2,1)S(1)}, bf16[64,25088]{1,0:T(8,128)(2,1)}, u32[]{:S(2)}) %copy-start) | copy-done | bytes 3211288
  18.4 4.4 %shard_map.29 = (bf16[1568,128]{1,0:T(8,128)(2,1)S(1)}, bf16[1568,128]{1,0:T(8,128)(2,1)S(1)}, bf16[560,128]{1,0:T(8,128)(2,1)S(1)}, bf16[560,128]{1,0:T(8,128)(2,1)S(1)}, bf16[336,128]{1,0:T(8,128)(2,1)S(1)}) custom-call(bf16[64,25088]{1,0:T(8,128)(2,1)S(1)} %copy-done), custom_call_target="tpu_custom_call" | custom-call | bytes 16777216 | tf_op jit(solution)/shard_map/pallas_call | solution.py:105
  22.8 0.1 collective-permute-start
  22.9 0.5 collective-permute-done.1.rest_6_.rest_2_
  23.4 0.5 collective-permute-start.2
  23.9 0.0 collective-permute-done.4.rest_2_
  24.0 4.4 %collective-permute-start.5 = (bf16[560,128]{1,0:T(8,128)(2,1)S(1)}, bf16[560,128]{1,0:T(8,128)(2,1)S(1)}, u32[]{:S(2)}, u32[]{:S(2)}) collective-permute-start(bf16[560,128]{1,0:T(8,128)(2,1)S(1)} %get-tuple-element.33), channel_id=1, source_target_pairs={{0,8},{1,9},{2,14},{3,15},{4,12},{5,13},{6,10},{7,11},{8,0},{9,1},... | collective-permute-start | bytes 430088 | tf_op jit(solution)/shard_map/ppermute | solution.py:249
  28.3 1.8 %collective-permute-start.12 = (bf16[688,128]{1,0:T(8,128)(2,1)S(1)}, bf16[688,128]{1,0:T(8,128)(2,1)S(1)}, u32[]{:S(2)}, u32[]{:S(2)}) collective-permute-start(bf16[688,128]{1,0:T(8,128)(2,1)S(1)} %collective-permute-done.4.rest_2_), channel_id=1, source_target_pairs={{0,2},{1,3},{2,0},{3,1},{4,6},{5,7},{6,4},{7,5},{8,10},{9,11},{10,... | collective-permute-start | bytes 528392 | tf_op jit(solution)/shard_map/ppermute | solution.py:249
  30.1 0.0 collective-permute-done.7.rest_4_
  30.2 9.5 %collective-permute-start.13 = (bf16[1024,128]{1,0:T(8,128)(2,1)S(1)}, bf16[1024,128]{1,0:T(8,128)(2,1)S(1)}, u32[]{:S(2)}, u32[]{:S(2)}) collective-permute-start(bf16[1024,128]{1,0:T(8,128)(2,1)S(1)} %collective-permute-done.7.rest_4_), channel_id=1, source_target_pairs={{0,2},{1,3},{2,0},{3,1},{4,6},{5,7},{6,4},{7,5},{8,10},{9,11},{10,... | collective-permute-start | bytes 786440 | tf_op jit(solution)/shard_map/ppermute | solution.py:249
  39.7 1.9 %collective-permute-done.5.rest_8_.rest_4_ = bf16[560,128]{1,0:T(8,128)(2,1)S(1)} collective-permute-done((bf16[560,128]{1,0:T(8,128)(2,1)S(1)}, bf16[560,128]{1,0:T(8,128)(2,1)S(1)}, u32[]{:S(2)}, u32[]{:S(2)}) %collective-permute-start.5) | collective-permute-done | bytes 143392 | tf_op jit(solution)/shard_map/ppermute | solution.py:249
  41.6 1.5 %collective-permute-start.8 = (bf16[560,128]{1,0:T(8,128)(2,1)S(1)}, bf16[560,128]{1,0:T(8,128)(2,1)S(1)}, u32[]{:S(2)}, u32[]{:S(2)}) collective-permute-start(bf16[560,128]{1,0:T(8,128)(2,1)S(1)} %get-tuple-element.38), channel_id=1, source_target_pairs={{0,13},{1,12},{2,11},{3,10},{4,9},{5,8},{6,15},{7,14},{8,5},{9,4},... | collective-permute-start | bytes 430088 | tf_op jit(solution)/shard_map/ppermute | solution.py:249
  43.1 0.0 collective-permute-done.12.rest_3_
  43.1 0.4 collective-permute-start.6
  43.5 0.0 collective-permute-done.rest_1_
  43.5 1.5 %collective-permute-start.10 = (bf16[336,128]{1,0:T(8,128)(2,1)S(1)}, bf16[336,128]{1,0:T(8,128)(2,1)S(1)}, u32[]{:S(2)}, u32[]{:S(2)}) collective-permute-start(bf16[336,128]{1,0:T(8,128)(2,1)S(1)} %get-tuple-element.39), channel_id=1, source_target_pairs={{0,8},{1,9},{2,14},{3,15},{4,12},{5,13},{6,10},{7,11},{8,0},{9,1},... | collective-permute-start | bytes 258056 | tf_op jit(solution)/shard_map/ppermute | solution.py:249
  44.9 4.0 %collective-permute-done.8.rest_6_ = bf16[560,128]{1,0:T(8,128)(2,1)S(1)} collective-permute-done((bf16[560,128]{1,0:T(8,128)(2,1)S(1)}, bf16[560,128]{1,0:T(8,128)(2,1)S(1)}, u32[]{:S(2)}, u32[]{:S(2)}) %collective-permute-start.8) | collective-permute-done | bytes 143392 | tf_op jit(solution)/shard_map/ppermute | solution.py:249
  48.9 0.0 collective-permute-start.9
  48.9 3.6 %collective-permute-done.10.rest_8_ = bf16[336,128]{1,0:T(8,128)(2,1)S(1)} collective-permute-done((bf16[336,128]{1,0:T(8,128)(2,1)S(1)}, bf16[336,128]{1,0:T(8,128)(2,1)S(1)}, u32[]{:S(2)}, u32[]{:S(2)}) %collective-permute-start.10) | collective-permute-done | bytes 86048 | tf_op jit(solution)/shard_map/ppermute | solution.py:249
  52.5 0.0 collective-permute-start.11
  52.5 0.0 collective-permute-done.6.rest_9_.rest_5_
  52.5 0.0 collective-permute-done.13.rest_5_
  52.5 0.0 collective-permute-done.2.rest_7_.rest_3_
  52.5 0.0 copy-start.1
  52.5 0.7 %copy-done.1 = bf16[16,128]{1,0:T(8,128)(2,1)S(1)} copy-done((bf16[16,128]{1,0:T(8,128)(2,1)S(1)}, bf16[16,128]{1,0:T(8,128)(2,1)}, u32[]{:S(2)}) %copy-start.1) | copy-done | bytes 4120
  53.2 3.9 %shard_map.30 = (f32[128,25088]{1,0:T(8,128)}, bf16[256,128]{1,0:T(8,128)(2,1)S(1)}, bf16[128,64]{1,0:T(8,128)(2,1)S(1)}) custom-call(bf16[64,25088]{1,0:T(8,128)(2,1)S(1)} %copy-done, bf16[1568,128]{1,0:T(8,128)(2,1)S(1)} %get-tuple-element.27.rest_0_, bf16[1568,128]{1,0:T(8,128)(2,1)S(1)} %collective-permute-done.rest_1_, ...), custom_call_target="tpu_custom_call" | custom-call | flops 792723456 | bytes 12386304 | tf_op jit(solution)/shard_map/pallas_call | solution.py:209
  57.1 0.5 collective-permute-done.11.rest_9_
  57.7 0.0 collective-permute-done.9.rest_7_
  57.7 2.6 %shard_map.31 = f32[128,25088]{1,0:T(8,128)} custom-call(bf16[64,25088]{1,0:T(8,128)(2,1)S(1)} %copy-done, bf16[1568,128]{1,0:T(8,128)(2,1)S(1)} %get-tuple-element.27.rest_0_, bf16[1568,128]{1,0:T(8,128)(2,1)S(1)} %collective-permute-done.rest_1_, bf16[1584,128]{1,0:T(8,128)(2,1)S(1)} %collective-permute-done.1.rest_6_.rest_2_, ...), custom_call_target="tpu_custom_call", output_to_operand_aliasing={{}: (13, {})} | custom-call | flops 440401920 | bytes 6881280 | tf_op jit(solution)/shard_map/pallas_call | solution.py:209
Async XLA Ops:
  6.9 16.5 %collective-permute-start.1 = (bf16[1584,128]{1,0:T(8,128)(2,1)}, bf16[1584,128]{1,0:T(8,128)(2,1)S(1)}, u32[]{:S(2)}, u32[]{:S(2)}) collective-permute-start(bf16[1584,128]{1,0:T(8,128)(2,1)} %get-tuple-element.29), channel_id=1, source_target_pairs={{0,4},{1,5},{2,7},{3,6},{4,0},{5,1},{6,3},{7,2},{8,12},{9,13},{10,... | collective-permute-start | bytes 1216520 | tf_op jit(solution)/shard_map/ppermute | solution.py:249
  10.0 3.8 %collective-permute-start.3 = (bf16[16,128]{1,0:T(8,128)(2,1)}, bf16[16,128]{1,0:T(8,128)(2,1)S(1)}, u32[]{:S(2)}, u32[]{:S(2)}) collective-permute-start(bf16[16,128]{1,0:T(8,128)(2,1)} %bitcast.4), channel_id=1, source_target_pairs={{0,2},{1,3},{2,0},{3,1},{4,6},{5,7},{6,4},{7,5},{8,10},{9,11},{10,... | collective-permute-start | bytes 12296 | tf_op jit(solution)/shard_map/ppermute | solution.py:249
  13.9 10.1 %collective-permute-start.4 = (bf16[688,128]{1,0:T(8,128)(2,1)}, bf16[688,128]{1,0:T(8,128)(2,1)S(1)}, u32[]{:S(2)}, u32[]{:S(2)}) collective-permute-start(bf16[688,128]{1,0:T(8,128)(2,1)} %get-tuple-element.31), channel_id=1, source_target_pairs={{0,8},{1,9},{2,14},{3,15},{4,12},{5,13},{6,10},{7,11},{8,0},{9,1},... | collective-permute-start | bytes 528392 | tf_op jit(solution)/shard_map/ppermute | solution.py:249
  16.4 13.7 %collective-permute-start.7 = (bf16[1024,128]{1,0:T(8,128)(2,1)}, bf16[1024,128]{1,0:T(8,128)(2,1)S(1)}, u32[]{:S(2)}, u32[]{:S(2)}) collective-permute-start(bf16[1024,128]{1,0:T(8,128)(2,1)} %get-tuple-element.36), channel_id=1, source_target_pairs={{0,13},{1,12},{2,11},{3,10},{4,9},{5,8},{6,15},{7,14},{8,5},{9,4},... | collective-permute-start | bytes 786440 | tf_op jit(solution)/shard_map/ppermute | solution.py:249
  16.4 1.9 %copy-start = (bf16[64,25088]{1,0:T(8,128)(2,1)S(1)}, bf16[64,25088]{1,0:T(8,128)(2,1)}, u32[]{:S(2)}) copy-start(bf16[64,25088]{1,0:T(8,128)(2,1)} %get-tuple-element.26.vt) | copy-start | bytes 9633796
  22.8 20.7 %collective-permute-start = (bf16[1568,128]{1,0:T(8,128)(2,1)S(1)}, bf16[1568,128]{1,0:T(8,128)(2,1)S(1)}, u32[]{:S(2)}, u32[]{:S(2)}) collective-permute-start(bf16[1568,128]{1,0:T(8,128)(2,1)S(1)} %get-tuple-element.28), channel_id=1, source_target_pairs={{0,1},{1,0},{2,3},{3,2},{4,5},{5,4},{6,7},{7,6},{8,9},{9,8},{10,11... | collective-permute-start | bytes 1204232 | tf_op jit(solution)/shard_map/ppermute | solution.py:249
  23.4 29.1 %collective-permute-start.2 = (bf16[1584,128]{1,0:T(8,128)(2,1)S(1)}, bf16[1584,128]{1,0:T(8,128)(2,1)S(1)}, u32[]{:S(2)}, u32[]{:S(2)}) collective-permute-start(bf16[1584,128]{1,0:T(8,128)(2,1)S(1)} %collective-permute-done.1.rest_6_.rest_2_), channel_id=1, source_target_pairs={{0,2},{1,3},{2,0},{3,1},{4,6},{5,7},{6,4},{7,5},{8,10},{9,11},{10,... | collective-permute-start | bytes 1216520 | tf_op jit(solution)/shard_map/ppermute | solution.py:249
  24.0 17.6 %collective-permute-start.5 = (bf16[560,128]{1,0:T(8,128)(2,1)S(1)}, bf16[560,128]{1,0:T(8,128)(2,1)S(1)}, u32[]{:S(2)}, u32[]{:S(2)}) collective-permute-start(bf16[560,128]{1,0:T(8,128)(2,1)S(1)} %get-tuple-element.33), channel_id=1, source_target_pairs={{0,8},{1,9},{2,14},{3,15},{4,12},{5,13},{6,10},{7,11},{8,0},{9,1},... | collective-permute-start | bytes 430088 | tf_op jit(solution)/shard_map/ppermute | solution.py:249
  28.3 14.8 %collective-permute-start.12 = (bf16[688,128]{1,0:T(8,128)(2,1)S(1)}, bf16[688,128]{1,0:T(8,128)(2,1)S(1)}, u32[]{:S(2)}, u32[]{:S(2)}) collective-permute-start(bf16[688,128]{1,0:T(8,128)(2,1)S(1)} %collective-permute-done.4.rest_2_), channel_id=1, source_target_pairs={{0,2},{1,3},{2,0},{3,1},{4,6},{5,7},{6,4},{7,5},{8,10},{9,11},{10,... | collective-permute-start | bytes 528392 | tf_op jit(solution)/shard_map/ppermute | solution.py:249
  30.2 22.3 %collective-permute-start.13 = (bf16[1024,128]{1,0:T(8,128)(2,1)S(1)}, bf16[1024,128]{1,0:T(8,128)(2,1)S(1)}, u32[]{:S(2)}, u32[]{:S(2)}) collective-permute-start(bf16[1024,128]{1,0:T(8,128)(2,1)S(1)} %collective-permute-done.7.rest_4_), channel_id=1, source_target_pairs={{0,2},{1,3},{2,0},{3,1},{4,6},{5,7},{6,4},{7,5},{8,10},{9,11},{10,... | collective-permute-start | bytes 786440 | tf_op jit(solution)/shard_map/ppermute | solution.py:249
  41.6 7.4 %collective-permute-start.8 = (bf16[560,128]{1,0:T(8,128)(2,1)S(1)}, bf16[560,128]{1,0:T(8,128)(2,1)S(1)}, u32[]{:S(2)}, u32[]{:S(2)}) collective-permute-start(bf16[560,128]{1,0:T(8,128)(2,1)S(1)} %get-tuple-element.38), channel_id=1, source_target_pairs={{0,13},{1,12},{2,11},{3,10},{4,9},{5,8},{6,15},{7,14},{8,5},{9,4},... | collective-permute-start | bytes 430088 | tf_op jit(solution)/shard_map/ppermute | solution.py:249
  43.1 9.4 %collective-permute-start.6 = (bf16[560,128]{1,0:T(8,128)(2,1)S(1)}, bf16[560,128]{1,0:T(8,128)(2,1)S(1)}, u32[]{:S(2)}, u32[]{:S(2)}) collective-permute-start(bf16[560,128]{1,0:T(8,128)(2,1)S(1)} %collective-permute-done.5.rest_8_.rest_4_), channel_id=1, source_target_pairs={{0,2},{1,3},{2,0},{3,1},{4,6},{5,7},{6,4},{7,5},{8,10},{9,11},{10,... | collective-permute-start | bytes 430088 | tf_op jit(solution)/shard_map/ppermute | solution.py:249
  43.5 9.0 %collective-permute-start.10 = (bf16[336,128]{1,0:T(8,128)(2,1)S(1)}, bf16[336,128]{1,0:T(8,128)(2,1)S(1)}, u32[]{:S(2)}, u32[]{:S(2)}) collective-permute-start(bf16[336,128]{1,0:T(8,128)(2,1)S(1)} %get-tuple-element.39), channel_id=1, source_target_pairs={{0,8},{1,9},{2,14},{3,15},{4,12},{5,13},{6,10},{7,11},{8,0},{9,1},... | collective-permute-start | bytes 258056 | tf_op jit(solution)/shard_map/ppermute | solution.py:249
  48.9 8.8 %collective-permute-start.9 = (bf16[560,128]{1,0:T(8,128)(2,1)S(1)}, bf16[560,128]{1,0:T(8,128)(2,1)S(1)}, u32[]{:S(2)}, u32[]{:S(2)}) collective-permute-start(bf16[560,128]{1,0:T(8,128)(2,1)S(1)} %collective-permute-done.8.rest_6_), channel_id=1, source_target_pairs={{0,2},{1,3},{2,0},{3,1},{4,6},{5,7},{6,4},{7,5},{8,10},{9,11},{10,... | collective-permute-start | bytes 430088 | tf_op jit(solution)/shard_map/ppermute | solution.py:249
  52.5 5.2 %collective-permute-start.11 = (bf16[336,128]{1,0:T(8,128)(2,1)S(1)}, bf16[336,128]{1,0:T(8,128)(2,1)S(1)}, u32[]{:S(2)}, u32[]{:S(2)}) collective-permute-start(bf16[336,128]{1,0:T(8,128)(2,1)S(1)} %collective-permute-done.10.rest_8_), channel_id=1, source_target_pairs={{0,2},{1,3},{2,0},{3,1},{4,6},{5,7},{6,4},{7,5},{8,10},{9,11},{10,... | collective-permute-start | bytes 258056 | tf_op jit(solution)/shard_map/ppermute | solution.py:249
  52.5 0.7 %copy-start.1 = (bf16[16,128]{1,0:T(8,128)(2,1)S(1)}, bf16[16,128]{1,0:T(8,128)(2,1)}, u32[]{:S(2)}) copy-start(bf16[16,128]{1,0:T(8,128)(2,1)} %get-tuple-element.42.rest_10_) | copy-start | bytes 12292

commit v4 on v3

--- a/solution.py
+++ b/solution.py
@@ -22,12 +22,15 @@
     return 2 * (2 + jnp.bitwise_xor(plane, cross)) + cross
 
 
-def pack_kernel(plan, opening, vt, *rest):
-    if opening:
-        amplitudes, outs, (local, rider) = rest[0], rest[1 : 1 + len(plan)], rest[1 + len(plan) : 3 + len(plan)]
-        rows, in_sems, rider_sem = rest[3 + len(plan) :]
+def pack_kernel(plan, opening, vt, amplitudes, *rest):
+    if not opening:
+        across, *rest = rest
+    outs, rest = rest[: len(plan)], rest[len(plan) :]
+    if opening:
+        local, rider, rows, in_sems, rider_sem = rest
+        riders = [rider]
     else:
-        outs, rows, local = rest[: len(plan)], rest[len(plan)], vt
+        (rows,), local, riders = rest, vt, [amplitudes, across]
     kw = vt.shape[0]
     vl = rows.shape[0]
     half = vl // 2
@@ -72,7 +75,7 @@
 
     low = lax.broadcasted_iota(jnp.int32, (vl, LANES), 1) < kw
     for out, (kind, first, count, rides) in zip(outs, plan):
-        far = {"own": 0, "core": 1, "near": 2 + plane, "same": far_of(0, plane), "cross": far_of(1, plane)}[kind]
+        far = {"own": 0, "core": 1, "near": 2 + plane, "near_same": 2, "near_cross": 3, "same": far_of(0, plane), "cross": far_of(1, plane)}[kind]
         base = jnp.bitwise_xor(me, far) * vl
 
         def gather(i, carry, out=out, base=base, first=first):
@@ -85,13 +88,15 @@
             return carry
 
         lax.fori_loop(0, count, gather, 0)
-        if rides:
-            out[count * 2 * vl :, :] = rider[...]
-
-
-def pack(vt, plan, vl, amplitudes=None):
-    extra = 0 if amplitudes is None else amplitudes.shape[0]
-    opening = amplitudes is not None
+        for n in range(rides):
+            size = riders[n].shape[0]
+            begin = count * 2 * vl + n * size
+            out[begin : begin + size, :] = riders[n][...]
+
+
+def pack(vt, plan, vl, amplitudes, across=None):
+    extra = amplitudes.shape[0]
+    opening = across is None
     vmem = pl.BlockSpec(memory_space=pltpu.VMEM)
     anywhere = pl.BlockSpec(memory_space=pl.ANY)
     chunks = 4
@@ -104,13 +109,13 @@
         scratch += [pltpu.SemaphoreType.DMA((chunks,)), pltpu.SemaphoreType.DMA]
     return pl.pallas_call(
         functools.partial(pack_kernel, plan, opening),
-        in_specs=[anywhere, anywhere] if opening else [vmem],
+        in_specs=[anywhere] * 2 if opening else [vmem] * 3,
         out_specs=[vmem] * len(shapes),
         out_shape=shapes,
         scratch_shapes=scratch,
         compiler_params=pltpu.CompilerParams(vmem_limit_bytes=(HEAD_MB if opening else 20) * 2**20),
-        cost_estimate=pl.CostEstimate(flops=0, bytes_accessed=PACK_COST * 2**20, transcendentals=0),
-    )(vt, *([amplitudes] if opening else []))
+        cost_estimate=pl.CostEstimate(flops=0, bytes_accessed=PACK_COST * 2**10, transcendentals=0),
+    )(vt, amplitudes, *([] if opening else [across]))
 
 
 def combine_kernel(sources, first, count, opening, vt, *rest):
@@ -129,17 +134,21 @@
     me = 2 * z + core
 
     def far(kind, side):
-        return {"own": 0, "core": 1, "near": 2 + side, "same": far_of(0, side), "cross": far_of(1, side)}[kind]
+        return {"own": 0, "core": 1, "near": 2 + side, "near_same": 2, "near_cross": 3, "same": far_of(0, side), "cross": far_of(1, side)}[kind]
 
     if opening:
         size = own.shape[0]
         tall[plane, z] = own[...]
         tall[1 - plane, z] = across[...]
         for ref, (kind, mine, start, at, _) in zip(arrivals, sources):
-            if kind in ("near", "same", "cross") and start == 0 and at == 0:
+            if kind in ("near", "near_cross", "same", "cross") and start == 0 and at == 0:
                 side = plane if mine else 1 - plane
-                there = jnp.bitwise_xor(z, 1 if kind == "near" else far(kind, side) // 2)
-                tall[side, there] = ref[ref.shape[0] - size :, :]
+                there = jnp.bitwise_xor(z, 1 if kind.startswith("near") else far(kind, side) // 2)
+                if kind == "near_cross":
+                    tall[1 - side, there] = ref[ref.shape[0] - size :, :]
+                    tall[side, there] = ref[ref.shape[0] - 2 * size : ref.shape[0] - size, :]
+                else:
+                    tall[side, there] = ref[ref.shape[0] - size :, :]
         row = lax.broadcasted_iota(jnp.int32, (pairs, LANES), 0)
         col = lax.broadcasted_iota(jnp.int32, (pairs, LANES), 1)
         occ_i, occ_j = row // NOCC, row % NOCC
@@ -214,16 +223,16 @@
         scratch_shapes=scratch,
         input_output_aliases=aliases,
         compiler_params=pltpu.CompilerParams(vmem_limit_bytes=20 * 2**20),
-        cost_estimate=pl.CostEstimate(
-            flops=4 * count * pairs * 3 * kw * width, bytes_accessed=count * 2 * pairs * width * 6, transcendentals=0
-        ),
+        cost_estimate=pl.CostEstimate(flops=0, bytes_accessed=JOIN_COST * 2**10, transcendentals=0),
     )(vt, *arrivals, *extra)
 
 
-HEAD_MB = 54
-PACK_COST = 16
-FLOWS = (('same', 0, 6, None), ('cross', 0, 9, None), ('near', 0, 14, None), ('same', 6, 5, 0), ('cross', 9, 5, 1), ('same', 11, 3, 3))
-PIECES = ((0, 9), (9, 5))
+HEAD_MB = 48
+PACK_COST = 1
+JOIN_COST = 1
+FLOWS = (('same', 0, 6, 1), ('cross', 0, 9, 1), ('near', 0, 14, 1), ('same', 6, 5, 0), ('same', 11, 3, 0), ('cross', 9, 5, 0))
+PIECES = ((0, 6), (6, 3), (9, 5))
+AFTER = (('z3', ('z0',)), ('z5', ('z1',)), ('z4', ('x0',)), ('x0', ('across',)), ('x1', ('x0',)))
 
 
 def shards_fast(amplitudes, integrals):
@@ -243,46 +252,80 @@
                 return number(z, 1 - plane, s)
             if kind == "near":
                 return number(z ^ 1, plane, s ^ plane)
+            if kind in ("near_same", "near_cross"):
+                return number(z ^ 1, plane, s ^ (kind == "near_cross"))
             cross = kind == "cross"
             return number(z ^ (2 + (plane ^ cross)), plane, s ^ cross)
 
         return lax.ppermute(x, ("blk", "occ", "sub"), [(number(*d), to(*d)) for d in everyone])
 
-    def before(first, then):
-        return lax.optimization_barrier((first, then))
-
-    across = send(amplitudes.T, "plane")
-    heads = [f for f, flow in enumerate(FLOWS) if flow[3] is None]
-    tails = [f for f, flow in enumerate(FLOWS) if flow[3] is not None]
-    plan = [(*FLOWS[f][:3], FLOWS[f][1] == 0) for f in heads]
-    *packed, vt, own = pack(integrals.T, plan, vl, amplitudes.T)
-    messages = dict(zip(heads, packed))
-    across, messages[0] = before(across, messages[0])
-    plan = [("core", 0, steps, False), ("own", 0, steps, False)] + [(*FLOWS[f][:3], False) for f in tails]
-    core, mine, *packed = pack(vt, plan, vl)
-    messages.update(zip(tails, packed))
-    core = send(core, "core")
-    got = []
-    for f, (kind, _, _, after) in enumerate(FLOWS):
-        if after is not None:
-            got[after], messages[f] = before(got[after], messages[f])
-        got.append(send(messages[f], kind))
-    passed = [send(x, "plane") for x in got]
-    out = None
-    for n, (first, count) in enumerate(PIECES):
-        arrivals = [mine, core]
-        sources = [("own", True, first, 0, count), ("core", True, first, 0, count)]
-        for flow, (kind, start, size, _) in enumerate(FLOWS):
+    values, after = {}, dict(AFTER)
+
+    def hold(x, name):
+        for first in after.get(name, ()):
+            values[first], x = lax.optimization_barrier((result(first), x))
+        return x
+
+    def riders(f):
+        kind, first = FLOWS[f][:2]
+        return 0 if first or kind == "near_same" else 2 if kind == "near_cross" else 1
+
+    def sources_of(first, count):
+        names, sources = ["own", "core"], [("own", True, first, 0, count), ("core", True, first, 0, count)]
+        for f, (kind, start, size, _) in enumerate(FLOWS):
             low, high = max(first, start), min(first + count, start + size)
             if low < high:
-                arrivals += [got[flow], passed[flow]]
                 span = (low - start, low - first, high - low)
-                sources += [(kind, True, *span), (kind, False, *span)]
-        if n == 0:
-            out, lhs, direct = combine(vt, arrivals, sources, first, count, vl, pairs, opening=(own, across))
-        else:
-            out = combine(vt, arrivals, sources, first, count, vl, pairs, later=(lhs, direct, out))
-    return out
+                names.append(f"z{f}")
+                sources.append((kind, True, *span))
+                if kind in ("near", "same", "cross"):
+                    names.append(f"x{f}")
+                    sources.append((kind, False, *span))
+        return names, sources
+
+    def result(name):
+        if name not in values:
+            values[name] = make(name)
+        return values[name]
+
+    def make(name):
+        index = int(name[1:]) if name[1:].isdigit() else None
+        if name == "across":
+            return send(hold(amplitudes.T, name), "plane")
+        if name == "head":
+            plan = [(*flow[:3], riders(f)) for f, flow in enumerate(FLOWS) if flow[3]]
+            return pack(integrals.T, plan, vl, amplitudes.T)
+        if name == "tail":
+            plan = [("core", 0, steps, 0), ("own", 0, steps, 0)]
+            plan += [(*flow[:3], riders(f)) for f, flow in enumerate(FLOWS) if not flow[3]]
+            *_, vt, own = result("head")
+            return pack(vt, plan, vl, hold(own, name), result("across"))
+        if name == "tail_core":
+            return result("tail")[0]
+        if name == "own":
+            return result("tail")[1]
+        if name == "core":
+            return send(hold(result("tail")[0], name), "core")
+        if name[0] == "z":
+            kind, _, _, head = FLOWS[index]
+            place = sum(flow[3] == head for flow in FLOWS[:index])
+            message = result("head")[place] if head else result("tail")[2 + place]
+            return send(hold(message, name), kind)
+        if name[0] == "x":
+            return send(hold(result(f"z{index}"), name), "plane")
+        if name[0] == "l":
+            return result(f"k{index}")[1]
+        first, count = PIECES[index]
+        names, sources = sources_of(first, count)
+        *_, vt, own = result("head")
+        arrivals = [result(n) for n in names]
+        if index == 0:
+            return combine(vt, arrivals, sources, first, count, vl, pairs, opening=(own, result("across")))
+        out = result(f"k{index - 1}")
+        previous = out[0] if index == 1 else out
+        return combine(vt, arrivals, sources, first, count, vl, pairs, later=(result("l0"), result("k0")[2], previous))
+
+    return result(f"k{len(PIECES) - 1}")
 
 
 def shards_any(amplitudes, integrals):

time: 60.5 us -> 55.9 us (0.924)
  starting transfers between devices: 26.3 us -> 23.3 us
  local copies, waits for them, and re-layouts: 2.58 us -> 0.69 us
  waiting for transfers between devices: 13.5 us -> 14.6 us
  Pallas kernels: 17.9 us -> 17.2 us
    ppermute x14, starting transfers between devices: 26.3 us -> 23.3 us  [send(): lax.ppermute(x, ('blk', 'occ', 'sub'), [(number(*d), to(*d)) for d in eve...]
    pallas_call x2, Pallas kernels: 11.4 us -> 9.41 us  [pack(): pl.pallas_call(functools.partial(pack_kernel, plan, opening), in_specs=[a...]
    unnamed x4 -> x2, local copies, waits for them, and re-layouts: 2.58 us -> 0.69 us
    pallas_call x2 -> x3, Pallas kernels: 6.54 us -> 7.75 us  [combine(): pl.pallas_call(functools.partial(combine_kernel, sources, first, count, o...]
    ppermute x14, waiting for transfers between devices: 13.5 us -> 14.6 us  [send(): lax.ppermute(x, ('blk', 'occ', 'sub'), [(number(*d), to(*d)) for d in eve...]
  transfers between devices with their start and end apart: 14 -> 14, of which waited for: 6 -> 5; matrix products, arithmetic and copies ran while one was open for 0% -> 0% of each run, Pallas kernels for 14% -> 17%
where the time goes in v4:
time: 55.9 us; the launch traced here: 55.8 us
  starting transfers between devices  23.3 us (42%)
  Pallas kernels  17.2 us (31%)
  waiting for transfers between devices  14.6 us (26%)
  local copies, waits for them, and re-layouts  0.69 us (1%)
    ppermute x14, starting transfers between devices, send(): lax.ppermute(x, ('blk', 'occ', 'sub'), [(number(*d), to(*d)) for d in eve...  23.3 us
    ppermute x14, waiting for transfers between devices, send(): lax.ppermute(x, ('blk', 'occ', 'sub'), [(number(*d), to(*d)) for d in eve...  14.6 us
    pallas_call x2, Pallas kernels, pack(): pl.pallas_call(functools.partial(pack_kernel, plan, opening), in_specs=[a...  9.41 us
    pallas_call x3, Pallas kernels, combine(): pl.pallas_call(functools.partial(combine_kernel, sources, first, count, o...  7.75 us
  transfers between devices with their start and end apart: 14, of which 5 were waited for; matrix products, arithmetic and copies ran while one was open for 0% of the time, Pallas kernels for 17%

profile of v4, /device:TPU:0, one launch (start us, length us, event | category | flops | bytes accessed | tf_op | source)
XLA Modules:
  0.0 55.8 jit_solution(7038833657937383116)
XLA Ops:
  0.0 0.0 copy-start
  0.0 0.7 %copy-done = bf16[128,16]{0,1:T(8,128)(2,1)S(1)} copy-done((bf16[128,16]{0,1:T(8,128)(2,1)S(1)}, bf16[128,16]{0,1:T(8,128)(2,1)}, u32[]{:S(2)}) %copy-start) | copy-done | bytes 4120
  0.7 5.0 %shard_map.28 = (bf16[688,128]{1,0:T(8,128)(2,1)S(1)}, bf16[1024,128]{1,0:T(8,128)(2,1)S(1)}, bf16[1584,128]{1,0:T(8,128)(2,1)S(1)}, bf16[64,25088]{1,0:T(8,128)(2,1)S(1)}, bf16[16,128]{1,0:T(8,128)(2,1)S(1)}) custom-call(bf16[64,25088]{1,0:T(8,128)(2,1)} %bitcast.4, bf16[16,128]{1,0:T(8,128)(2,1)S(1)} %bitcast.2), custom_call_target="tpu_custom_call" | custom-call | bytes 1024 | tf_op jit(solution)/shard_map/pallas_call | solution.py:110
  5.7 3.1 %collective-permute-start.2 = (bf16[1584,128]{1,0:T(8,128)(2,1)S(1)}, bf16[1584,128]{1,0:T(8,128)(2,1)S(1)}, u32[]{:S(2)}, u32[]{:S(2)}) collective-permute-start(bf16[1584,128]{1,0:T(8,128)(2,1)S(1)} %get-tuple-element.32), channel_id=1, source_target_pairs={{0,4},{1,5},{2,7},{3,6},{4,0},{5,1},{6,3},{7,2},{8,12},{9,13},{10,... | collective-permute-start | bytes 1216520 | tf_op jit(solution)/shard_map/ppermute | solution.py:260
  8.8 2.6 %collective-permute-start.4 = (bf16[688,128]{1,0:T(8,128)(2,1)S(1)}, bf16[688,128]{1,0:T(8,128)(2,1)S(1)}, u32[]{:S(2)}, u32[]{:S(2)}) collective-permute-start(bf16[688,128]{1,0:T(8,128)(2,1)S(1)} %get-tuple-element.33), channel_id=1, source_target_pairs={{0,8},{1,9},{2,14},{3,15},{4,12},{5,13},{6,10},{7,11},{8,0},{9,1},... | collective-permute-start | bytes 528392 | tf_op jit(solution)/shard_map/ppermute | solution.py:260
  11.4 1.0 %collective-permute-start = (bf16[16,128]{1,0:T(8,128)(2,1)S(1)}, bf16[16,128]{1,0:T(8,128)(2,1)S(1)}, u32[]{:S(2)}, u32[]{:S(2)}) collective-permute-start(bf16[16,128]{1,0:T(8,128)(2,1)S(1)} %bitcast.3), channel_id=1, source_target_pairs={{0,2},{1,3},{2,0},{3,1},{4,6},{5,7},{6,4},{7,5},{8,10},{9,11},{10,... | collective-permute-start | bytes 12296 | tf_op jit(solution)/shard_map/ppermute | solution.py:260
  12.4 0.9 %collective-permute-start.10 = (bf16[1024,128]{1,0:T(8,128)(2,1)S(1)}, bf16[1024,128]{1,0:T(8,128)(2,1)S(1)}, u32[]{:S(2)}, u32[]{:S(2)}) collective-permute-start(bf16[1024,128]{1,0:T(8,128)(2,1)S(1)} %get-tuple-element.40), channel_id=1, source_target_pairs={{0,13},{1,12},{2,11},{3,10},{4,9},{5,8},{6,15},{7,14},{8,5},{9,4},... | collective-permute-start | bytes 786440 | tf_op jit(solution)/shard_map/ppermute | solution.py:260
  13.3 1.7 %collective-permute-done.rest_0_.rest_9_ = bf16[16,128]{1,0:T(8,128)(2,1)S(1)} collective-permute-done((bf16[16,128]{1,0:T(8,128)(2,1)S(1)}, bf16[16,128]{1,0:T(8,128)(2,1)S(1)}, u32[]{:S(2)}, u32[]{:S(2)}) %collective-permute-start) | collective-permute-done | bytes 4128 | tf_op jit(solution)/shard_map/ppermute | solution.py:260
  15.0 4.4 %shard_map.29 = (bf16[1568,128]{1,0:T(8,128)(2,1)S(1)}, bf16[1568,128]{1,0:T(8,128)(2,1)S(1)}, bf16[560,128]{1,0:T(8,128)(2,1)S(1)}, bf16[336,128]{1,0:T(8,128)(2,1)S(1)}, bf16[560,128]{1,0:T(8,128)(2,1)S(1)}) custom-call(bf16[64,25088]{1,0:T(8,128)(2,1)S(1)} %get-tuple-element.28.vt, bf16[16,128]{1,0:T(8,128)(2,1)S(1)} %get-tuple-element.29.amplitudes.rest_8_, ...), custom_call_target="tpu_custom_call" | custom-call | bytes 1024 | tf_op jit(solution)/shard_map/pallas_call | solution.py:110
  19.4 0.1 collective-permute-start.1
  19.5 2.9 %collective-permute-done.4.rest_2_ = bf16[688,128]{1,0:T(8,128)(2,1)S(1)} collective-permute-done((bf16[688,128]{1,0:T(8,128)(2,1)S(1)}, bf16[688,128]{1,0:T(8,128)(2,1)S(1)}, u32[]{:S(2)}, u32[]{:S(2)}) %collective-permute-start.4) | collective-permute-done | bytes 176160 | tf_op jit(solution)/shard_map/ppermute | solution.py:260
  22.4 4.0 %collective-permute-start.7 = (bf16[688,128]{1,0:T(8,128)(2,1)S(1)}, bf16[688,128]{1,0:T(8,128)(2,1)S(1)}, u32[]{:S(2)}, u32[]{:S(2)}) collective-permute-start(bf16[688,128]{1,0:T(8,128)(2,1)S(1)} %collective-permute-done.4.rest_2_), channel_id=1, source_target_pairs={{0,2},{1,3},{2,0},{3,1},{4,6},{5,7},{6,4},{7,5},{8,10},{9,11},{10,... | collective-permute-start | bytes 528392 | tf_op jit(solution)/shard_map/ppermute | solution.py:260
  26.4 0.0 collective-permute-done.2.rest_6_.rest_4_.rest_2_
  26.4 2.5 %collective-permute-start.3 = (bf16[1584,128]{1,0:T(8,128)(2,1)S(1)}, bf16[1584,128]{1,0:T(8,128)(2,1)S(1)}, u32[]{:S(2)}, u32[]{:S(2)}) collective-permute-start(bf16[1584,128]{1,0:T(8,128)(2,1)S(1)} %collective-permute-done.2.rest_6_.rest_4_.rest_2_), channel_id=1, source_target_pairs={{0,2},{1,3},{2,0},{3,1},{4,6},{5,7},{6,4},{7,5},{8,10},{9,11},{10,... | collective-permute-start | bytes 1216520 | tf_op jit(solution)/shard_map/ppermute | solution.py:260
  28.9 0.5 collective-permute-start.5
  29.4 0.0 collective-permute-done.10.rest_4_.rest_2_
  29.4 1.4 %collective-permute-start.11 = (bf16[560,128]{1,0:T(8,128)(2,1)S(1)}, bf16[560,128]{1,0:T(8,128)(2,1)S(1)}, u32[]{:S(2)}, u32[]{:S(2)}) collective-permute-start(bf16[560,128]{1,0:T(8,128)(2,1)S(1)} %get-tuple-element.42), channel_id=1, source_target_pairs={{0,13},{1,12},{2,11},{3,10},{4,9},{5,8},{6,15},{7,14},{8,5},{9,4},... | collective-permute-start | bytes 430088 | tf_op jit(solution)/shard_map/ppermute | solution.py:260
  30.7 0.9 %collective-permute-done.7.rest_3_ = bf16[688,128]{1,0:T(8,128)(2,1)S(1)} collective-permute-done((bf16[688,128]{1,0:T(8,128)(2,1)S(1)}, bf16[688,128]{1,0:T(8,128)(2,1)S(1)}, u32[]{:S(2)}, u32[]{:S(2)}) %collective-permute-start.7) | collective-permute-done | bytes 176160 | tf_op jit(solution)/shard_map/ppermute | solution.py:260
  31.6 1.8 %collective-permute-start.13 = (bf16[1024,128]{1,0:T(8,128)(2,1)S(1)}, bf16[1024,128]{1,0:T(8,128)(2,1)S(1)}, u32[]{:S(2)}, u32[]{:S(2)}) collective-permute-start(bf16[1024,128]{1,0:T(8,128)(2,1)S(1)} %collective-permute-done.10.rest_4_.rest_2_), channel_id=1, source_target_pairs={{0,2},{1,3},{2,0},{3,1},{4,6},{5,7},{6,4},{7,5},{8,10},{9,11},{10,... | collective-permute-start | bytes 786440 | tf_op jit(solution)/shard_map/ppermute | solution.py:260
  33.4 7.9 %collective-permute-done.5.rest_6_.rest_4_ = bf16[560,128]{1,0:T(8,128)(2,1)S(1)} collective-permute-done((bf16[560,128]{1,0:T(8,128)(2,1)S(1)}, bf16[560,128]{1,0:T(8,128)(2,1)S(1)}, u32[]{:S(2)}, u32[]{:S(2)}) %collective-permute-start.5) | collective-permute-done | bytes 143392 | tf_op jit(solution)/shard_map/ppermute | solution.py:260
  41.3 0.0 collective-permute-start.8
  41.3 0.0 collective-permute-done.1.rest_1_
  41.3 0.0 collective-permute-start.6
  41.3 0.0 collective-permute-done.11.rest_8_
  41.3 5.4 %collective-permute-start.12 = (bf16[560,128]{1,0:T(8,128)(2,1)S(1)}, bf16[560,128]{1,0:T(8,128)(2,1)S(1)}, u32[]{:S(2)}, u32[]{:S(2)}) collective-permute-start(bf16[560,128]{1,0:T(8,128)(2,1)S(1)} %collective-permute-done.11.rest_8_), channel_id=1, source_target_pairs={{0,2},{1,3},{2,0},{3,1},{4,6},{5,7},{6,4},{7,5},{8,10},{9,11},{10,... | collective-permute-start | bytes 430088 | tf_op jit(solution)/shard_map/ppermute | solution.py:260
  46.8 1.2 %collective-permute-done.8.rest_6_ = bf16[336,128]{1,0:T(8,128)(2,1)S(1)} collective-permute-done((bf16[336,128]{1,0:T(8,128)(2,1)S(1)}, bf16[336,128]{1,0:T(8,128)(2,1)S(1)}, u32[]{:S(2)}, u32[]{:S(2)}) %collective-permute-start.8) | collective-permute-done | bytes 86048 | tf_op jit(solution)/shard_map/ppermute | solution.py:260
  48.0 0.0 collective-permute-start.9
  48.0 0.0 collective-permute-done.13.rest_5_.rest_3_
  48.0 0.0 collective-permute-done.3.rest_7_.rest_5_.rest_3_
  48.0 3.1 %shard_map.30 = (f32[128,25088]{1,0:T(8,128)}, bf16[256,128]{1,0:T(8,128)(2,1)S(1)}, bf16[128,64]{1,0:T(8,128)(2,1)S(1)}) custom-call(bf16[64,25088]{1,0:T(8,128)(2,1)S(1)} %get-tuple-element.28.vt, bf16[1568,128]{1,0:T(8,128)(2,1)S(1)} %get-tuple-element.30.rest_0_, bf16[1568,128]{1,0:T(8,128)(2,1)S(1)} %collective-permute-done.1.rest_1_, ...), custom_call_target="tpu_custom_call" | custom-call | bytes 1024 | tf_op jit(solution)/shard_map/pallas_call | solution.py:218
  51.1 0.0 collective-permute-done.6.rest_7_.rest_5_
  51.1 2.0 %shard_map.31.rest_12_ = f32[128,25088]{1,0:T(8,128)} custom-call(bf16[64,25088]{1,0:T(8,128)(2,1)S(1)} %get-tuple-element.28.vt, bf16[1568,128]{1,0:T(8,128)(2,1)S(1)} %get-tuple-element.30.rest_0_, bf16[1568,128]{1,0:T(8,128)(2,1)S(1)} %collective-permute-done.1.rest_1_, ...), custom_call_target="tpu_custom_call", output_to_operand_aliasing={{}: (11, {})} | custom-call | bytes 1024 | tf_op jit(solution)/shard_map/pallas_call | solution.py:218
  53.1 0.0 collective-permute-done.9.rest_7_
  53.1 0.0 collective-permute-done.12.rest_9_
  53.2 2.6 %shard_map.32 = f32[128,25088]{1,0:T(8,128)} custom-call(bf16[64,25088]{1,0:T(8,128)(2,1)S(1)} %get-tuple-element.28.vt, bf16[1568,128]{1,0:T(8,128)(2,1)S(1)} %get-tuple-element.30.rest_0_, bf16[1568,128]{1,0:T(8,128)(2,1)S(1)} %collective-permute-done.1.rest_1_, ...), custom_call_target="tpu_custom_call", output_to_operand_aliasing={{}: (13, {})} | custom-call | bytes 1024 | tf_op jit(solution)/shard_map/pallas_call | solution.py:218
Async XLA Ops:
  0.0 0.7 %copy-start = (bf16[128,16]{0,1:T(8,128)(2,1)S(1)}, bf16[128,16]{0,1:T(8,128)(2,1)}, u32[]{:S(2)}) copy-start(bf16[128,16]{0,1:T(8,128)(2,1)} %param.2) | copy-start | bytes 12292
  5.7 20.7 %collective-permute-start.2 = (bf16[1584,128]{1,0:T(8,128)(2,1)S(1)}, bf16[1584,128]{1,0:T(8,128)(2,1)S(1)}, u32[]{:S(2)}, u32[]{:S(2)}) collective-permute-start(bf16[1584,128]{1,0:T(8,128)(2,1)S(1)} %get-tuple-element.32), channel_id=1, source_target_pairs={{0,4},{1,5},{2,7},{3,6},{4,0},{5,1},{6,3},{7,2},{8,12},{9,13},{10,... | collective-permute-start | bytes 1216520 | tf_op jit(solution)/shard_map/ppermute | solution.py:260
  8.8 13.6 %collective-permute-start.4 = (bf16[688,128]{1,0:T(8,128)(2,1)S(1)}, bf16[688,128]{1,0:T(8,128)(2,1)S(1)}, u32[]{:S(2)}, u32[]{:S(2)}) collective-permute-start(bf16[688,128]{1,0:T(8,128)(2,1)S(1)} %get-tuple-element.33), channel_id=1, source_target_pairs={{0,8},{1,9},{2,14},{3,15},{4,12},{5,13},{6,10},{7,11},{8,0},{9,1},... | collective-permute-start | bytes 528392 | tf_op jit(solution)/shard_map/ppermute | solution.py:260
  11.4 3.6 %collective-permute-start = (bf16[16,128]{1,0:T(8,128)(2,1)S(1)}, bf16[16,128]{1,0:T(8,128)(2,1)S(1)}, u32[]{:S(2)}, u32[]{:S(2)}) collective-permute-start(bf16[16,128]{1,0:T(8,128)(2,1)S(1)} %bitcast.3), channel_id=1, source_target_pairs={{0,2},{1,3},{2,0},{3,1},{4,6},{5,7},{6,4},{7,5},{8,10},{9,11},{10,... | collective-permute-start | bytes 12296 | tf_op jit(solution)/shard_map/ppermute | solution.py:260
  12.4 17.0 %collective-permute-start.10 = (bf16[1024,128]{1,0:T(8,128)(2,1)S(1)}, bf16[1024,128]{1,0:T(8,128)(2,1)S(1)}, u32[]{:S(2)}, u32[]{:S(2)}) collective-permute-start(bf16[1024,128]{1,0:T(8,128)(2,1)S(1)} %get-tuple-element.40), channel_id=1, source_target_pairs={{0,13},{1,12},{2,11},{3,10},{4,9},{5,8},{6,15},{7,14},{8,5},{9,4},... | collective-permute-start | bytes 786440 | tf_op jit(solution)/shard_map/ppermute | solution.py:260
  19.4 21.9 %collective-permute-start.1 = (bf16[1568,128]{1,0:T(8,128)(2,1)S(1)}, bf16[1568,128]{1,0:T(8,128)(2,1)S(1)}, u32[]{:S(2)}, u32[]{:S(2)}) collective-permute-start(bf16[1568,128]{1,0:T(8,128)(2,1)S(1)} %get-tuple-element.31), channel_id=1, source_target_pairs={{0,1},{1,0},{2,3},{3,2},{4,5},{5,4},{6,7},{7,6},{8,9},{9,8},{10,11... | collective-permute-start | bytes 1204232 | tf_op jit(solution)/shard_map/ppermute | solution.py:260
  22.4 9.2 %collective-permute-start.7 = (bf16[688,128]{1,0:T(8,128)(2,1)S(1)}, bf16[688,128]{1,0:T(8,128)(2,1)S(1)}, u32[]{:S(2)}, u32[]{:S(2)}) collective-permute-start(bf16[688,128]{1,0:T(8,128)(2,1)S(1)} %collective-permute-done.4.rest_2_), channel_id=1, source_target_pairs={{0,2},{1,3},{2,0},{3,1},{4,6},{5,7},{6,4},{7,5},{8,10},{9,11},{10,... | collective-permute-start | bytes 528392 | tf_op jit(solution)/shard_map/ppermute | solution.py:260
  26.4 21.6 %collective-permute-start.3 = (bf16[1584,128]{1,0:T(8,128)(2,1)S(1)}, bf16[1584,128]{1,0:T(8,128)(2,1)S(1)}, u32[]{:S(2)}, u32[]{:S(2)}) collective-permute-start(bf16[1584,128]{1,0:T(8,128)(2,1)S(1)} %collective-permute-done.2.rest_6_.rest_4_.rest_2_), channel_id=1, source_target_pairs={{0,2},{1,3},{2,0},{3,1},{4,6},{5,7},{6,4},{7,5},{8,10},{9,11},{10,... | collective-permute-start | bytes 1216520 | tf_op jit(solution)/shard_map/ppermute | solution.py:260
  28.9 12.4 %collective-permute-start.5 = (bf16[560,128]{1,0:T(8,128)(2,1)S(1)}, bf16[560,128]{1,0:T(8,128)(2,1)S(1)}, u32[]{:S(2)}, u32[]{:S(2)}) collective-permute-start(bf16[560,128]{1,0:T(8,128)(2,1)S(1)} %get-tuple-element.35), channel_id=1, source_target_pairs={{0,8},{1,9},{2,14},{3,15},{4,12},{5,13},{6,10},{7,11},{8,0},{9,1},... | collective-permute-start | bytes 430088 | tf_op jit(solution)/shard_map/ppermute | solution.py:260
  29.4 11.9 %collective-permute-start.11 = (bf16[560,128]{1,0:T(8,128)(2,1)S(1)}, bf16[560,128]{1,0:T(8,128)(2,1)S(1)}, u32[]{:S(2)}, u32[]{:S(2)}) collective-permute-start(bf16[560,128]{1,0:T(8,128)(2,1)S(1)} %get-tuple-element.42), channel_id=1, source_target_pairs={{0,13},{1,12},{2,11},{3,10},{4,9},{5,8},{6,15},{7,14},{8,5},{9,4},... | collective-permute-start | bytes 430088 | tf_op jit(solution)/shard_map/ppermute | solution.py:260
  31.6 16.4 %collective-permute-start.13 = (bf16[1024,128]{1,0:T(8,128)(2,1)S(1)}, bf16[1024,128]{1,0:T(8,128)(2,1)S(1)}, u32[]{:S(2)}, u32[]{:S(2)}) collective-permute-start(bf16[1024,128]{1,0:T(8,128)(2,1)S(1)} %collective-permute-done.10.rest_4_.rest_2_), channel_id=1, source_target_pairs={{0,2},{1,3},{2,0},{3,1},{4,6},{5,7},{6,4},{7,5},{8,10},{9,11},{10,... | collective-permute-start | bytes 786440 | tf_op jit(solution)/shard_map/ppermute | solution.py:260
  41.3 6.7 %collective-permute-start.8 = (bf16[336,128]{1,0:T(8,128)(2,1)S(1)}, bf16[336,128]{1,0:T(8,128)(2,1)S(1)}, u32[]{:S(2)}, u32[]{:S(2)}) collective-permute-start(bf16[336,128]{1,0:T(8,128)(2,1)S(1)} %get-tuple-element.39), channel_id=1, source_target_pairs={{0,8},{1,9},{2,14},{3,15},{4,12},{5,13},{6,10},{7,11},{8,0},{9,1},... | collective-permute-start | bytes 258056 | tf_op jit(solution)/shard_map/ppermute | solution.py:260
  41.3 9.8 %collective-permute-start.6 = (bf16[560,128]{1,0:T(8,128)(2,1)S(1)}, bf16[560,128]{1,0:T(8,128)(2,1)S(1)}, u32[]{:S(2)}, u32[]{:S(2)}) collective-permute-start(bf16[560,128]{1,0:T(8,128)(2,1)S(1)} %collective-permute-done.5.rest_6_.rest_4_), channel_id=1, source_target_pairs={{0,2},{1,3},{2,0},{3,1},{4,6},{5,7},{6,4},{7,5},{8,10},{9,11},{10,... | collective-permute-start | bytes 430088 | tf_op jit(solution)/shard_map/ppermute | solution.py:260
  41.3 11.8 %collective-permute-start.12 = (bf16[560,128]{1,0:T(8,128)(2,1)S(1)}, bf16[560,128]{1,0:T(8,128)(2,1)S(1)}, u32[]{:S(2)}, u32[]{:S(2)}) collective-permute-start(bf16[560,128]{1,0:T(8,128)(2,1)S(1)} %collective-permute-done.11.rest_8_), channel_id=1, source_target_pairs={{0,2},{1,3},{2,0},{3,1},{4,6},{5,7},{6,4},{7,5},{8,10},{9,11},{10,... | collective-permute-start | bytes 430088 | tf_op jit(solution)/shard_map/ppermute | solution.py:260
  48.0 5.2 %collective-permute-start.9 = (bf16[336,128]{1,0:T(8,128)(2,1)S(1)}, bf16[336,128]{1,0:T(8,128)(2,1)S(1)}, u32[]{:S(2)}, u32[]{:S(2)}) collective-permute-start(bf16[336,128]{1,0:T(8,128)(2,1)S(1)} %collective-permute-done.8.rest_6_), channel_id=1, source_target_pairs={{0,2},{1,3},{2,0},{3,1},{4,6},{5,7},{6,4},{7,5},{8,10},{9,11},{10,... | collective-permute-start | bytes 258056 | tf_op jit(solution)/shard_map/ppermute | solution.py:260

commit v5 on v3

--- a/solution.py
+++ b/solution.py
@@ -13,21 +13,40 @@
 NT = (((1,), (1,)), ((), ()))
 NN = (((1,), (0,)), ((), ()))
 
+MESSAGES = (
+    ("same", 0, 6, True),
+    ("cross", 0, 10, True),
+    ("near", 0, 14, True),
+    ("same", 6, 5, False),
+    ("same", 11, 3, False),
+    ("cross", 10, 4, False),
+)
+PIECES = ((0, 6), (6, 4), (10, 4))
+AFTER = {"z3": ("z0",), "z5": ("z1",), "z4": ("x0",), "x1": ("x0",), "tail": ("across",)}
+
 
 def position():
     return lax.axis_index("blk"), lax.axis_index("sub"), lax.axis_index("occ")
 
 
-def far_of(cross, plane):
+def far_of(kind, plane):
+    if kind == "own":
+        return 0
+    if kind == "core":
+        return 1
+    if kind == "near":
+        return 2 + plane
+    cross = int(kind == "cross")
     return 2 * (2 + jnp.bitwise_xor(plane, cross)) + cross
 
 
 def pack_kernel(plan, opening, vt, *rest):
-    if opening:
-        amplitudes, outs, (local, rider) = rest[0], rest[1 : 1 + len(plan)], rest[1 + len(plan) : 3 + len(plan)]
-        rows, in_sems, rider_sem = rest[3 + len(plan) :]
+    amplitudes, rest = (rest[0], rest[1:]) if opening else (None, rest)
+    outs, rest = rest[: len(plan)], rest[len(plan) :]
+    if opening:
+        local, rider, rows, in_sems, rider_sem = rest
     else:
-        outs, rows, local = rest[: len(plan)], rest[len(plan)], vt
+        (rows,), local = rest, vt
     kw = vt.shape[0]
     vl = rows.shape[0]
     half = vl // 2
@@ -72,7 +91,7 @@
 
     low = lax.broadcasted_iota(jnp.int32, (vl, LANES), 1) < kw
     for out, (kind, first, count, rides) in zip(outs, plan):
-        far = {"own": 0, "core": 1, "near": 2 + plane, "same": far_of(0, plane), "cross": far_of(1, plane)}[kind]
+        far = far_of(kind, plane)
         base = jnp.bitwise_xor(me, far) * vl
 
         def gather(i, carry, out=out, base=base, first=first):
@@ -90,11 +109,11 @@
 
 
 def pack(vt, plan, vl, amplitudes=None):
-    extra = 0 if amplitudes is None else amplitudes.shape[0]
     opening = amplitudes is not None
+    extra = amplitudes.shape[0] if opening else 0
     vmem = pl.BlockSpec(memory_space=pltpu.VMEM)
-    anywhere = pl.BlockSpec(memory_space=pl.ANY)
-    chunks = 4
+    hbm = pl.BlockSpec(memory_space=pltpu.HBM)
+    chunks = 7
     shapes = [
         jax.ShapeDtypeStruct((count * 2 * vl + extra * rides, LANES), jnp.bfloat16) for _, _, count, rides in plan
     ]
@@ -104,12 +123,12 @@
         scratch += [pltpu.SemaphoreType.DMA((chunks,)), pltpu.SemaphoreType.DMA]
     return pl.pallas_call(
         functools.partial(pack_kernel, plan, opening),
-        in_specs=[anywhere, anywhere] if opening else [vmem],
+        in_specs=[hbm] * 2 if opening else [vmem],
         out_specs=[vmem] * len(shapes),
         out_shape=shapes,
         scratch_shapes=scratch,
-        compiler_params=pltpu.CompilerParams(vmem_limit_bytes=(HEAD_MB if opening else 20) * 2**20),
-        cost_estimate=pl.CostEstimate(flops=0, bytes_accessed=PACK_COST * 2**20, transcendentals=0),
+        compiler_params=pltpu.CompilerParams(vmem_limit_bytes=(48 if opening else 20) * 2**20),
+        cost_estimate=pl.CostEstimate(flops=0, bytes_accessed=1024, transcendentals=0),
     )(vt, *([amplitudes] if opening else []))
 
 
@@ -128,9 +147,6 @@
     z, core, plane = position()
     me = 2 * z + core
 
-    def far(kind, side):
-        return {"own": 0, "core": 1, "near": 2 + side, "same": far_of(0, side), "cross": far_of(1, side)}[kind]
-
     if opening:
         size = own.shape[0]
         tall[plane, z] = own[...]
@@ -138,8 +154,7 @@
         for ref, (kind, mine, start, at, _) in zip(arrivals, sources):
             if kind in ("near", "same", "cross") and start == 0 and at == 0:
                 side = plane if mine else 1 - plane
-                there = jnp.bitwise_xor(z, 1 if kind == "near" else far(kind, side) // 2)
-                tall[side, there] = ref[ref.shape[0] - size :, :]
+                tall[side, jnp.bitwise_xor(z, far_of(kind, side) // 2)] = ref[ref.shape[0] - size :, :]
         row = lax.broadcasted_iota(jnp.int32, (pairs, LANES), 0)
         col = lax.broadcasted_iota(jnp.int32, (pairs, LANES), 1)
         occ_i, occ_j = row // NOCC, row % NOCC
@@ -168,7 +183,7 @@
         buffer = turned.at[m % turned.shape[0]]
         for ref, (kind, mine, start, at, size) in zip(arrivals, sources):
             if at <= m < at + size:
-                q = jnp.bitwise_xor(me, far(kind, plane if mine else 1 - plane))
+                q = jnp.bitwise_xor(me, far_of(kind, plane if mine else 1 - plane))
                 block = ref[(start + m - at) * 2 * vl : (start + m - at + 1) * 2 * vl, :].astype(jnp.float32)
                 buffer[q] = block[:vl]
                 buffer[q + n_dev] = block[vl:]
@@ -214,16 +229,8 @@
         scratch_shapes=scratch,
         input_output_aliases=aliases,
         compiler_params=pltpu.CompilerParams(vmem_limit_bytes=20 * 2**20),
-        cost_estimate=pl.CostEstimate(
-            flops=4 * count * pairs * 3 * kw * width, bytes_accessed=count * 2 * pairs * width * 6, transcendentals=0
-        ),
+        cost_estimate=pl.CostEstimate(flops=0, bytes_accessed=1024, transcendentals=0),
     )(vt, *arrivals, *extra)
-
-
-HEAD_MB = 54
-PACK_COST = 16
-FLOWS = (('same', 0, 6, None), ('cross', 0, 9, None), ('near', 0, 14, None), ('same', 6, 5, 0), ('cross', 9, 5, 1), ('same', 11, 3, 3))
-PIECES = ((0, 9), (9, 5))
 
 
 def shards_fast(amplitudes, integrals):
@@ -248,40 +255,52 @@
 
         return lax.ppermute(x, ("blk", "occ", "sub"), [(number(*d), to(*d)) for d in everyone])
 
-    def before(first, then):
-        return lax.optimization_barrier((first, then))
-
-    across = send(amplitudes.T, "plane")
-    heads = [f for f, flow in enumerate(FLOWS) if flow[3] is None]
-    tails = [f for f, flow in enumerate(FLOWS) if flow[3] is not None]
-    plan = [(*FLOWS[f][:3], FLOWS[f][1] == 0) for f in heads]
-    *packed, vt, own = pack(integrals.T, plan, vl, amplitudes.T)
-    messages = dict(zip(heads, packed))
-    across, messages[0] = before(across, messages[0])
-    plan = [("core", 0, steps, False), ("own", 0, steps, False)] + [(*FLOWS[f][:3], False) for f in tails]
-    core, mine, *packed = pack(vt, plan, vl)
-    messages.update(zip(tails, packed))
-    core = send(core, "core")
-    got = []
-    for f, (kind, _, _, after) in enumerate(FLOWS):
-        if after is not None:
-            got[after], messages[f] = before(got[after], messages[f])
-        got.append(send(messages[f], kind))
-    passed = [send(x, "plane") for x in got]
-    out = None
-    for n, (first, count) in enumerate(PIECES):
-        arrivals = [mine, core]
-        sources = [("own", True, first, 0, count), ("core", True, first, 0, count)]
-        for flow, (kind, start, size, _) in enumerate(FLOWS):
+    values = {}
+
+    def result(name):
+        if name not in values:
+            values[name] = make(name)
+        return values[name]
+
+    def hold(x, name):
+        for first in AFTER.get(name, ()):
+            values[first], x = lax.optimization_barrier((result(first), x))
+        return x
+
+    def make(name):
+        if name == "head":
+            plan = [(kind, first, count, first == 0) for kind, first, count, opening in MESSAGES if opening]
+            return pack(integrals.T, plan, vl, amplitudes.T)
+        if name == "across":
+            return send(hold(result("head")[-1], name), "plane")
+        if name == "tail":
+            plan = [("core", 0, steps, False), ("own", 0, steps, False)]
+            plan += [(kind, first, count, False) for kind, first, count, opening in MESSAGES if not opening]
+            return pack(hold(result("head")[-2], name), plan, vl)
+        if name == "core":
+            return send(hold(result("tail")[0], name), "core")
+        if name == "own":
+            return result("tail")[1]
+        index = int(name[1:])
+        if name[0] == "x":
+            return send(hold(result(f"z{index}"), name), "plane")
+        kind, _, _, opening = MESSAGES[index]
+        place = sum(message[3] == opening for message in MESSAGES[:index])
+        return send(hold(result("head")[place] if opening else result("tail")[2 + place], name), kind)
+
+    pieces = []
+    for first, count in reversed(PIECES):
+        names, sources = ["own", "core"], [("own", True, first, 0, count), ("core", True, first, 0, count)]
+        for n, (kind, start, size, _) in enumerate(MESSAGES):
             low, high = max(first, start), min(first + count, start + size)
             if low < high:
-                arrivals += [got[flow], passed[flow]]
-                span = (low - start, low - first, high - low)
-                sources += [(kind, True, *span), (kind, False, *span)]
-        if n == 0:
-            out, lhs, direct = combine(vt, arrivals, sources, first, count, vl, pairs, opening=(own, across))
-        else:
-            out = combine(vt, arrivals, sources, first, count, vl, pairs, later=(lhs, direct, out))
+                names += [f"z{n}", f"x{n}"]
+                sources += [(kind, mine, low - start, low - first, high - low) for mine in (True, False)]
+        pieces.append(([result(name) for name in names], sources, first, count))
+    vt, own = result("head")[-2:]
+    out, lhs, direct = combine(vt, *pieces.pop(), vl, pairs, opening=(own, result("across")))
+    while pieces:
+        out = combine(vt, *pieces.pop(), vl, pairs, later=(lhs, direct, out))
     return out
 
 

time: 60.5 us -> 55.7 us (0.921)
  waiting for transfers between devices: 13.5 us -> 10.1 us
  local copies, waits for them, and re-layouts: 2.58 us -> 0.69 us
  starting transfers between devices: 26.3 us -> 27.4 us
    ppermute x14, waiting for transfers between devices: 13.5 us -> 10.1 us  [send(): lax.ppermute(x, ('blk', 'occ', 'sub'), [(number(*d), to(*d)) for d in eve...]
    pallas_call x2, Pallas kernels: 11.4 us -> 9.45 us  [pack(): pl.pallas_call(functools.partial(pack_kernel, plan, opening), in_specs=[h...]
    unnamed x4 -> x2, local copies, waits for them, and re-layouts: 2.58 us -> 0.69 us
    pallas_call x2 -> x3, Pallas kernels: 6.54 us -> 7.81 us  [combine(): pl.pallas_call(functools.partial(combine_kernel, sources, first, count, o...]
    ppermute x14, starting transfers between devices: 26.3 us -> 27.4 us  [send(): lax.ppermute(x, ('blk', 'occ', 'sub'), [(number(*d), to(*d)) for d in eve...]
  transfers between devices with their start and end apart: 14 -> 14, of which waited for: 6 -> 6; matrix products, arithmetic and copies ran while one was open for 0% -> 0% of each run, Pallas kernels for 14% -> 18%
where the time goes in v5:
time: 55.7 us; the launch traced here: 55.6 us
  starting transfers between devices  27.4 us (49%)
  Pallas kernels  17.3 us (31%)
  waiting for transfers between devices  10.1 us (18%)
  local copies, waits for them, and re-layouts  0.69 us (1%)
    ppermute x14, starting transfers between devices, send(): lax.ppermute(x, ('blk', 'occ', 'sub'), [(number(*d), to(*d)) for d in eve...  27.4 us
    ppermute x14, waiting for transfers between devices, send(): lax.ppermute(x, ('blk', 'occ', 'sub'), [(number(*d), to(*d)) for d in eve...  10.1 us
    pallas_call x2, Pallas kernels, pack(): pl.pallas_call(functools.partial(pack_kernel, plan, opening), in_specs=[h...  9.45 us
    pallas_call x3, Pallas kernels, combine(): pl.pallas_call(functools.partial(combine_kernel, sources, first, count, o...  7.81 us
  transfers between devices with their start and end apart: 14, of which 6 were waited for; matrix products, arithmetic and copies ran while one was open for 0% of the time, Pallas kernels for 18%

profile of v5, /device:TPU:0, one launch (start us, length us, event | category | flops | bytes accessed | tf_op | source)
XLA Modules:
  0.0 55.6 jit_solution(10649710620541715671)
XLA Ops:
  0.0 0.0 copy-start
  0.0 0.7 %copy-done = bf16[128,16]{0,1:T(8,128)(2,1)S(1)} copy-done((bf16[128,16]{0,1:T(8,128)(2,1)S(1)}, bf16[128,16]{0,1:T(8,128)(2,1)}, u32[]{:S(2)}) %copy-start) | copy-done | bytes 4120
  0.7 5.1 %shard_map.28 = (bf16[688,128]{1,0:T(8,128)(2,1)S(1)}, bf16[1136,128]{1,0:T(8,128)(2,1)S(1)}, bf16[1584,128]{1,0:T(8,128)(2,1)S(1)}, bf16[64,25088]{1,0:T(8,128)(2,1)S(1)}, bf16[16,128]{1,0:T(8,128)(2,1)S(1)}) custom-call(bf16[64,25088]{1,0:T(8,128)(2,1)} %bitcast.3, bf16[16,128]{1,0:T(8,128)(2,1)S(1)} %bitcast.2), custom_call_target="tpu_custom_call" | custom-call | bytes 1024 | tf_op jit(solution)/shard_map/pallas_call | solution.py:124
  5.8 3.1 %collective-permute-start.2 = (bf16[1584,128]{1,0:T(8,128)(2,1)S(1)}, bf16[1584,128]{1,0:T(8,128)(2,1)S(1)}, u32[]{:S(2)}, u32[]{:S(2)}) collective-permute-start(bf16[1584,128]{1,0:T(8,128)(2,1)S(1)} %get-tuple-element.33), channel_id=1, source_target_pairs={{0,4},{1,5},{2,7},{3,6},{4,0},{5,1},{6,3},{7,2},{8,12},{9,13},{10,... | collective-permute-start | bytes 1216520 | tf_op jit(solution)/shard_map/ppermute | solution.py:256
  8.9 2.6 %collective-permute-start.4 = (bf16[688,128]{1,0:T(8,128)(2,1)S(1)}, bf16[688,128]{1,0:T(8,128)(2,1)S(1)}, u32[]{:S(2)}, u32[]{:S(2)}) collective-permute-start(bf16[688,128]{1,0:T(8,128)(2,1)S(1)} %get-tuple-element.34), channel_id=1, source_target_pairs={{0,8},{1,9},{2,14},{3,15},{4,12},{5,13},{6,10},{7,11},{8,0},{9,1},... | collective-permute-start | bytes 528392 | tf_op jit(solution)/shard_map/ppermute | solution.py:256
  11.5 0.0 collective-permute-start.10
  11.5 1.2 %collective-permute-start = (bf16[16,128]{1,0:T(8,128)(2,1)S(1)}, bf16[16,128]{1,0:T(8,128)(2,1)S(1)}, u32[]{:S(2)}, u32[]{:S(2)}) collective-permute-start(bf16[16,128]{1,0:T(8,128)(2,1)S(1)} %get-tuple-element.29.rest_8_), channel_id=1, source_target_pairs={{0,2},{1,3},{2,0},{3,1},{4,6},{5,7},{6,4},{7,5},{8,10},{9,11},{10,... | collective-permute-start | bytes 12296 | tf_op jit(solution)/shard_map/ppermute | solution.py:256
  12.7 2.4 %collective-permute-done.rest_9_ = bf16[16,128]{1,0:T(8,128)(2,1)S(1)} collective-permute-done((bf16[16,128]{1,0:T(8,128)(2,1)S(1)}, bf16[16,128]{1,0:T(8,128)(2,1)S(1)}, u32[]{:S(2)}, u32[]{:S(2)}) %collective-permute-start) | collective-permute-done | bytes 4128 | tf_op jit(solution)/shard_map/ppermute | solution.py:256
  15.1 4.4 %shard_map.29 = (bf16[1568,128]{1,0:T(8,128)(2,1)S(1)}, bf16[1568,128]{1,0:T(8,128)(2,1)S(1)}, bf16[560,128]{1,0:T(8,128)(2,1)S(1)}, bf16[336,128]{1,0:T(8,128)(2,1)S(1)}, bf16[448,128]{1,0:T(8,128)(2,1)S(1)}) custom-call(bf16[64,25088]{1,0:T(8,128)(2,1)S(1)} %get-tuple-element.30.vt), custom_call_target="tpu_custom_call" | custom-call | bytes 1024 | tf_op jit(solution)/shard_map/pallas_call | solution.py:124
  19.4 0.1 collective-permute-start.1
  19.5 3.0 %collective-permute-done.4.rest_2_ = bf16[688,128]{1,0:T(8,128)(2,1)S(1)} collective-permute-done((bf16[688,128]{1,0:T(8,128)(2,1)S(1)}, bf16[688,128]{1,0:T(8,128)(2,1)S(1)}, u32[]{:S(2)}, u32[]{:S(2)}) %collective-permute-start.4) | collective-permute-done | bytes 176160 | tf_op jit(solution)/shard_map/ppermute | solution.py:256
  22.5 4.0 %collective-permute-start.7 = (bf16[688,128]{1,0:T(8,128)(2,1)S(1)}, bf16[688,128]{1,0:T(8,128)(2,1)S(1)}, u32[]{:S(2)}, u32[]{:S(2)}) collective-permute-start(bf16[688,128]{1,0:T(8,128)(2,1)S(1)} %collective-permute-done.4.rest_2_), channel_id=1, source_target_pairs={{0,2},{1,3},{2,0},{3,1},{4,6},{5,7},{6,4},{7,5},{8,10},{9,11},{10,... | collective-permute-start | bytes 528392 | tf_op jit(solution)/shard_map/ppermute | solution.py:256
  26.5 0.0 collective-permute-done.2.rest_6_.rest_4_.rest_2_
  26.5 2.5 %collective-permute-start.3 = (bf16[1584,128]{1,0:T(8,128)(2,1)S(1)}, bf16[1584,128]{1,0:T(8,128)(2,1)S(1)}, u32[]{:S(2)}, u32[]{:S(2)}) collective-permute-start(bf16[1584,128]{1,0:T(8,128)(2,1)S(1)} %collective-permute-done.2.rest_6_.rest_4_.rest_2_), channel_id=1, source_target_pairs={{0,2},{1,3},{2,0},{3,1},{4,6},{5,7},{6,4},{7,5},{8,10},{9,11},{10,... | collective-permute-start | bytes 1216520 | tf_op jit(solution)/shard_map/ppermute | solution.py:256
  29.0 0.5 collective-permute-start.5
  29.5 0.0 collective-permute-done.10.rest_4_.rest_2_
  29.5 2.2 %collective-permute-done.7.rest_3_ = bf16[688,128]{1,0:T(8,128)(2,1)S(1)} collective-permute-done((bf16[688,128]{1,0:T(8,128)(2,1)S(1)}, bf16[688,128]{1,0:T(8,128)(2,1)S(1)}, u32[]{:S(2)}, u32[]{:S(2)}) %collective-permute-start.7) | collective-permute-done | bytes 176160 | tf_op jit(solution)/shard_map/ppermute | solution.py:256
  31.7 3.8 %collective-permute-start.13 = (bf16[1136,128]{1,0:T(8,128)(2,1)S(1)}, bf16[1136,128]{1,0:T(8,128)(2,1)S(1)}, u32[]{:S(2)}, u32[]{:S(2)}) collective-permute-start(bf16[1136,128]{1,0:T(8,128)(2,1)S(1)} %collective-permute-done.10.rest_4_.rest_2_), channel_id=1, source_target_pairs={{0,2},{1,3},{2,0},{3,1},{4,6},{5,7},{6,4},{7,5},{8,10},{9,11},{10,... | collective-permute-start | bytes 872456 | tf_op jit(solution)/shard_map/ppermute | solution.py:256
  35.5 2.1 %collective-permute-start.11 = (bf16[448,128]{1,0:T(8,128)(2,1)S(1)}, bf16[448,128]{1,0:T(8,128)(2,1)S(1)}, u32[]{:S(2)}, u32[]{:S(2)}) collective-permute-start(bf16[448,128]{1,0:T(8,128)(2,1)S(1)} %get-tuple-element.42), channel_id=1, source_target_pairs={{0,13},{1,12},{2,11},{3,10},{4,9},{5,8},{6,15},{7,14},{8,5},{9,4},... | collective-permute-start | bytes 344072 | tf_op jit(solution)/shard_map/ppermute | solution.py:256
  37.6 0.6 %collective-permute-done.5.rest_6_.rest_4_ = bf16[560,128]{1,0:T(8,128)(2,1)S(1)} collective-permute-done((bf16[560,128]{1,0:T(8,128)(2,1)S(1)}, bf16[560,128]{1,0:T(8,128)(2,1)S(1)}, u32[]{:S(2)}, u32[]{:S(2)}) %collective-permute-start.5) | collective-permute-done | bytes 143392 | tf_op jit(solution)/shard_map/ppermute | solution.py:256
  38.2 0.0 collective-permute-start.8
  38.2 0.0 collective-permute-done.1.rest_1_
  38.2 3.5 %collective-permute-start.6 = (bf16[560,128]{1,0:T(8,128)(2,1)S(1)}, bf16[560,128]{1,0:T(8,128)(2,1)S(1)}, u32[]{:S(2)}, u32[]{:S(2)}) collective-permute-start(bf16[560,128]{1,0:T(8,128)(2,1)S(1)} %collective-permute-done.5.rest_6_.rest_4_), channel_id=1, source_target_pairs={{0,2},{1,3},{2,0},{3,1},{4,6},{5,7},{6,4},{7,5},{8,10},{9,11},{10,... | collective-permute-start | bytes 430088 | tf_op jit(solution)/shard_map/ppermute | solution.py:256
  41.7 1.1 %collective-permute-done.11.rest_8_ = bf16[448,128]{1,0:T(8,128)(2,1)S(1)} collective-permute-done((bf16[448,128]{1,0:T(8,128)(2,1)S(1)}, bf16[448,128]{1,0:T(8,128)(2,1)S(1)}, u32[]{:S(2)}, u32[]{:S(2)}) %collective-permute-start.11) | collective-permute-done | bytes 114720 | tf_op jit(solution)/shard_map/ppermute | solution.py:256
  42.8 4.0 %collective-permute-start.12 = (bf16[448,128]{1,0:T(8,128)(2,1)S(1)}, bf16[448,128]{1,0:T(8,128)(2,1)S(1)}, u32[]{:S(2)}, u32[]{:S(2)}) collective-permute-start(bf16[448,128]{1,0:T(8,128)(2,1)S(1)} %collective-permute-done.11.rest_8_), channel_id=1, source_target_pairs={{0,2},{1,3},{2,0},{3,1},{4,6},{5,7},{6,4},{7,5},{8,10},{9,11},{10,... | collective-permute-start | bytes 344072 | tf_op jit(solution)/shard_map/ppermute | solution.py:256
  46.9 0.0 collective-permute-done.8.rest_6_
  46.9 0.0 collective-permute-start.9
  46.9 0.0 collective-permute-done.13.rest_5_.rest_3_
  46.9 0.0 collective-permute-done.3.rest_7_.rest_5_.rest_3_
  46.9 3.1 %shard_map.30 = (f32[128,25088]{1,0:T(8,128)}, bf16[256,128]{1,0:T(8,128)(2,1)S(1)}, bf16[128,64]{1,0:T(8,128)(2,1)S(1)}) custom-call(bf16[64,25088]{1,0:T(8,128)(2,1)S(1)} %get-tuple-element.30.vt, bf16[1568,128]{1,0:T(8,128)(2,1)S(1)} %get-tuple-element.31.rest_0_, bf16[1568,128]{1,0:T(8,128)(2,1)S(1)} %collective-permute-done.1.rest_1_, ...), custom_call_target="tpu_custom_call" | custom-call | bytes 1024 | tf_op jit(solution)/shard_map/pallas_call | solution.py:224
  50.0 0.0 collective-permute-done.6.rest_7_.rest_5_
  50.0 2.4 %shard_map.31.rest_12_ = f32[128,25088]{1,0:T(8,128)} custom-call(bf16[64,25088]{1,0:T(8,128)(2,1)S(1)} %get-tuple-element.30.vt, bf16[1568,128]{1,0:T(8,128)(2,1)S(1)} %get-tuple-element.31.rest_0_, bf16[1568,128]{1,0:T(8,128)(2,1)S(1)} %collective-permute-done.1.rest_1_, ...), custom_call_target="tpu_custom_call", output_to_operand_aliasing={{}: (11, {})} | custom-call | bytes 1024 | tf_op jit(solution)/shard_map/pallas_call | solution.py:224
  52.4 0.0 collective-permute-done.12.rest_9_
  52.4 0.8 %collective-permute-done.9.rest_7_ = bf16[336,128]{1,0:T(8,128)(2,1)S(1)} collective-permute-done((bf16[336,128]{1,0:T(8,128)(2,1)S(1)}, bf16[336,128]{1,0:T(8,128)(2,1)S(1)}, u32[]{:S(2)}, u32[]{:S(2)}) %collective-permute-start.9) | collective-permute-done | bytes 86048 | tf_op jit(solution)/shard_map/ppermute | solution.py:256
  53.2 2.3 %shard_map.32 = f32[128,25088]{1,0:T(8,128)} custom-call(bf16[64,25088]{1,0:T(8,128)(2,1)S(1)} %get-tuple-element.30.vt, bf16[1568,128]{1,0:T(8,128)(2,1)S(1)} %get-tuple-element.31.rest_0_, bf16[1568,128]{1,0:T(8,128)(2,1)S(1)} %collective-permute-done.1.rest_1_, ...), custom_call_target="tpu_custom_call", output_to_operand_aliasing={{}: (13, {})} | custom-call | bytes 1024 | tf_op jit(solution)/shard_map/pallas_call | solution.py:224
Async XLA Ops:
  0.0 0.7 %copy-start = (bf16[128,16]{0,1:T(8,128)(2,1)S(1)}, bf16[128,16]{0,1:T(8,128)(2,1)}, u32[]{:S(2)}) copy-start(bf16[128,16]{0,1:T(8,128)(2,1)} %param.2) | copy-start | bytes 12292
  5.8 20.7 %collective-permute-start.2 = (bf16[1584,128]{1,0:T(8,128)(2,1)S(1)}, bf16[1584,128]{1,0:T(8,128)(2,1)S(1)}, u32[]{:S(2)}, u32[]{:S(2)}) collective-permute-start(bf16[1584,128]{1,0:T(8,128)(2,1)S(1)} %get-tuple-element.33), channel_id=1, source_target_pairs={{0,4},{1,5},{2,7},{3,6},{4,0},{5,1},{6,3},{7,2},{8,12},{9,13},{10,... | collective-permute-start | bytes 1216520 | tf_op jit(solution)/shard_map/ppermute | solution.py:256
  8.9 13.6 %collective-permute-start.4 = (bf16[688,128]{1,0:T(8,128)(2,1)S(1)}, bf16[688,128]{1,0:T(8,128)(2,1)S(1)}, u32[]{:S(2)}, u32[]{:S(2)}) collective-permute-start(bf16[688,128]{1,0:T(8,128)(2,1)S(1)} %get-tuple-element.34), channel_id=1, source_target_pairs={{0,8},{1,9},{2,14},{3,15},{4,12},{5,13},{6,10},{7,11},{8,0},{9,1},... | collective-permute-start | bytes 528392 | tf_op jit(solution)/shard_map/ppermute | solution.py:256
  11.5 18.0 %collective-permute-start.10 = (bf16[1136,128]{1,0:T(8,128)(2,1)S(1)}, bf16[1136,128]{1,0:T(8,128)(2,1)S(1)}, u32[]{:S(2)}, u32[]{:S(2)}) collective-permute-start(bf16[1136,128]{1,0:T(8,128)(2,1)S(1)} %get-tuple-element.40), channel_id=1, source_target_pairs={{0,13},{1,12},{2,11},{3,10},{4,9},{5,8},{6,15},{7,14},{8,5},{9,4},... | collective-permute-start | bytes 872456 | tf_op jit(solution)/shard_map/ppermute | solution.py:256
  11.5 3.6 %collective-permute-start = (bf16[16,128]{1,0:T(8,128)(2,1)S(1)}, bf16[16,128]{1,0:T(8,128)(2,1)S(1)}, u32[]{:S(2)}, u32[]{:S(2)}) collective-permute-start(bf16[16,128]{1,0:T(8,128)(2,1)S(1)} %get-tuple-element.29.rest_8_), channel_id=1, source_target_pairs={{0,2},{1,3},{2,0},{3,1},{4,6},{5,7},{6,4},{7,5},{8,10},{9,11},{10,... | collective-permute-start | bytes 12296 | tf_op jit(solution)/shard_map/ppermute | solution.py:256
  19.4 18.8 %collective-permute-start.1 = (bf16[1568,128]{1,0:T(8,128)(2,1)S(1)}, bf16[1568,128]{1,0:T(8,128)(2,1)S(1)}, u32[]{:S(2)}, u32[]{:S(2)}) collective-permute-start(bf16[1568,128]{1,0:T(8,128)(2,1)S(1)} %get-tuple-element.32), channel_id=1, source_target_pairs={{0,1},{1,0},{2,3},{3,2},{4,5},{5,4},{6,7},{7,6},{8,9},{9,8},{10,11... | collective-permute-start | bytes 1204232 | tf_op jit(solution)/shard_map/ppermute | solution.py:256
  22.5 9.2 %collective-permute-start.7 = (bf16[688,128]{1,0:T(8,128)(2,1)S(1)}, bf16[688,128]{1,0:T(8,128)(2,1)S(1)}, u32[]{:S(2)}, u32[]{:S(2)}) collective-permute-start(bf16[688,128]{1,0:T(8,128)(2,1)S(1)} %collective-permute-done.4.rest_2_), channel_id=1, source_target_pairs={{0,2},{1,3},{2,0},{3,1},{4,6},{5,7},{6,4},{7,5},{8,10},{9,11},{10,... | collective-permute-start | bytes 528392 | tf_op jit(solution)/shard_map/ppermute | solution.py:256
  26.5 20.4 %collective-permute-start.3 = (bf16[1584,128]{1,0:T(8,128)(2,1)S(1)}, bf16[1584,128]{1,0:T(8,128)(2,1)S(1)}, u32[]{:S(2)}, u32[]{:S(2)}) collective-permute-start(bf16[1584,128]{1,0:T(8,128)(2,1)S(1)} %collective-permute-done.2.rest_6_.rest_4_.rest_2_), channel_id=1, source_target_pairs={{0,2},{1,3},{2,0},{3,1},{4,6},{5,7},{6,4},{7,5},{8,10},{9,11},{10,... | collective-permute-start | bytes 1216520 | tf_op jit(solution)/shard_map/ppermute | solution.py:256
  29.0 9.3 %collective-permute-start.5 = (bf16[560,128]{1,0:T(8,128)(2,1)S(1)}, bf16[560,128]{1,0:T(8,128)(2,1)S(1)}, u32[]{:S(2)}, u32[]{:S(2)}) collective-permute-start(bf16[560,128]{1,0:T(8,128)(2,1)S(1)} %get-tuple-element.36), channel_id=1, source_target_pairs={{0,8},{1,9},{2,14},{3,15},{4,12},{5,13},{6,10},{7,11},{8,0},{9,1},... | collective-permute-start | bytes 430088 | tf_op jit(solution)/shard_map/ppermute | solution.py:256
  31.7 15.2 %collective-permute-start.13 = (bf16[1136,128]{1,0:T(8,128)(2,1)S(1)}, bf16[1136,128]{1,0:T(8,128)(2,1)S(1)}, u32[]{:S(2)}, u32[]{:S(2)}) collective-permute-start(bf16[1136,128]{1,0:T(8,128)(2,1)S(1)} %collective-permute-done.10.rest_4_.rest_2_), channel_id=1, source_target_pairs={{0,2},{1,3},{2,0},{3,1},{4,6},{5,7},{6,4},{7,5},{8,10},{9,11},{10,... | collective-permute-start | bytes 872456 | tf_op jit(solution)/shard_map/ppermute | solution.py:256
  35.5 7.3 %collective-permute-start.11 = (bf16[448,128]{1,0:T(8,128)(2,1)S(1)}, bf16[448,128]{1,0:T(8,128)(2,1)S(1)}, u32[]{:S(2)}, u32[]{:S(2)}) collective-permute-start(bf16[448,128]{1,0:T(8,128)(2,1)S(1)} %get-tuple-element.42), channel_id=1, source_target_pairs={{0,13},{1,12},{2,11},{3,10},{4,9},{5,8},{6,15},{7,14},{8,5},{9,4},... | collective-permute-start | bytes 344072 | tf_op jit(solution)/shard_map/ppermute | solution.py:256
  38.2 8.6 %collective-permute-start.8 = (bf16[336,128]{1,0:T(8,128)(2,1)S(1)}, bf16[336,128]{1,0:T(8,128)(2,1)S(1)}, u32[]{:S(2)}, u32[]{:S(2)}) collective-permute-start(bf16[336,128]{1,0:T(8,128)(2,1)S(1)} %get-tuple-element.39), channel_id=1, source_target_pairs={{0,8},{1,9},{2,14},{3,15},{4,12},{5,13},{6,10},{7,11},{8,0},{9,1},... | collective-permute-start | bytes 258056 | tf_op jit(solution)/shard_map/ppermute | solution.py:256
  38.2 11.8 %collective-permute-start.6 = (bf16[560,128]{1,0:T(8,128)(2,1)S(1)}, bf16[560,128]{1,0:T(8,128)(2,1)S(1)}, u32[]{:S(2)}, u32[]{:S(2)}) collective-permute-start(bf16[560,128]{1,0:T(8,128)(2,1)S(1)} %collective-permute-done.5.rest_6_.rest_4_), channel_id=1, source_target_pairs={{0,2},{1,3},{2,0},{3,1},{4,6},{5,7},{6,4},{7,5},{8,10},{9,11},{10,... | collective-permute-start | bytes 430088 | tf_op jit(solution)/shard_map/ppermute | solution.py:256
  42.8 9.6 %collective-permute-start.12 = (bf16[448,128]{1,0:T(8,128)(2,1)S(1)}, bf16[448,128]{1,0:T(8,128)(2,1)S(1)}, u32[]{:S(2)}, u32[]{:S(2)}) collective-permute-start(bf16[448,128]{1,0:T(8,128)(2,1)S(1)} %collective-permute-done.11.rest_8_), channel_id=1, source_target_pairs={{0,2},{1,3},{2,0},{3,1},{4,6},{5,7},{6,4},{7,5},{8,10},{9,11},{10,... | collective-permute-start | bytes 344072 | tf_op jit(solution)/shard_map/ppermute | solution.py:256
  46.9 6.3 %collective-permute-start.9 = (bf16[336,128]{1,0:T(8,128)(2,1)S(1)}, bf16[336,128]{1,0:T(8,128)(2,1)S(1)}, u32[]{:S(2)}, u32[]{:S(2)}) collective-permute-start(bf16[336,128]{1,0:T(8,128)(2,1)S(1)} %collective-permute-done.8.rest_6_), channel_id=1, source_target_pairs={{0,2},{1,3},{2,0},{3,1},{4,6},{5,7},{6,4},{7,5},{8,10},{9,11},{10,... | collective-permute-start | bytes 258056 | tf_op jit(solution)/shard_map/ppermute | solution.py:256

commit v6 on v5

--- a/solution.py
+++ b/solution.py
@@ -103,7 +103,7 @@
             out[pl.ds(spot, 2 * vl), :] = jnp.concatenate(both, axis=0).astype(jnp.bfloat16)
             return carry
 
-        lax.fori_loop(0, count, gather, 0)
+        lax.fori_loop(0, count, gather, 0, unroll=2)
         if rides:
             out[count * 2 * vl :, :] = rider[...]
 
@@ -113,7 +113,7 @@
     extra = amplitudes.shape[0] if opening else 0
     vmem = pl.BlockSpec(memory_space=pltpu.VMEM)
     hbm = pl.BlockSpec(memory_space=pltpu.HBM)
-    chunks = 7
+    chunks = 4
     shapes = [
         jax.ShapeDtypeStruct((count * 2 * vl + extra * rides, LANES), jnp.bfloat16) for _, _, count, rides in plan
     ]

time: 55.7 us -> 55.6 us (level)
  transfers between devices with their start and end apart: 14 -> 14, of which waited for: 6 -> 6; matrix products, arithmetic and copies ran while one was open for 0% -> 0% of each run, Pallas kernels for 18% -> 17%
where the time goes in v6:
time: 55.6 us; the launch traced here: 55.4 us
  starting transfers between devices  27.4 us (49%)
  Pallas kernels  17 us (31%)
  waiting for transfers between devices  10.3 us (19%)
  local copies, waits for them, and re-layouts  0.69 us (1%)
    ppermute x14, starting transfers between devices, send(): lax.ppermute(x, ('blk', 'occ', 'sub'), [(number(*d), to(*d)) for d in eve...  27.4 us
    ppermute x14, waiting for transfers between devices, send(): lax.ppermute(x, ('blk', 'occ', 'sub'), [(number(*d), to(*d)) for d in eve...  10.3 us
    pallas_call x2, Pallas kernels, pack(): pl.pallas_call(functools.partial(pack_kernel, plan, opening), in_specs=[h...  9.16 us
    pallas_call x3, Pallas kernels, combine(): pl.pallas_call(functools.partial(combine_kernel, sources, first, count, o...  7.81 us
  transfers between devices with their start and end apart: 14, of which 6 were waited for; matrix products, arithmetic and copies ran while one was open for 0% of the time, Pallas kernels for 17%

profile of v6, /device:TPU:0, one launch (start us, length us, event | category | flops | bytes accessed | tf_op | source)
XLA Modules:
  0.0 55.4 jit_solution(5699535618190089014)
XLA Ops:
  0.0 0.0 copy-start
  0.0 0.7 %copy-done = bf16[128,16]{0,1:T(8,128)(2,1)S(1)} copy-done((bf16[128,16]{0,1:T(8,128)(2,1)S(1)}, bf16[128,16]{0,1:T(8,128)(2,1)}, u32[]{:S(2)}) %copy-start) | copy-done | bytes 4120
  0.7 5.0 %shard_map.28 = (bf16[688,128]{1,0:T(8,128)(2,1)S(1)}, bf16[1136,128]{1,0:T(8,128)(2,1)S(1)}, bf16[1584,128]{1,0:T(8,128)(2,1)S(1)}, bf16[64,25088]{1,0:T(8,128)(2,1)S(1)}, bf16[16,128]{1,0:T(8,128)(2,1)S(1)}) custom-call(bf16[64,25088]{1,0:T(8,128)(2,1)} %bitcast.3, bf16[16,128]{1,0:T(8,128)(2,1)S(1)} %bitcast.2), custom_call_target="tpu_custom_call" | custom-call | bytes 1024 | tf_op jit(solution)/shard_map/pallas_call | solution.py:124
  5.7 3.1 %collective-permute-start.2 = (bf16[1584,128]{1,0:T(8,128)(2,1)S(1)}, bf16[1584,128]{1,0:T(8,128)(2,1)S(1)}, u32[]{:S(2)}, u32[]{:S(2)}) collective-permute-start(bf16[1584,128]{1,0:T(8,128)(2,1)S(1)} %get-tuple-element.33), channel_id=1, source_target_pairs={{0,4},{1,5},{2,7},{3,6},{4,0},{5,1},{6,3},{7,2},{8,12},{9,13},{10,... | collective-permute-start | bytes 1216520 | tf_op jit(solution)/shard_map/ppermute | solution.py:256
  8.7 2.6 %collective-permute-start.4 = (bf16[688,128]{1,0:T(8,128)(2,1)S(1)}, bf16[688,128]{1,0:T(8,128)(2,1)S(1)}, u32[]{:S(2)}, u32[]{:S(2)}) collective-permute-start(bf16[688,128]{1,0:T(8,128)(2,1)S(1)} %get-tuple-element.34), channel_id=1, source_target_pairs={{0,8},{1,9},{2,14},{3,15},{4,12},{5,13},{6,10},{7,11},{8,0},{9,1},... | collective-permute-start | bytes 528392 | tf_op jit(solution)/shard_map/ppermute | solution.py:256
  11.3 0.0 collective-permute-start.10
  11.3 1.2 %collective-permute-start = (bf16[16,128]{1,0:T(8,128)(2,1)S(1)}, bf16[16,128]{1,0:T(8,128)(2,1)S(1)}, u32[]{:S(2)}, u32[]{:S(2)}) collective-permute-start(bf16[16,128]{1,0:T(8,128)(2,1)S(1)} %get-tuple-element.29.rest_8_), channel_id=1, source_target_pairs={{0,2},{1,3},{2,0},{3,1},{4,6},{5,7},{6,4},{7,5},{8,10},{9,11},{10,... | collective-permute-start | bytes 12296 | tf_op jit(solution)/shard_map/ppermute | solution.py:256
  12.5 2.4 %collective-permute-done.rest_9_ = bf16[16,128]{1,0:T(8,128)(2,1)S(1)} collective-permute-done((bf16[16,128]{1,0:T(8,128)(2,1)S(1)}, bf16[16,128]{1,0:T(8,128)(2,1)S(1)}, u32[]{:S(2)}, u32[]{:S(2)}) %collective-permute-start) | collective-permute-done | bytes 4128 | tf_op jit(solution)/shard_map/ppermute | solution.py:256
  14.9 4.2 %shard_map.29 = (bf16[1568,128]{1,0:T(8,128)(2,1)S(1)}, bf16[1568,128]{1,0:T(8,128)(2,1)S(1)}, bf16[560,128]{1,0:T(8,128)(2,1)S(1)}, bf16[336,128]{1,0:T(8,128)(2,1)S(1)}, bf16[448,128]{1,0:T(8,128)(2,1)S(1)}) custom-call(bf16[64,25088]{1,0:T(8,128)(2,1)S(1)} %get-tuple-element.30.vt), custom_call_target="tpu_custom_call" | custom-call | bytes 1024 | tf_op jit(solution)/shard_map/pallas_call | solution.py:124
  19.2 0.1 collective-permute-start.1
  19.2 3.1 %collective-permute-done.4.rest_2_ = bf16[688,128]{1,0:T(8,128)(2,1)S(1)} collective-permute-done((bf16[688,128]{1,0:T(8,128)(2,1)S(1)}, bf16[688,128]{1,0:T(8,128)(2,1)S(1)}, u32[]{:S(2)}, u32[]{:S(2)}) %collective-permute-start.4) | collective-permute-done | bytes 176160 | tf_op jit(solution)/shard_map/ppermute | solution.py:256
  22.4 4.0 %collective-permute-start.7 = (bf16[688,128]{1,0:T(8,128)(2,1)S(1)}, bf16[688,128]{1,0:T(8,128)(2,1)S(1)}, u32[]{:S(2)}, u32[]{:S(2)}) collective-permute-start(bf16[688,128]{1,0:T(8,128)(2,1)S(1)} %collective-permute-done.4.rest_2_), channel_id=1, source_target_pairs={{0,2},{1,3},{2,0},{3,1},{4,6},{5,7},{6,4},{7,5},{8,10},{9,11},{10,... | collective-permute-start | bytes 528392 | tf_op jit(solution)/shard_map/ppermute | solution.py:256
  26.4 0.0 collective-permute-done.2.rest_6_.rest_4_.rest_2_
  26.4 2.5 %collective-permute-start.3 = (bf16[1584,128]{1,0:T(8,128)(2,1)S(1)}, bf16[1584,128]{1,0:T(8,128)(2,1)S(1)}, u32[]{:S(2)}, u32[]{:S(2)}) collective-permute-start(bf16[1584,128]{1,0:T(8,128)(2,1)S(1)} %collective-permute-done.2.rest_6_.rest_4_.rest_2_), channel_id=1, source_target_pairs={{0,2},{1,3},{2,0},{3,1},{4,6},{5,7},{6,4},{7,5},{8,10},{9,11},{10,... | collective-permute-start | bytes 1216520 | tf_op jit(solution)/shard_map/ppermute | solution.py:256
  28.8 0.5 collective-permute-start.5
  29.4 0.0 collective-permute-done.10.rest_4_.rest_2_
  29.4 2.2 %collective-permute-done.7.rest_3_ = bf16[688,128]{1,0:T(8,128)(2,1)S(1)} collective-permute-done((bf16[688,128]{1,0:T(8,128)(2,1)S(1)}, bf16[688,128]{1,0:T(8,128)(2,1)S(1)}, u32[]{:S(2)}, u32[]{:S(2)}) %collective-permute-start.7) | collective-permute-done | bytes 176160 | tf_op jit(solution)/shard_map/ppermute | solution.py:256
  31.6 3.8 %collective-permute-start.13 = (bf16[1136,128]{1,0:T(8,128)(2,1)S(1)}, bf16[1136,128]{1,0:T(8,128)(2,1)S(1)}, u32[]{:S(2)}, u32[]{:S(2)}) collective-permute-start(bf16[1136,128]{1,0:T(8,128)(2,1)S(1)} %collective-permute-done.10.rest_4_.rest_2_), channel_id=1, source_target_pairs={{0,2},{1,3},{2,0},{3,1},{4,6},{5,7},{6,4},{7,5},{8,10},{9,11},{10,... | collective-permute-start | bytes 872456 | tf_op jit(solution)/shard_map/ppermute | solution.py:256
  35.4 2.1 %collective-permute-start.11 = (bf16[448,128]{1,0:T(8,128)(2,1)S(1)}, bf16[448,128]{1,0:T(8,128)(2,1)S(1)}, u32[]{:S(2)}, u32[]{:S(2)}) collective-permute-start(bf16[448,128]{1,0:T(8,128)(2,1)S(1)} %get-tuple-element.42), channel_id=1, source_target_pairs={{0,13},{1,12},{2,11},{3,10},{4,9},{5,8},{6,15},{7,14},{8,5},{9,4},... | collective-permute-start | bytes 344072 | tf_op jit(solution)/shard_map/ppermute | solution.py:256
  37.5 0.6 %collective-permute-done.5.rest_6_.rest_4_ = bf16[560,128]{1,0:T(8,128)(2,1)S(1)} collective-permute-done((bf16[560,128]{1,0:T(8,128)(2,1)S(1)}, bf16[560,128]{1,0:T(8,128)(2,1)S(1)}, u32[]{:S(2)}, u32[]{:S(2)}) %collective-permute-start.5) | collective-permute-done | bytes 143392 | tf_op jit(solution)/shard_map/ppermute | solution.py:256
  38.1 0.0 collective-permute-start.8
  38.1 0.0 collective-permute-done.1.rest_1_
  38.1 3.5 %collective-permute-start.6 = (bf16[560,128]{1,0:T(8,128)(2,1)S(1)}, bf16[560,128]{1,0:T(8,128)(2,1)S(1)}, u32[]{:S(2)}, u32[]{:S(2)}) collective-permute-start(bf16[560,128]{1,0:T(8,128)(2,1)S(1)} %collective-permute-done.5.rest_6_.rest_4_), channel_id=1, source_target_pairs={{0,2},{1,3},{2,0},{3,1},{4,6},{5,7},{6,4},{7,5},{8,10},{9,11},{10,... | collective-permute-start | bytes 430088 | tf_op jit(solution)/shard_map/ppermute | solution.py:256
  41.6 1.1 %collective-permute-done.11.rest_8_ = bf16[448,128]{1,0:T(8,128)(2,1)S(1)} collective-permute-done((bf16[448,128]{1,0:T(8,128)(2,1)S(1)}, bf16[448,128]{1,0:T(8,128)(2,1)S(1)}, u32[]{:S(2)}, u32[]{:S(2)}) %collective-permute-start.11) | collective-permute-done | bytes 114720 | tf_op jit(solution)/shard_map/ppermute | solution.py:256
  42.7 4.0 %collective-permute-start.12 = (bf16[448,128]{1,0:T(8,128)(2,1)S(1)}, bf16[448,128]{1,0:T(8,128)(2,1)S(1)}, u32[]{:S(2)}, u32[]{:S(2)}) collective-permute-start(bf16[448,128]{1,0:T(8,128)(2,1)S(1)} %collective-permute-done.11.rest_8_), channel_id=1, source_target_pairs={{0,2},{1,3},{2,0},{3,1},{4,6},{5,7},{6,4},{7,5},{8,10},{9,11},{10,... | collective-permute-start | bytes 344072 | tf_op jit(solution)/shard_map/ppermute | solution.py:256
  46.7 0.0 collective-permute-done.8.rest_6_
  46.7 0.0 collective-permute-start.9
  46.8 0.0 collective-permute-done.13.rest_5_.rest_3_
  46.8 0.0 collective-permute-done.3.rest_7_.rest_5_.rest_3_
  46.8 3.1 %shard_map.30 = (f32[128,25088]{1,0:T(8,128)}, bf16[256,128]{1,0:T(8,128)(2,1)S(1)}, bf16[128,64]{1,0:T(8,128)(2,1)S(1)}) custom-call(bf16[64,25088]{1,0:T(8,128)(2,1)S(1)} %get-tuple-element.30.vt, bf16[1568,128]{1,0:T(8,128)(2,1)S(1)} %get-tuple-element.31.rest_0_, bf16[1568,128]{1,0:T(8,128)(2,1)S(1)} %collective-permute-done.1.rest_1_, ...), custom_call_target="tpu_custom_call" | custom-call | bytes 1024 | tf_op jit(solution)/shard_map/pallas_call | solution.py:224
  49.9 0.0 collective-permute-done.6.rest_7_.rest_5_
  49.9 2.4 %shard_map.31.rest_12_ = f32[128,25088]{1,0:T(8,128)} custom-call(bf16[64,25088]{1,0:T(8,128)(2,1)S(1)} %get-tuple-element.30.vt, bf16[1568,128]{1,0:T(8,128)(2,1)S(1)} %get-tuple-element.31.rest_0_, bf16[1568,128]{1,0:T(8,128)(2,1)S(1)} %collective-permute-done.1.rest_1_, ...), custom_call_target="tpu_custom_call", output_to_operand_aliasing={{}: (11, {})} | custom-call | bytes 1024 | tf_op jit(solution)/shard_map/pallas_call | solution.py:224
  52.3 0.0 collective-permute-done.12.rest_9_
  52.3 0.8 %collective-permute-done.9.rest_7_ = bf16[336,128]{1,0:T(8,128)(2,1)S(1)} collective-permute-done((bf16[336,128]{1,0:T(8,128)(2,1)S(1)}, bf16[336,128]{1,0:T(8,128)(2,1)S(1)}, u32[]{:S(2)}, u32[]{:S(2)}) %collective-permute-start.9) | collective-permute-done | bytes 86048 | tf_op jit(solution)/shard_map/ppermute | solution.py:256
  53.1 2.3 %shard_map.32 = f32[128,25088]{1,0:T(8,128)} custom-call(bf16[64,25088]{1,0:T(8,128)(2,1)S(1)} %get-tuple-element.30.vt, bf16[1568,128]{1,0:T(8,128)(2,1)S(1)} %get-tuple-element.31.rest_0_, bf16[1568,128]{1,0:T(8,128)(2,1)S(1)} %collective-permute-done.1.rest_1_, ...), custom_call_target="tpu_custom_call", output_to_operand_aliasing={{}: (13, {})} | custom-call | bytes 1024 | tf_op jit(solution)/shard_map/pallas_call | solution.py:224
Async XLA Ops:
  0.0 0.7 %copy-start = (bf16[128,16]{0,1:T(8,128)(2,1)S(1)}, bf16[128,16]{0,1:T(8,128)(2,1)}, u32[]{:S(2)}) copy-start(bf16[128,16]{0,1:T(8,128)(2,1)} %param.2) | copy-start | bytes 12292
  5.7 20.7 %collective-permute-start.2 = (bf16[1584,128]{1,0:T(8,128)(2,1)S(1)}, bf16[1584,128]{1,0:T(8,128)(2,1)S(1)}, u32[]{:S(2)}, u32[]{:S(2)}) collective-permute-start(bf16[1584,128]{1,0:T(8,128)(2,1)S(1)} %get-tuple-element.33), channel_id=1, source_target_pairs={{0,4},{1,5},{2,7},{3,6},{4,0},{5,1},{6,3},{7,2},{8,12},{9,13},{10,... | collective-permute-start | bytes 1216520 | tf_op jit(solution)/shard_map/ppermute | solution.py:256
  8.7 13.6 %collective-permute-start.4 = (bf16[688,128]{1,0:T(8,128)(2,1)S(1)}, bf16[688,128]{1,0:T(8,128)(2,1)S(1)}, u32[]{:S(2)}, u32[]{:S(2)}) collective-permute-start(bf16[688,128]{1,0:T(8,128)(2,1)S(1)} %get-tuple-element.34), channel_id=1, source_target_pairs={{0,8},{1,9},{2,14},{3,15},{4,12},{5,13},{6,10},{7,11},{8,0},{9,1},... | collective-permute-start | bytes 528392 | tf_op jit(solution)/shard_map/ppermute | solution.py:256
  11.3 18.0 %collective-permute-start.10 = (bf16[1136,128]{1,0:T(8,128)(2,1)S(1)}, bf16[1136,128]{1,0:T(8,128)(2,1)S(1)}, u32[]{:S(2)}, u32[]{:S(2)}) collective-permute-start(bf16[1136,128]{1,0:T(8,128)(2,1)S(1)} %get-tuple-element.40), channel_id=1, source_target_pairs={{0,13},{1,12},{2,11},{3,10},{4,9},{5,8},{6,15},{7,14},{8,5},{9,4},... | collective-permute-start | bytes 872456 | tf_op jit(solution)/shard_map/ppermute | solution.py:256
  11.3 3.6 %collective-permute-start = (bf16[16,128]{1,0:T(8,128)(2,1)S(1)}, bf16[16,128]{1,0:T(8,128)(2,1)S(1)}, u32[]{:S(2)}, u32[]{:S(2)}) collective-permute-start(bf16[16,128]{1,0:T(8,128)(2,1)S(1)} %get-tuple-element.29.rest_8_), channel_id=1, source_target_pairs={{0,2},{1,3},{2,0},{3,1},{4,6},{5,7},{6,4},{7,5},{8,10},{9,11},{10,... | collective-permute-start | bytes 12296 | tf_op jit(solution)/shard_map/ppermute | solution.py:256
  19.2 19.0 %collective-permute-start.1 = (bf16[1568,128]{1,0:T(8,128)(2,1)S(1)}, bf16[1568,128]{1,0:T(8,128)(2,1)S(1)}, u32[]{:S(2)}, u32[]{:S(2)}) collective-permute-start(bf16[1568,128]{1,0:T(8,128)(2,1)S(1)} %get-tuple-element.32), channel_id=1, source_target_pairs={{0,1},{1,0},{2,3},{3,2},{4,5},{5,4},{6,7},{7,6},{8,9},{9,8},{10,11... | collective-permute-start | bytes 1204232 | tf_op jit(solution)/shard_map/ppermute | solution.py:256
  22.4 9.2 %collective-permute-start.7 = (bf16[688,128]{1,0:T(8,128)(2,1)S(1)}, bf16[688,128]{1,0:T(8,128)(2,1)S(1)}, u32[]{:S(2)}, u32[]{:S(2)}) collective-permute-start(bf16[688,128]{1,0:T(8,128)(2,1)S(1)} %collective-permute-done.4.rest_2_), channel_id=1, source_target_pairs={{0,2},{1,3},{2,0},{3,1},{4,6},{5,7},{6,4},{7,5},{8,10},{9,11},{10,... | collective-permute-start | bytes 528392 | tf_op jit(solution)/shard_map/ppermute | solution.py:256
  26.4 20.4 %collective-permute-start.3 = (bf16[1584,128]{1,0:T(8,128)(2,1)S(1)}, bf16[1584,128]{1,0:T(8,128)(2,1)S(1)}, u32[]{:S(2)}, u32[]{:S(2)}) collective-permute-start(bf16[1584,128]{1,0:T(8,128)(2,1)S(1)} %collective-permute-done.2.rest_6_.rest_4_.rest_2_), channel_id=1, source_target_pairs={{0,2},{1,3},{2,0},{3,1},{4,6},{5,7},{6,4},{7,5},{8,10},{9,11},{10,... | collective-permute-start | bytes 1216520 | tf_op jit(solution)/shard_map/ppermute | solution.py:256
  28.8 9.3 %collective-permute-start.5 = (bf16[560,128]{1,0:T(8,128)(2,1)S(1)}, bf16[560,128]{1,0:T(8,128)(2,1)S(1)}, u32[]{:S(2)}, u32[]{:S(2)}) collective-permute-start(bf16[560,128]{1,0:T(8,128)(2,1)S(1)} %get-tuple-element.36), channel_id=1, source_target_pairs={{0,8},{1,9},{2,14},{3,15},{4,12},{5,13},{6,10},{7,11},{8,0},{9,1},... | collective-permute-start | bytes 430088 | tf_op jit(solution)/shard_map/ppermute | solution.py:256
  31.6 15.2 %collective-permute-start.13 = (bf16[1136,128]{1,0:T(8,128)(2,1)S(1)}, bf16[1136,128]{1,0:T(8,128)(2,1)S(1)}, u32[]{:S(2)}, u32[]{:S(2)}) collective-permute-start(bf16[1136,128]{1,0:T(8,128)(2,1)S(1)} %collective-permute-done.10.rest_4_.rest_2_), channel_id=1, source_target_pairs={{0,2},{1,3},{2,0},{3,1},{4,6},{5,7},{6,4},{7,5},{8,10},{9,11},{10,... | collective-permute-start | bytes 872456 | tf_op jit(solution)/shard_map/ppermute | solution.py:256
  35.4 7.3 %collective-permute-start.11 = (bf16[448,128]{1,0:T(8,128)(2,1)S(1)}, bf16[448,128]{1,0:T(8,128)(2,1)S(1)}, u32[]{:S(2)}, u32[]{:S(2)}) collective-permute-start(bf16[448,128]{1,0:T(8,128)(2,1)S(1)} %get-tuple-element.42), channel_id=1, source_target_pairs={{0,13},{1,12},{2,11},{3,10},{4,9},{5,8},{6,15},{7,14},{8,5},{9,4},... | collective-permute-start | bytes 344072 | tf_op jit(solution)/shard_map/ppermute | solution.py:256
  38.1 8.6 %collective-permute-start.8 = (bf16[336,128]{1,0:T(8,128)(2,1)S(1)}, bf16[336,128]{1,0:T(8,128)(2,1)S(1)}, u32[]{:S(2)}, u32[]{:S(2)}) collective-permute-start(bf16[336,128]{1,0:T(8,128)(2,1)S(1)} %get-tuple-element.39), channel_id=1, source_target_pairs={{0,8},{1,9},{2,14},{3,15},{4,12},{5,13},{6,10},{7,11},{8,0},{9,1},... | collective-permute-start | bytes 258056 | tf_op jit(solution)/shard_map/ppermute | solution.py:256
  38.1 11.8 %collective-permute-start.6 = (bf16[560,128]{1,0:T(8,128)(2,1)S(1)}, bf16[560,128]{1,0:T(8,128)(2,1)S(1)}, u32[]{:S(2)}, u32[]{:S(2)}) collective-permute-start(bf16[560,128]{1,0:T(8,128)(2,1)S(1)} %collective-permute-done.5.rest_6_.rest_4_), channel_id=1, source_target_pairs={{0,2},{1,3},{2,0},{3,1},{4,6},{5,7},{6,4},{7,5},{8,10},{9,11},{10,... | collective-permute-start | bytes 430088 | tf_op jit(solution)/shard_map/ppermute | solution.py:256
  42.7 9.6 %collective-permute-start.12 = (bf16[448,128]{1,0:T(8,128)(2,1)S(1)}, bf16[448,128]{1,0:T(8,128)(2,1)S(1)}, u32[]{:S(2)}, u32[]{:S(2)}) collective-permute-start(bf16[448,128]{1,0:T(8,128)(2,1)S(1)} %collective-permute-done.11.rest_8_), channel_id=1, source_target_pairs={{0,2},{1,3},{2,0},{3,1},{4,6},{5,7},{6,4},{7,5},{8,10},{9,11},{10,... | collective-permute-start | bytes 344072 | tf_op jit(solution)/shard_map/ppermute | solution.py:256
  46.7 6.3 %collective-permute-start.9 = (bf16[336,128]{1,0:T(8,128)(2,1)S(1)}, bf16[336,128]{1,0:T(8,128)(2,1)S(1)}, u32[]{:S(2)}, u32[]{:S(2)}) collective-permute-start(bf16[336,128]{1,0:T(8,128)(2,1)S(1)} %collective-permute-done.8.rest_6_), channel_id=1, source_target_pairs={{0,2},{1,3},{2,0},{3,1},{4,6},{5,7},{6,4},{7,5},{8,10},{9,11},{10,... | collective-permute-start | bytes 258056 | tf_op jit(solution)/shard_map/ppermute | solution.py:256
